TPU v7x, 128 devices: a whole 4x4x4 slice. The times are simulated.
128 devices in a mesh: tm: 8 (over z, x_hi), space: 16 (over x_lo, y, core).
Axes of the slice: x: 4 (x_hi: 2, x_lo: 2; x = x_hi * 2 + x_lo), y: 4, z: 4, core: 2. Of those that a mesh axis runs over, the one named last changes fastest.
Arguments:
- fine_nodes: float32 [8, 3, 4, 128, 32, 256], P('tm', None, None, 'space'), may hold values from -5 to 5
- heating: float32 [128, 32, 256], P('space'), may hold values from -4 to 4
Outputs:
- next_nodes: float32 [8, 3, 4, 128, 32, 256], P('tm', None, None, 'space')
All inputs are finite; a program needn't handle non-finite values.
Results may differ from a plain program's by a relative error of at most 0.0001.
Values sent between devices are 32-bit elements; how exact they have to be, the bound alone decides.
No kernel may reach another device: no remote copies, remote signals or barrier semaphores. Data moves between devices by JAX's collectives and lax.ppermute only.
A program may use at most 128 MiB of HBM per device.

v0:
```python
import jax
import jax.numpy as jnp
from jax import lax
from jax.sharding import PartitionSpec as P

ROTATION = 2.0
VISCOSITY = 0.4
DIFFUSIVITY = 0.3
STRATIFICATION = 1.0
SLAB_TIME = 0.25
HALF_TIME = 0.125
EDGE_WEIGHT = 5.0 / 24.0
MIDDLE_WEIGHT = 1.0 / 3.0
FAR_WEIGHT = -1.0 / 24.0
SIXTH = 1.0 / 6.0
TWO_THIRDS = 2.0 / 3.0


def padded(cells, sides, width):
    for axis, dim in sides:
        count = lax.axis_size(axis)
        ends = count - 1
        head = lax.slice_in_dim(cells, 0, width, axis=dim)
        tail = lax.slice_in_dim(cells, cells.shape[dim] - width, cells.shape[dim], axis=dim)
        cells = jnp.concatenate(
            [
                lax.ppermute(tail, axis, [(i, (i + 1) % count) for i in range(ends)]),
                cells,
                lax.ppermute(head, axis, [((i + 1) % count, i) for i in range(ends)]),
            ],
            axis=dim,
        )
    return cells


def passed_along(x, axis, by):
    devices = lax.axis_size(axis)
    pairs = [(i, i + by) for i in range(devices) if 0 <= i + by < devices]
    return lax.ppermute(x, axis, pairs)


def laplacian(widened, spacing):
    centre = widened[..., 2:-2, :, :]
    depth_part = (
        16.0 * (widened[..., 1:-3, :, :] + widened[..., 3:-1, :, :])
        - (widened[..., :-4, :, :] + widened[..., 4:, :, :])
        - 30.0 * centre
    )
    across = (
        16.0 * (jnp.roll(centre, 1, -2) + jnp.roll(centre, -1, -2))
        - (jnp.roll(centre, 2, -2) + jnp.roll(centre, -2, -2))
        - 30.0 * centre
    )
    along_part = (
        16.0 * (jnp.roll(centre, 1, -1) + jnp.roll(centre, -1, -1))
        - (jnp.roll(centre, 2, -1) + jnp.roll(centre, -2, -1))
        - 30.0 * centre
    )
    return (depth_part + across + along_part) * (1.0 / (12.0 * spacing * spacing))


def tendency(widened, source, spacing):
    laplace = laplacian(widened, spacing)
    centre = widened[..., 2:-2, :, :]
    east_flow = centre[..., 0, :, :, :]
    north_flow = centre[..., 1, :, :, :]
    upward = centre[..., 2, :, :, :]
    buoyancy = centre[..., 3, :, :, :]
    return jnp.stack(
        [
            ROTATION * north_flow + VISCOSITY * laplace[..., 0, :, :, :],
            -ROTATION * east_flow + VISCOSITY * laplace[..., 1, :, :, :],
            buoyancy + VISCOSITY * laplace[..., 2, :, :, :],
            STRATIFICATION * upward + DIFFUSIVITY * laplace[..., 3, :, :, :] + source,
        ],
        axis=-4,
    )


def pair_table(count):
    coarse_index = jnp.arange(count // 2, dtype=jnp.int32)[:, None]
    fine_index = jnp.arange(count, dtype=jnp.int32)[None, :] // 2
    return (coarse_index == fine_index).astype(jnp.float32)


def restrict(field):
    leading_shape = field.shape[:-3]
    depth, rows, columns = field.shape[-3:]
    planes = field.reshape(leading_shape + (depth // 2, 2, rows, columns))
    halved = jnp.sum(planes, axis=-3) * 0.5
    row_table = pair_table(rows) * 0.5
    column_table = pair_table(columns) * 0.5
    halved = jnp.einsum("pr,...rc->...pc", row_table, halved, precision=lax.Precision.HIGHEST)
    return jnp.dot(halved, column_table.T, precision=lax.Precision.HIGHEST)


def prolong(field):
    rows, columns = field.shape[-2:]
    row_table = pair_table(2 * rows)
    column_table = pair_table(2 * columns)
    spread = jnp.repeat(field, 2, -3)
    spread = jnp.einsum("pr,...pc->...rc", row_table, spread, precision=lax.Precision.HIGHEST)
    return jnp.dot(spread, column_table, precision=lax.Precision.HIGHEST)


def per_device(fine_nodes, heating):
    node_values = fine_nodes[0]
    leading = lax.axis_index("tm") == 0
    coarse_heat = restrict(heating)
    slopes = tendency(padded(node_values, (("space", 2),), 2), heating, 1.0)
    first_node = node_values[0] + SLAB_TIME * (
        EDGE_WEIGHT * slopes[0] + MIDDLE_WEIGHT * slopes[1] + FAR_WEIGHT * slopes[2]
    )
    first_slope = tendency(padded(first_node, (("space", 1),), 2), heating, 1.0)
    second_node = (
        first_node
        + HALF_TIME * (first_slope - slopes[1])
        + SLAB_TIME * (FAR_WEIGHT * slopes[0] + MIDDLE_WEIGHT * slopes[1] + EDGE_WEIGHT * slopes[2])
    )
    second_slope = tendency(padded(second_node, (("space", 1),), 2), heating, 1.0)
    fine_sum = SLAB_TIME * (SIXTH * slopes[0] + TWO_THIRDS * first_slope + SIXTH * second_slope)
    coarse_first = restrict(node_values[0])
    coarse_last = restrict(second_node)
    coarse_slopes = tendency(
        padded(jnp.stack([coarse_first, coarse_last]), (("space", 2),), 2), coarse_heat, 2.0
    )
    correction = restrict(fine_sum) - HALF_TIME * (coarse_slopes[0] + coarse_slopes[1])
    rest = (
        -SLAB_TIME * coarse_slopes[0]
        + HALF_TIME * (coarse_slopes[0] + coarse_slopes[1])
        + correction
    )
    rest_all = rest[None]
    correction_all = correction[None]

    def sweeps(coarse_start, rest_here, correction_here):
        slope_start = tendency(padded(coarse_start, (("space", 1),), 2), coarse_heat, 2.0)
        middle = coarse_start + SLAB_TIME * slope_start + rest_here
        slope_middle = tendency(padded(middle, (("space", 1),), 2), coarse_heat, 2.0)
        return coarse_start + HALF_TIME * (slope_start + slope_middle) + correction_here

    def turn(turn_index, coarse_start):
        arrived = passed_along(sweeps(coarse_start, rest_all[0], correction_all[0]), "tm", 1)
        return jnp.where(leading, coarse_first, arrived)

    coarse_start = lax.fori_loop(0, lax.axis_size("tm") - 1, turn, coarse_first)
    finish = sweeps(coarse_start, rest_all[0], correction_all[0])
    middle_out = first_node + prolong(0.5 * (coarse_start - coarse_first + (finish - coarse_last)))
    last_node = second_node + prolong(finish - coarse_last)
    opening = jnp.where(leading, node_values[0], passed_along(last_node, "tm", 1))
    return jnp.stack([opening, middle_out, last_node])[None]


def solution(mesh):
    in_specs = (P("tm", None, None, "space", None, None), P("space", None, None))
    out_specs = P("tm", None, None, "space", None, None)
    return jax.shard_map(
        per_device, mesh=mesh, in_specs=in_specs, out_specs=out_specs, check_vma=False
    )
```

profile of v0, /device:TPU:57, one launch (start us, length us, event | category | flops | bytes accessed | tf_op | source)
XLA Modules:
  0.0 403.2 jit_solution(7836741996646983609)
XLA Ops:
  34.8 11.8 %fusion.47 = f32[3,4,8,32,256]{4,3,2,1,0:T(8,128)} fusion(f32[3,4,8,32,256]{4,3,2,1,0:T(8,128)S(1)} %bitcast.162, f32[3,4,2,32,256]{4,3,2,1,0:T(8,128)} %collective-permute-done.6, f32[3,4,2,32,256]{4,3,2,1,0:T(8,128)} %collective-permute-done.5, f32[3,4,8,31,256]{4,3,2,1,0:T(8,128)} %get-tuple-element.130, f32[3,4,8,1,256]{4,3,2,1,0:T(1,128)S(1)} %copy-done.21, ...), kind=kLoop, calls=%fused_computation.86 | loop fusion | flops 24379392 | bytes 33030144 | tf_op jit(solution)/shard_map/mul | solution.py:59
  52.8 5.8 %collective-permute-start.7 = (f32[4,2,32,256]{3,2,1,0:T(8,128)S(1)}, f32[4,2,32,256]{3,2,1,0:T(8,128)S(1)}, u32[]{:S(2)}, u32[]{:S(2)}) collective-permute-start(f32[4,2,32,256]{3,2,1,0:T(8,128)S(1)} %get-tuple-element.175), channel_id=1, source_target_pairs={{0,1},{1,2},{2,3},{3,4},{4,5},{5,6},{6,7},{7,8},{8,9},{9,10},{10,1... | collective-permute-start | bytes 786440 | tf_op jit(solution)/shard_map/ppermute | solution.py:27
  61.8 6.5 %collective-permute-done.8 = f32[4,2,32,256]{3,2,1,0:T(8,128)S(1)} collective-permute-done((f32[4,2,32,256]{3,2,1,0:T(8,128)S(1)}, f32[4,2,32,256]{3,2,1,0:T(8,128)S(1)}, u32[]{:S(2)}, u32[]{:S(2)}) %collective-permute-start.8) | collective-permute-done | bytes 262176 | tf_op jit(solution)/shard_map/ppermute | solution.py:29
  78.8 5.8 %collective-permute-start.9 = (f32[2,4,2,16,128]{4,3,2,1,0:T(8,128)S(1)}, f32[2,4,2,16,128]{4,3,2,1,0:T(8,128)S(1)}, u32[]{:S(2)}, u32[]{:S(2)}) collective-permute-start(f32[2,4,2,16,128]{4,3,2,1,0:T(8,128)S(1)} %get-tuple-element.205), channel_id=1, source_target_pairs={{0,1},{1,2},{2,3},{3,4},{4,5},{5,6},{6,7},{7,8},{8,9},{9,10},{10,1... | collective-permute-start | bytes 393224 | tf_op jit(solution)/shard_map/ppermute | solution.py:27
  89.9 6.5 %collective-permute-done.12 = f32[4,2,32,256]{3,2,1,0:T(8,128)S(1)} collective-permute-done((f32[4,2,32,256]{3,2,1,0:T(8,128)S(1)}, f32[4,2,32,256]{3,2,1,0:T(8,128)S(1)}, u32[]{:S(2)}, u32[]{:S(2)}) %collective-permute-start.12) | collective-permute-done | bytes 262176 | tf_op jit(solution)/shard_map/ppermute | solution.py:29
  100.5 246.4 %while.10 = (s32[]{:T(128)}, f32[4,4,16,128]{3,2,1,0:T(8,128)S(1)}, pred[]{:T(512)}, f32[4,16,128]{2,1,0:T(8,128)}, f32[4,4,16,128]{3,2,1,0:T(8,128)}, /*index=5...) while((s32[]{:T(128)}, f32[4,4,16,128]{3,2,1,0:T(8,128)S(1)}, pred[]{:T(512)}, ...), condition=%wide.region_5.6_spmd, body=%wide.region_4.5_spmd.sunk | while | flops 2637826 | bytes 14352782 | solution.py:146
  113.0 5.8 %collective-permute-start.3 = (f32[4,2,16,128]{3,2,1,0:T(8,128)S(1)}, f32[4,2,16,128]{3,2,1,0:T(8,128)S(1)}, u32[]{:S(2)}, u32[]{:S(2)}) collective-permute-start(f32[4,2,16,128]{3,2,1,0:T(8,128)S(1)} %get-tuple-element.361), channel_id=1, source_target_pairs={{0,1},{1,2},{2,3},{3,4},{4,5},{5,6},{6,7},{7,8},{8,9},{9,10},{10,1... | collective-permute-start | bytes 196616 | tf_op jit(solution)/shard_map/while/body/eval_jaxpr/ppermute | solution.py:27
  131.0 7.5 %collective-permute-start = (f32[4,2,16,128]{3,2,1,0:T(8,128)S(1)}, f32[4,2,16,128]{3,2,1,0:T(8,128)S(1)}, u32[]{:S(2)}, u32[]{:S(2)}) collective-permute-start(f32[4,2,16,128]{3,2,1,0:T(8,128)S(1)} %get-tuple-element.336), channel_id=1, source_target_pairs={{0,1},{1,2},{2,3},{3,4},{4,5},{5,6},{6,7},{7,8},{8,9},{9,10},{10,1... | collective-permute-start | bytes 196616 | tf_op jit(solution)/shard_map/while/body/eval_jaxpr/ppermute | solution.py:27
  141.0 5.2 %collective-permute-done.1 = f32[4,2,16,128]{3,2,1,0:T(8,128)S(1)} collective-permute-done((f32[4,2,16,128]{3,2,1,0:T(8,128)S(1)}, f32[4,2,16,128]{3,2,1,0:T(8,128)S(1)}, u32[]{:S(2)}, u32[]{:S(2)}) %collective-permute-start.1) | collective-permute-done | bytes 65568 | tf_op jit(solution)/shard_map/while/body/eval_jaxpr/ppermute | solution.py:29
  149.0 5.8 %collective-permute-start.3 = (f32[4,2,16,128]{3,2,1,0:T(8,128)S(1)}, f32[4,2,16,128]{3,2,1,0:T(8,128)S(1)}, u32[]{:S(2)}, u32[]{:S(2)}) collective-permute-start(f32[4,2,16,128]{3,2,1,0:T(8,128)S(1)} %get-tuple-element.361), channel_id=1, source_target_pairs={{0,1},{1,2},{2,3},{3,4},{4,5},{5,6},{6,7},{7,8},{8,9},{9,10},{10,1... | collective-permute-start | bytes 196616 | tf_op jit(solution)/shard_map/while/body/eval_jaxpr/ppermute | solution.py:27
  167.0 7.5 %collective-permute-start = (f32[4,2,16,128]{3,2,1,0:T(8,128)S(1)}, f32[4,2,16,128]{3,2,1,0:T(8,128)S(1)}, u32[]{:S(2)}, u32[]{:S(2)}) collective-permute-start(f32[4,2,16,128]{3,2,1,0:T(8,128)S(1)} %get-tuple-element.336), channel_id=1, source_target_pairs={{0,1},{1,2},{2,3},{3,4},{4,5},{5,6},{6,7},{7,8},{8,9},{9,10},{10,1... | collective-permute-start | bytes 196616 | tf_op jit(solution)/shard_map/while/body/eval_jaxpr/ppermute | solution.py:27
  177.0 5.2 %collective-permute-done.1 = f32[4,2,16,128]{3,2,1,0:T(8,128)S(1)} collective-permute-done((f32[4,2,16,128]{3,2,1,0:T(8,128)S(1)}, f32[4,2,16,128]{3,2,1,0:T(8,128)S(1)}, u32[]{:S(2)}, u32[]{:S(2)}) %collective-permute-start.1) | collective-permute-done | bytes 65568 | tf_op jit(solution)/shard_map/while/body/eval_jaxpr/ppermute | solution.py:29
  185.0 5.8 %collective-permute-start.3 = (f32[4,2,16,128]{3,2,1,0:T(8,128)S(1)}, f32[4,2,16,128]{3,2,1,0:T(8,128)S(1)}, u32[]{:S(2)}, u32[]{:S(2)}) collective-permute-start(f32[4,2,16,128]{3,2,1,0:T(8,128)S(1)} %get-tuple-element.361), channel_id=1, source_target_pairs={{0,1},{1,2},{2,3},{3,4},{4,5},{5,6},{6,7},{7,8},{8,9},{9,10},{10,1... | collective-permute-start | bytes 196616 | tf_op jit(solution)/shard_map/while/body/eval_jaxpr/ppermute | solution.py:27
  195.6 5.8 %collective-permute-done.4 = f32[4,4,16,128]{3,2,1,0:T(8,128)S(1)} collective-permute-done((f32[4,4,16,128]{3,2,1,0:T(8,128)}, f32[4,4,16,128]{3,2,1,0:T(8,128)S(1)}, u32[]{:S(2)}, u32[]{:S(2)}) %collective-permute-start.4) | collective-permute-done | bytes 131104 | tf_op jit(solution)/shard_map/while/body/eval_jaxpr/ppermute | solution.py:39
  203.0 7.5 %collective-permute-start = (f32[4,2,16,128]{3,2,1,0:T(8,128)S(1)}, f32[4,2,16,128]{3,2,1,0:T(8,128)S(1)}, u32[]{:S(2)}, u32[]{:S(2)}) collective-permute-start(f32[4,2,16,128]{3,2,1,0:T(8,128)S(1)} %get-tuple-element.336), channel_id=1, source_target_pairs={{0,1},{1,2},{2,3},{3,4},{4,5},{5,6},{6,7},{7,8},{8,9},{9,10},{10,1... | collective-permute-start | bytes 196616 | tf_op jit(solution)/shard_map/while/body/eval_jaxpr/ppermute | solution.py:27
  213.0 5.2 %collective-permute-done.1 = f32[4,2,16,128]{3,2,1,0:T(8,128)S(1)} collective-permute-done((f32[4,2,16,128]{3,2,1,0:T(8,128)S(1)}, f32[4,2,16,128]{3,2,1,0:T(8,128)S(1)}, u32[]{:S(2)}, u32[]{:S(2)}) %collective-permute-start.1) | collective-permute-done | bytes 65568 | tf_op jit(solution)/shard_map/while/body/eval_jaxpr/ppermute | solution.py:29
  221.0 5.8 %collective-permute-start.3 = (f32[4,2,16,128]{3,2,1,0:T(8,128)S(1)}, f32[4,2,16,128]{3,2,1,0:T(8,128)S(1)}, u32[]{:S(2)}, u32[]{:S(2)}) collective-permute-start(f32[4,2,16,128]{3,2,1,0:T(8,128)S(1)} %get-tuple-element.361), channel_id=1, source_target_pairs={{0,1},{1,2},{2,3},{3,4},{4,5},{5,6},{6,7},{7,8},{8,9},{9,10},{10,1... | collective-permute-start | bytes 196616 | tf_op jit(solution)/shard_map/while/body/eval_jaxpr/ppermute | solution.py:27
  231.4 5.9 %collective-permute-done.4 = f32[4,4,16,128]{3,2,1,0:T(8,128)S(1)} collective-permute-done((f32[4,4,16,128]{3,2,1,0:T(8,128)}, f32[4,4,16,128]{3,2,1,0:T(8,128)S(1)}, u32[]{:S(2)}, u32[]{:S(2)}) %collective-permute-start.4) | collective-permute-done | bytes 131104 | tf_op jit(solution)/shard_map/while/body/eval_jaxpr/ppermute | solution.py:39
  239.0 7.5 %collective-permute-start = (f32[4,2,16,128]{3,2,1,0:T(8,128)S(1)}, f32[4,2,16,128]{3,2,1,0:T(8,128)S(1)}, u32[]{:S(2)}, u32[]{:S(2)}) collective-permute-start(f32[4,2,16,128]{3,2,1,0:T(8,128)S(1)} %get-tuple-element.336), channel_id=1, source_target_pairs={{0,1},{1,2},{2,3},{3,4},{4,5},{5,6},{6,7},{7,8},{8,9},{9,10},{10,1... | collective-permute-start | bytes 196616 | tf_op jit(solution)/shard_map/while/body/eval_jaxpr/ppermute | solution.py:27
  249.0 5.2 %collective-permute-done.1 = f32[4,2,16,128]{3,2,1,0:T(8,128)S(1)} collective-permute-done((f32[4,2,16,128]{3,2,1,0:T(8,128)S(1)}, f32[4,2,16,128]{3,2,1,0:T(8,128)S(1)}, u32[]{:S(2)}, u32[]{:S(2)}) %collective-permute-start.1) | collective-permute-done | bytes 65568 | tf_op jit(solution)/shard_map/while/body/eval_jaxpr/ppermute | solution.py:29
  257.0 5.8 %collective-permute-start.3 = (f32[4,2,16,128]{3,2,1,0:T(8,128)S(1)}, f32[4,2,16,128]{3,2,1,0:T(8,128)S(1)}, u32[]{:S(2)}, u32[]{:S(2)}) collective-permute-start(f32[4,2,16,128]{3,2,1,0:T(8,128)S(1)} %get-tuple-element.361), channel_id=1, source_target_pairs={{0,1},{1,2},{2,3},{3,4},{4,5},{5,6},{6,7},{7,8},{8,9},{9,10},{10,1... | collective-permute-start | bytes 196616 | tf_op jit(solution)/shard_map/while/body/eval_jaxpr/ppermute | solution.py:27
  267.4 5.9 %collective-permute-done.4 = f32[4,4,16,128]{3,2,1,0:T(8,128)S(1)} collective-permute-done((f32[4,4,16,128]{3,2,1,0:T(8,128)}, f32[4,4,16,128]{3,2,1,0:T(8,128)S(1)}, u32[]{:S(2)}, u32[]{:S(2)}) %collective-permute-start.4) | collective-permute-done | bytes 131104 | tf_op jit(solution)/shard_map/while/body/eval_jaxpr/ppermute | solution.py:39
  275.0 7.5 %collective-permute-start = (f32[4,2,16,128]{3,2,1,0:T(8,128)S(1)}, f32[4,2,16,128]{3,2,1,0:T(8,128)S(1)}, u32[]{:S(2)}, u32[]{:S(2)}) collective-permute-start(f32[4,2,16,128]{3,2,1,0:T(8,128)S(1)} %get-tuple-element.336), channel_id=1, source_target_pairs={{0,1},{1,2},{2,3},{3,4},{4,5},{5,6},{6,7},{7,8},{8,9},{9,10},{10,1... | collective-permute-start | bytes 196616 | tf_op jit(solution)/shard_map/while/body/eval_jaxpr/ppermute | solution.py:27
  293.0 5.8 %collective-permute-start.3 = (f32[4,2,16,128]{3,2,1,0:T(8,128)S(1)}, f32[4,2,16,128]{3,2,1,0:T(8,128)S(1)}, u32[]{:S(2)}, u32[]{:S(2)}) collective-permute-start(f32[4,2,16,128]{3,2,1,0:T(8,128)S(1)} %get-tuple-element.361), channel_id=1, source_target_pairs={{0,1},{1,2},{2,3},{3,4},{4,5},{5,6},{6,7},{7,8},{8,9},{9,10},{10,1... | collective-permute-start | bytes 196616 | tf_op jit(solution)/shard_map/while/body/eval_jaxpr/ppermute | solution.py:27
  303.4 5.9 %collective-permute-done.4 = f32[4,4,16,128]{3,2,1,0:T(8,128)S(1)} collective-permute-done((f32[4,4,16,128]{3,2,1,0:T(8,128)}, f32[4,4,16,128]{3,2,1,0:T(8,128)S(1)}, u32[]{:S(2)}, u32[]{:S(2)}) %collective-permute-start.4) | collective-permute-done | bytes 131104 | tf_op jit(solution)/shard_map/while/body/eval_jaxpr/ppermute | solution.py:39
  311.0 7.5 %collective-permute-start = (f32[4,2,16,128]{3,2,1,0:T(8,128)S(1)}, f32[4,2,16,128]{3,2,1,0:T(8,128)S(1)}, u32[]{:S(2)}, u32[]{:S(2)}) collective-permute-start(f32[4,2,16,128]{3,2,1,0:T(8,128)S(1)} %get-tuple-element.336), channel_id=1, source_target_pairs={{0,1},{1,2},{2,3},{3,4},{4,5},{5,6},{6,7},{7,8},{8,9},{9,10},{10,1... | collective-permute-start | bytes 196616 | tf_op jit(solution)/shard_map/while/body/eval_jaxpr/ppermute | solution.py:27
  329.0 5.8 %collective-permute-start.3 = (f32[4,2,16,128]{3,2,1,0:T(8,128)S(1)}, f32[4,2,16,128]{3,2,1,0:T(8,128)S(1)}, u32[]{:S(2)}, u32[]{:S(2)}) collective-permute-start(f32[4,2,16,128]{3,2,1,0:T(8,128)S(1)} %get-tuple-element.361), channel_id=1, source_target_pairs={{0,1},{1,2},{2,3},{3,4},{4,5},{5,6},{6,7},{7,8},{8,9},{9,10},{10,1... | collective-permute-start | bytes 196616 | tf_op jit(solution)/shard_map/while/body/eval_jaxpr/ppermute | solution.py:27
  339.4 5.9 %collective-permute-done.4 = f32[4,4,16,128]{3,2,1,0:T(8,128)S(1)} collective-permute-done((f32[4,4,16,128]{3,2,1,0:T(8,128)}, f32[4,4,16,128]{3,2,1,0:T(8,128)S(1)}, u32[]{:S(2)}, u32[]{:S(2)}) %collective-permute-start.4) | collective-permute-done | bytes 131104 | tf_op jit(solution)/shard_map/while/body/eval_jaxpr/ppermute | solution.py:39
  347.5 7.5 %collective-permute-start.13 = (f32[4,2,16,128]{3,2,1,0:T(8,128)S(1)}, f32[4,2,16,128]{3,2,1,0:T(8,128)S(1)}, u32[]{:S(2)}, u32[]{:S(2)}) collective-permute-start(f32[4,2,16,128]{3,2,1,0:T(8,128)S(1)} %get-tuple-element.243), channel_id=1, source_target_pairs={{0,1},{1,2},{2,3},{3,4},{4,5},{5,6},{6,7},{7,8},{8,9},{9,10},{10,1... | collective-permute-start | bytes 196616 | tf_op jit(solution)/shard_map/ppermute | solution.py:27
  357.2 5.5 %collective-permute-done.14 = f32[4,2,16,128]{3,2,1,0:T(8,128)S(1)} collective-permute-done((f32[4,2,16,128]{3,2,1,0:T(8,128)S(1)}, f32[4,2,16,128]{3,2,1,0:T(8,128)S(1)}, u32[]{:S(2)}, u32[]{:S(2)}) %collective-permute-start.14) | collective-permute-done | bytes 65568 | tf_op jit(solution)/shard_map/ppermute | solution.py:29
  368.1 5.8 %collective-permute-done.16 = f32[4,2,16,128]{3,2,1,0:T(8,128)S(1)} collective-permute-done((f32[4,2,16,128]{3,2,1,0:T(8,128)S(1)}, f32[4,2,16,128]{3,2,1,0:T(8,128)S(1)}, u32[]{:S(2)}, u32[]{:S(2)}) %collective-permute-start.16) | collective-permute-done | bytes 65568 | tf_op jit(solution)/shard_map/ppermute | solution.py:29
  378.3 22.7 %collective-permute-done.17 = f32[4,8,32,256]{3,2,1,0:T(8,128)S(1)} collective-permute-done((f32[4,8,32,256]{3,2,1,0:T(8,128)S(1)}, f32[4,8,32,256]{3,2,1,0:T(8,128)S(1)}, u32[]{:S(2)}, u32[]{:S(2)}) %collective-permute-start.17) | collective-permute-done | bytes 1048608 | tf_op jit(solution)/shard_map/ppermute | solution.py:39
  (457 shorter events, 186.5 us)
Async XLA Ops:
  2.9 29.9 %collective-permute-start.5 = (f32[3,4,2,32,256]{4,3,2,1,0:T(8,128)}, f32[3,4,2,32,256]{4,3,2,1,0:T(8,128)}, u32[]{:S(2)}, u32[]{:S(2)}) collective-permute-start(f32[3,4,2,32,256]{4,3,2,1,0:T(8,128)} %get-tuple-element.133), channel_id=1, source_target_pairs={{0,1},{1,2},{2,3},{3,4},{4,5},{5,6},{6,7},{7,8},{8,9},{9,10},{10,1... | collective-permute-start | bytes 2359304 | tf_op jit(solution)/shard_map/ppermute | solution.py:27
  6.2 26.6 %collective-permute-start.6 = (f32[3,4,2,32,256]{4,3,2,1,0:T(8,128)}, f32[3,4,2,32,256]{4,3,2,1,0:T(8,128)}, u32[]{:S(2)}, u32[]{:S(2)}) collective-permute-start(f32[3,4,2,32,256]{4,3,2,1,0:T(8,128)} %get-tuple-element.134), channel_id=1, source_target_pairs={{1,0},{2,1},{3,2},{4,3},{5,4},{6,5},{7,6},{8,7},{9,8},{10,9},{11,1... | collective-permute-start | bytes 2359304 | tf_op jit(solution)/shard_map/ppermute | solution.py:29
  52.8 9.1 %collective-permute-start.7 = (f32[4,2,32,256]{3,2,1,0:T(8,128)S(1)}, f32[4,2,32,256]{3,2,1,0:T(8,128)S(1)}, u32[]{:S(2)}, u32[]{:S(2)}) collective-permute-start(f32[4,2,32,256]{3,2,1,0:T(8,128)S(1)} %get-tuple-element.175), channel_id=1, source_target_pairs={{0,1},{1,2},{2,3},{3,4},{4,5},{5,6},{6,7},{7,8},{8,9},{9,10},{10,1... | collective-permute-start | bytes 786440 | tf_op jit(solution)/shard_map/ppermute | solution.py:27
  58.5 9.8 %collective-permute-start.8 = (f32[4,2,32,256]{3,2,1,0:T(8,128)S(1)}, f32[4,2,32,256]{3,2,1,0:T(8,128)S(1)}, u32[]{:S(2)}, u32[]{:S(2)}) collective-permute-start(f32[4,2,32,256]{3,2,1,0:T(8,128)S(1)} %get-tuple-element.176), channel_id=1, source_target_pairs={{1,0},{2,1},{3,2},{4,3},{5,4},{6,5},{7,6},{8,7},{9,8},{10,9},{11,1... | collective-permute-start | bytes 786440 | tf_op jit(solution)/shard_map/ppermute | solution.py:29
  76.9 12.1 %collective-permute-start.10 = (f32[2,4,2,16,128]{4,3,2,1,0:T(8,128)S(1)}, f32[2,4,2,16,128]{4,3,2,1,0:T(8,128)S(1)}, u32[]{:S(2)}, u32[]{:S(2)}) collective-permute-start(f32[2,4,2,16,128]{4,3,2,1,0:T(8,128)S(1)} %get-tuple-element.206), channel_id=1, source_target_pairs={{1,0},{2,1},{3,2},{4,3},{5,4},{6,5},{7,6},{8,7},{9,8},{10,9},{11,1... | collective-permute-start | bytes 393224 | tf_op jit(solution)/shard_map/ppermute | solution.py:29
  78.8 10.2 %collective-permute-start.9 = (f32[2,4,2,16,128]{4,3,2,1,0:T(8,128)S(1)}, f32[2,4,2,16,128]{4,3,2,1,0:T(8,128)S(1)}, u32[]{:S(2)}, u32[]{:S(2)}) collective-permute-start(f32[2,4,2,16,128]{4,3,2,1,0:T(8,128)S(1)} %get-tuple-element.205), channel_id=1, source_target_pairs={{0,1},{1,2},{2,3},{3,4},{4,5},{5,6},{6,7},{7,8},{8,9},{9,10},{10,1... | collective-permute-start | bytes 393224 | tf_op jit(solution)/shard_map/ppermute | solution.py:27
  86.6 9.8 %collective-permute-start.12 = (f32[4,2,32,256]{3,2,1,0:T(8,128)S(1)}, f32[4,2,32,256]{3,2,1,0:T(8,128)S(1)}, u32[]{:S(2)}, u32[]{:S(2)}) collective-permute-start(f32[4,2,32,256]{3,2,1,0:T(8,128)S(1)} %get-tuple-element.158), channel_id=1, source_target_pairs={{1,0},{2,1},{3,2},{4,3},{5,4},{6,5},{7,6},{8,7},{9,8},{10,9},{11,1... | collective-permute-start | bytes 786440 | tf_op jit(solution)/shard_map/ppermute | solution.py:29
  111.0 7.7 %collective-permute-start.2 = (f32[4,2,16,128]{3,2,1,0:T(8,128)S(1)}, f32[4,2,16,128]{3,2,1,0:T(8,128)S(1)}, u32[]{:S(2)}, u32[]{:S(2)}) collective-permute-start(f32[4,2,16,128]{3,2,1,0:T(8,128)S(1)} %get-tuple-element.360), channel_id=1, source_target_pairs={{1,0},{2,1},{3,2},{4,3},{5,4},{6,5},{7,6},{8,7},{9,8},{10,9},{11,1... | collective-permute-start | bytes 196616 | tf_op jit(solution)/shard_map/while/body/eval_jaxpr/ppermute | solution.py:29
  121.0 8.3 %collective-permute-start.4 = (f32[4,4,16,128]{3,2,1,0:T(8,128)}, f32[4,4,16,128]{3,2,1,0:T(8,128)S(1)}, u32[]{:S(2)}, u32[]{:S(2)}) collective-permute-start(f32[4,4,16,128]{3,2,1,0:T(8,128)} %fusion.383), channel_id=1, source_target_pairs={{0,16},{16,32},{32,48},{48,64},{64,80},{80,96},{96,112},{1,17},{17... | collective-permute-start | bytes 393224 | tf_op jit(solution)/shard_map/while/body/eval_jaxpr/ppermute | solution.py:39
  131.0 10.0 %collective-permute-start = (f32[4,2,16,128]{3,2,1,0:T(8,128)S(1)}, f32[4,2,16,128]{3,2,1,0:T(8,128)S(1)}, u32[]{:S(2)}, u32[]{:S(2)}) collective-permute-start(f32[4,2,16,128]{3,2,1,0:T(8,128)S(1)} %get-tuple-element.336), channel_id=1, source_target_pairs={{0,1},{1,2},{2,3},{3,4},{4,5},{5,6},{6,7},{7,8},{8,9},{9,10},{10,1... | collective-permute-start | bytes 196616 | tf_op jit(solution)/shard_map/while/body/eval_jaxpr/ppermute | solution.py:27
  138.5 7.7 %collective-permute-start.1 = (f32[4,2,16,128]{3,2,1,0:T(8,128)S(1)}, f32[4,2,16,128]{3,2,1,0:T(8,128)S(1)}, u32[]{:S(2)}, u32[]{:S(2)}) collective-permute-start(f32[4,2,16,128]{3,2,1,0:T(8,128)S(1)} %get-tuple-element.338), channel_id=1, source_target_pairs={{1,0},{2,1},{3,2},{4,3},{5,4},{6,5},{7,6},{8,7},{9,8},{10,9},{11,1... | collective-permute-start | bytes 196616 | tf_op jit(solution)/shard_map/while/body/eval_jaxpr/ppermute | solution.py:29
  147.1 7.7 %collective-permute-start.2 = (f32[4,2,16,128]{3,2,1,0:T(8,128)S(1)}, f32[4,2,16,128]{3,2,1,0:T(8,128)S(1)}, u32[]{:S(2)}, u32[]{:S(2)}) collective-permute-start(f32[4,2,16,128]{3,2,1,0:T(8,128)S(1)} %get-tuple-element.360), channel_id=1, source_target_pairs={{1,0},{2,1},{3,2},{4,3},{5,4},{6,5},{7,6},{8,7},{9,8},{10,9},{11,1... | collective-permute-start | bytes 196616 | tf_op jit(solution)/shard_map/while/body/eval_jaxpr/ppermute | solution.py:29
  157.0 8.3 %collective-permute-start.4 = (f32[4,4,16,128]{3,2,1,0:T(8,128)}, f32[4,4,16,128]{3,2,1,0:T(8,128)S(1)}, u32[]{:S(2)}, u32[]{:S(2)}) collective-permute-start(f32[4,4,16,128]{3,2,1,0:T(8,128)} %fusion.383), channel_id=1, source_target_pairs={{0,16},{16,32},{32,48},{48,64},{64,80},{80,96},{96,112},{1,17},{17... | collective-permute-start | bytes 393224 | tf_op jit(solution)/shard_map/while/body/eval_jaxpr/ppermute | solution.py:39
  167.0 10.0 %collective-permute-start = (f32[4,2,16,128]{3,2,1,0:T(8,128)S(1)}, f32[4,2,16,128]{3,2,1,0:T(8,128)S(1)}, u32[]{:S(2)}, u32[]{:S(2)}) collective-permute-start(f32[4,2,16,128]{3,2,1,0:T(8,128)S(1)} %get-tuple-element.336), channel_id=1, source_target_pairs={{0,1},{1,2},{2,3},{3,4},{4,5},{5,6},{6,7},{7,8},{8,9},{9,10},{10,1... | collective-permute-start | bytes 196616 | tf_op jit(solution)/shard_map/while/body/eval_jaxpr/ppermute | solution.py:27
  174.5 7.7 %collective-permute-start.1 = (f32[4,2,16,128]{3,2,1,0:T(8,128)S(1)}, f32[4,2,16,128]{3,2,1,0:T(8,128)S(1)}, u32[]{:S(2)}, u32[]{:S(2)}) collective-permute-start(f32[4,2,16,128]{3,2,1,0:T(8,128)S(1)} %get-tuple-element.338), channel_id=1, source_target_pairs={{1,0},{2,1},{3,2},{4,3},{5,4},{6,5},{7,6},{8,7},{9,8},{10,9},{11,1... | collective-permute-start | bytes 196616 | tf_op jit(solution)/shard_map/while/body/eval_jaxpr/ppermute | solution.py:29
  183.1 7.7 %collective-permute-start.2 = (f32[4,2,16,128]{3,2,1,0:T(8,128)S(1)}, f32[4,2,16,128]{3,2,1,0:T(8,128)S(1)}, u32[]{:S(2)}, u32[]{:S(2)}) collective-permute-start(f32[4,2,16,128]{3,2,1,0:T(8,128)S(1)} %get-tuple-element.360), channel_id=1, source_target_pairs={{1,0},{2,1},{3,2},{4,3},{5,4},{6,5},{7,6},{8,7},{9,8},{10,9},{11,1... | collective-permute-start | bytes 196616 | tf_op jit(solution)/shard_map/while/body/eval_jaxpr/ppermute | solution.py:29
  193.0 8.3 %collective-permute-start.4 = (f32[4,4,16,128]{3,2,1,0:T(8,128)}, f32[4,4,16,128]{3,2,1,0:T(8,128)S(1)}, u32[]{:S(2)}, u32[]{:S(2)}) collective-permute-start(f32[4,4,16,128]{3,2,1,0:T(8,128)} %fusion.383), channel_id=1, source_target_pairs={{0,16},{16,32},{32,48},{48,64},{64,80},{80,96},{96,112},{1,17},{17... | collective-permute-start | bytes 393224 | tf_op jit(solution)/shard_map/while/body/eval_jaxpr/ppermute | solution.py:39
  203.0 10.0 %collective-permute-start = (f32[4,2,16,128]{3,2,1,0:T(8,128)S(1)}, f32[4,2,16,128]{3,2,1,0:T(8,128)S(1)}, u32[]{:S(2)}, u32[]{:S(2)}) collective-permute-start(f32[4,2,16,128]{3,2,1,0:T(8,128)S(1)} %get-tuple-element.336), channel_id=1, source_target_pairs={{0,1},{1,2},{2,3},{3,4},{4,5},{5,6},{6,7},{7,8},{8,9},{9,10},{10,1... | collective-permute-start | bytes 196616 | tf_op jit(solution)/shard_map/while/body/eval_jaxpr/ppermute | solution.py:27
  219.1 7.7 %collective-permute-start.2 = (f32[4,2,16,128]{3,2,1,0:T(8,128)S(1)}, f32[4,2,16,128]{3,2,1,0:T(8,128)S(1)}, u32[]{:S(2)}, u32[]{:S(2)}) collective-permute-start(f32[4,2,16,128]{3,2,1,0:T(8,128)S(1)} %get-tuple-element.360), channel_id=1, source_target_pairs={{1,0},{2,1},{3,2},{4,3},{5,4},{6,5},{7,6},{8,7},{9,8},{10,9},{11,1... | collective-permute-start | bytes 196616 | tf_op jit(solution)/shard_map/while/body/eval_jaxpr/ppermute | solution.py:29
  229.0 8.3 %collective-permute-start.4 = (f32[4,4,16,128]{3,2,1,0:T(8,128)}, f32[4,4,16,128]{3,2,1,0:T(8,128)S(1)}, u32[]{:S(2)}, u32[]{:S(2)}) collective-permute-start(f32[4,4,16,128]{3,2,1,0:T(8,128)} %fusion.383), channel_id=1, source_target_pairs={{0,16},{16,32},{32,48},{48,64},{64,80},{80,96},{96,112},{1,17},{17... | collective-permute-start | bytes 393224 | tf_op jit(solution)/shard_map/while/body/eval_jaxpr/ppermute | solution.py:39
  239.0 10.0 %collective-permute-start = (f32[4,2,16,128]{3,2,1,0:T(8,128)S(1)}, f32[4,2,16,128]{3,2,1,0:T(8,128)S(1)}, u32[]{:S(2)}, u32[]{:S(2)}) collective-permute-start(f32[4,2,16,128]{3,2,1,0:T(8,128)S(1)} %get-tuple-element.336), channel_id=1, source_target_pairs={{0,1},{1,2},{2,3},{3,4},{4,5},{5,6},{6,7},{7,8},{8,9},{9,10},{10,1... | collective-permute-start | bytes 196616 | tf_op jit(solution)/shard_map/while/body/eval_jaxpr/ppermute | solution.py:27
  255.1 7.7 %collective-permute-start.2 = (f32[4,2,16,128]{3,2,1,0:T(8,128)S(1)}, f32[4,2,16,128]{3,2,1,0:T(8,128)S(1)}, u32[]{:S(2)}, u32[]{:S(2)}) collective-permute-start(f32[4,2,16,128]{3,2,1,0:T(8,128)S(1)} %get-tuple-element.360), channel_id=1, source_target_pairs={{1,0},{2,1},{3,2},{4,3},{5,4},{6,5},{7,6},{8,7},{9,8},{10,9},{11,1... | collective-permute-start | bytes 196616 | tf_op jit(solution)/shard_map/while/body/eval_jaxpr/ppermute | solution.py:29
  265.0 8.3 %collective-permute-start.4 = (f32[4,4,16,128]{3,2,1,0:T(8,128)}, f32[4,4,16,128]{3,2,1,0:T(8,128)S(1)}, u32[]{:S(2)}, u32[]{:S(2)}) collective-permute-start(f32[4,4,16,128]{3,2,1,0:T(8,128)} %fusion.383), channel_id=1, source_target_pairs={{0,16},{16,32},{32,48},{48,64},{64,80},{80,96},{96,112},{1,17},{17... | collective-permute-start | bytes 393224 | tf_op jit(solution)/shard_map/while/body/eval_jaxpr/ppermute | solution.py:39
  275.0 10.0 %collective-permute-start = (f32[4,2,16,128]{3,2,1,0:T(8,128)S(1)}, f32[4,2,16,128]{3,2,1,0:T(8,128)S(1)}, u32[]{:S(2)}, u32[]{:S(2)}) collective-permute-start(f32[4,2,16,128]{3,2,1,0:T(8,128)S(1)} %get-tuple-element.336), channel_id=1, source_target_pairs={{0,1},{1,2},{2,3},{3,4},{4,5},{5,6},{6,7},{7,8},{8,9},{9,10},{10,1... | collective-permute-start | bytes 196616 | tf_op jit(solution)/shard_map/while/body/eval_jaxpr/ppermute | solution.py:27
  291.1 7.7 %collective-permute-start.2 = (f32[4,2,16,128]{3,2,1,0:T(8,128)S(1)}, f32[4,2,16,128]{3,2,1,0:T(8,128)S(1)}, u32[]{:S(2)}, u32[]{:S(2)}) collective-permute-start(f32[4,2,16,128]{3,2,1,0:T(8,128)S(1)} %get-tuple-element.360), channel_id=1, source_target_pairs={{1,0},{2,1},{3,2},{4,3},{5,4},{6,5},{7,6},{8,7},{9,8},{10,9},{11,1... | collective-permute-start | bytes 196616 | tf_op jit(solution)/shard_map/while/body/eval_jaxpr/ppermute | solution.py:29
  301.1 8.3 %collective-permute-start.4 = (f32[4,4,16,128]{3,2,1,0:T(8,128)}, f32[4,4,16,128]{3,2,1,0:T(8,128)S(1)}, u32[]{:S(2)}, u32[]{:S(2)}) collective-permute-start(f32[4,4,16,128]{3,2,1,0:T(8,128)} %fusion.383), channel_id=1, source_target_pairs={{0,16},{16,32},{32,48},{48,64},{64,80},{80,96},{96,112},{1,17},{17... | collective-permute-start | bytes 393224 | tf_op jit(solution)/shard_map/while/body/eval_jaxpr/ppermute | solution.py:39
  311.0 10.0 %collective-permute-start = (f32[4,2,16,128]{3,2,1,0:T(8,128)S(1)}, f32[4,2,16,128]{3,2,1,0:T(8,128)S(1)}, u32[]{:S(2)}, u32[]{:S(2)}) collective-permute-start(f32[4,2,16,128]{3,2,1,0:T(8,128)S(1)} %get-tuple-element.336), channel_id=1, source_target_pairs={{0,1},{1,2},{2,3},{3,4},{4,5},{5,6},{6,7},{7,8},{8,9},{9,10},{10,1... | collective-permute-start | bytes 196616 | tf_op jit(solution)/shard_map/while/body/eval_jaxpr/ppermute | solution.py:27
  327.1 7.7 %collective-permute-start.2 = (f32[4,2,16,128]{3,2,1,0:T(8,128)S(1)}, f32[4,2,16,128]{3,2,1,0:T(8,128)S(1)}, u32[]{:S(2)}, u32[]{:S(2)}) collective-permute-start(f32[4,2,16,128]{3,2,1,0:T(8,128)S(1)} %get-tuple-element.360), channel_id=1, source_target_pairs={{1,0},{2,1},{3,2},{4,3},{5,4},{6,5},{7,6},{8,7},{9,8},{10,9},{11,1... | collective-permute-start | bytes 196616 | tf_op jit(solution)/shard_map/while/body/eval_jaxpr/ppermute | solution.py:29
  337.1 8.3 %collective-permute-start.4 = (f32[4,4,16,128]{3,2,1,0:T(8,128)}, f32[4,4,16,128]{3,2,1,0:T(8,128)S(1)}, u32[]{:S(2)}, u32[]{:S(2)}) collective-permute-start(f32[4,4,16,128]{3,2,1,0:T(8,128)} %fusion.383), channel_id=1, source_target_pairs={{0,16},{16,32},{32,48},{48,64},{64,80},{80,96},{96,112},{1,17},{17... | collective-permute-start | bytes 393224 | tf_op jit(solution)/shard_map/while/body/eval_jaxpr/ppermute | solution.py:39
  347.5 9.7 %collective-permute-start.13 = (f32[4,2,16,128]{3,2,1,0:T(8,128)S(1)}, f32[4,2,16,128]{3,2,1,0:T(8,128)S(1)}, u32[]{:S(2)}, u32[]{:S(2)}) collective-permute-start(f32[4,2,16,128]{3,2,1,0:T(8,128)S(1)} %get-tuple-element.243), channel_id=1, source_target_pairs={{0,1},{1,2},{2,3},{3,4},{4,5},{5,6},{6,7},{7,8},{8,9},{9,10},{10,1... | collective-permute-start | bytes 196616 | tf_op jit(solution)/shard_map/ppermute | solution.py:27
  365.7 8.2 %collective-permute-start.16 = (f32[4,2,16,128]{3,2,1,0:T(8,128)S(1)}, f32[4,2,16,128]{3,2,1,0:T(8,128)S(1)}, u32[]{:S(2)}, u32[]{:S(2)}) collective-permute-start(f32[4,2,16,128]{3,2,1,0:T(8,128)S(1)} %get-tuple-element.224), channel_id=1, source_target_pairs={{1,0},{2,1},{3,2},{4,3},{5,4},{6,5},{7,6},{8,7},{9,8},{10,9},{11,1... | collective-permute-start | bytes 196616 | tf_op jit(solution)/shard_map/ppermute | solution.py:29
  375.3 25.7 %collective-permute-start.17 = (f32[4,8,32,256]{3,2,1,0:T(8,128)S(1)}, f32[4,8,32,256]{3,2,1,0:T(8,128)S(1)}, u32[]{:S(2)}, u32[]{:S(2)}) collective-permute-start(f32[4,8,32,256]{3,2,1,0:T(8,128)S(1)} %convolution_add_fusion.1), channel_id=1, source_target_pairs={{0,16},{16,32},{32,48},{48,64},{64,80},{80,96},{96,112},{1,17},{17... | collective-permute-start | bytes 3145736 | tf_op jit(solution)/shard_map/ppermute | solution.py:39
  (62 other events, 436.1 us)
where the time goes:
time: 405 us; the launch traced here: 403 us
  starting transfers between devices  176 us (43%)
  waiting for transfers between devices  131 us (32%)
  local copies, waits for them, and re-layouts  44.9 us (11%)
  other arithmetic  42.1 us (10%)
  matrix products  6.2 us (2%)
    ppermute x20, starting transfers between devices, padded(): lax.ppermute(tail, axis, [(i, (i + 1) % count) for i in range(ends)])  114 us
    ppermute x8, waiting for transfers between devices, passed_along(): return lax.ppermute(x, axis, pairs)  61.1 us
    ppermute x20, waiting for transfers between devices, padded(): lax.ppermute(head, axis, [((i + 1) % count, i) for i in range(ends)])  60.2 us
    ppermute x20, starting transfers between devices, padded(): lax.ppermute(head, axis, [((i + 1) % count, i) for i in range(ends)])  40.3 us
    ppermute x8, starting transfers between devices, passed_along(): return lax.ppermute(x, axis, pairs)  21.7 us
    mul x20, other arithmetic, laplacian(): (depth_part + across + along_part) * (1.0 / (12.0 * spacing * spacing))  20.3 us
    slice x38, local copies, waits for them, and re-layouts, laplacian(): jnp.roll(centre, -1, -1)  10.4 us
    slice x38, local copies, waits for them, and re-layouts, laplacian(): jnp.roll(centre, -2, -1)  10.4 us
  transfers between devices with their start and end apart: 48, of which 27 were waited for; matrix products, arithmetic and copies ran while one was open for 7% of the time, Pallas kernels for 0%

commit v1 on v0

v1 whole, which is shorter than its diff:
```python
import numpy as np
import jax
import jax.numpy as jnp
from jax import lax
from jax.experimental import pallas as pl
from jax.experimental.pallas import tpu as pltpu
from jax.sharding import PartitionSpec as P

VISCOSITY = 0.4
DIFFUSIVITY = 0.3
SLAB_TIME = 0.25
HALF_TIME = 0.125

SLABS = 8
BLOCKS = 16
NZ, NY, NX = 128, 32, 256
CZ, CY, CX = NZ // 2, NY // 2, NX // 2
FINE = NZ // BLOCKS
COARSE = CZ // BLOCKS
CHUNK = CX // SLABS
SPILL = 5
AXES = ("tm", "space")
F32 = jnp.float32
BF16 = jnp.bfloat16


def real_basis(count):
    j = np.arange(count)
    rows, values = [], []
    for k in range(count):
        theta = 2.0 * np.pi * k / count
        if k == 0:
            row = np.ones(count)
        elif 2 * k == count:
            row = np.cos(np.pi * j)
        elif 2 * k < count:
            row = np.cos(theta * j) * np.sqrt(2.0)
        else:
            row = np.sin(theta * j) * np.sqrt(2.0)
        rows.append(row / np.sqrt(count))
        values.append((32.0 * np.cos(theta) - 2.0 * np.cos(2.0 * theta) - 30.0) / 48.0)
    return np.array(rows), np.array(values)


def pairs(count):
    return np.repeat(np.eye(count), 2, axis=0)


def circulant(count):
    eye = np.eye(count)
    return (
        16.0 * (np.roll(eye, 1, 0) + np.roll(eye, -1, 0))
        - (np.roll(eye, 2, 0) + np.roll(eye, -2, 0))
        - 30.0 * eye
    )


def split(matrix):
    matrix = np.asarray(matrix, np.float32)
    high = matrix.astype(jnp.bfloat16)
    low = (matrix - high.astype(np.float32)).astype(jnp.bfloat16)
    return np.stack([high, low])


FY, LAM_Y = real_basis(CY)
FX, LAM_X = real_basis(CX)


def depth_basis():
    eye = np.eye(CZ)
    band = -30.0 * eye
    for offset, weight in ((1, 16.0), (2, -1.0)):
        band += weight * (np.eye(CZ, k=offset) + np.eye(CZ, k=-offset))
    values, vectors = np.linalg.eigh(band / 48.0)
    return values, vectors


LAM_Z, QZ = depth_basis()

DOWN_Y = FY @ pairs(CY).T * 0.5
DOWN_YL = DOWN_Y @ circulant(NY)
DOWN_X = (FX @ pairs(CX).T * 0.5).T
DOWN_XL = circulant(NX) @ DOWN_X
UP_Y = pairs(CY) @ FY.T
UP_X = FX @ pairs(CX).T

K10 = split(np.kron(np.eye(10), DOWN_Y))
K8 = split(np.kron(np.eye(8), DOWN_Y))
K8L = split(np.kron(np.eye(8), DOWN_YL))
K4 = split(np.kron(np.eye(4), DOWN_Y))
X0 = split(DOWN_X)
X1 = split(DOWN_XL)
LAM_XY = (LAM_Y[:, None] + LAM_X[None, :]).astype(np.float32)


def depth_forward():
    table = np.zeros((2, CZ, BLOCKS, 8))
    for half in range(2):
        for block in range(BLOCKS):
            for slot in range(8):
                z = block * COARSE + half * 8 + slot - SPILL
                if 0 <= z < CZ:
                    table[half, :, block, slot] = QZ[z]
    return table.reshape(2 * CZ, BLOCKS * 8)


ZF = split(depth_forward())
ZB = split(QZ)


def up_y_table():
    table = np.zeros((COARSE, NY, CY, COARSE))
    for z in range(COARSE):
        table[z, :, :, z] = UP_Y
    return table.reshape(COARSE * NY, CY * COARSE)


YB = split(up_y_table())
XB = split(UP_X)


def mode_values():
    table = np.zeros((SLABS, BLOCKS, 2, 4, CHUNK))
    for t in range(SLABS):
        for p in range(BLOCKS):
            table[t, p] = LAM_Y[p] + LAM_X[t * CHUNK:(t + 1) * CHUNK]
    return table.reshape(SLABS * BLOCKS, 128).astype(np.float32)


def lane_constants():
    own = np.array([VISCOSITY, VISCOSITY, VISCOSITY, DIFFUSIVITY])
    partner = np.array([VISCOSITY, VISCOSITY, DIFFUSIVITY, VISCOSITY])
    couple = np.array([2.0, -2.0, 1.0, 1.0])
    product = np.array([-4.0, -4.0, 1.0, 1.0])
    table = np.zeros((8, 2, 4, CHUNK))
    for row, values in enumerate((own, partner, couple, product)):
        table[row] = values[None, :, None]
    return table.reshape(8, 128).astype(np.float32)


MODE_XY = mode_values()
LANES = lane_constants()
LAM_Z_COLUMN = np.repeat(LAM_Z[:, None], 128, axis=1).astype(np.float32)


def halves(x):
    high = x.astype(BF16)
    return high, (x - high.astype(F32)).astype(BF16)


def dot(a, b):
    return jnp.dot(a, b, preferred_element_type=F32)


def left(table, x):
    high, low = halves(x)
    return dot(table[0], high) + (dot(table[0], low) + dot(table[1], high))


def right(x, table):
    high, low = halves(x)
    return dot(high, table[0]) + (dot(low, table[0]) + dot(high, table[1]))


def rolled(x, by, axis):
    return pltpu.roll(x, by % x.shape[axis], axis)


def lateral(x):
    near = rolled(x, 1, 0) + rolled(x, -1, 0) + (rolled(x, 1, 1) + rolled(x, -1, 1))
    far = rolled(x, 2, 0) + rolled(x, -2, 0) + (rolled(x, 2, 1) + rolled(x, -2, 1))
    return 16.0 * near - far


def total(terms):
    out = terms[0]
    for term in terms[1:]:
        out = out + term
    return out


def chunk_transpose(values):
    values = list(values)
    lane = lax.broadcasted_iota(jnp.int32, values[0].shape, 1)
    for bit in (1, 2, 4):
        shift = CHUNK * bit
        low = (lane & shift) == 0
        for i in range(8):
            if i & bit:
                continue
            j = i | bit
            first, second = values[i], values[j]
            values[i] = jnp.where(low, first, rolled(second, shift, 1))
            values[j] = jnp.where(low, rolled(first, -shift, 1), second)
    return values


def field_scalars(f):
    nu = jnp.where(f == 3, DIFFUSIVITY, VISCOSITY).astype(F32)
    couple = jnp.where(f == 0, 2.0, jnp.where(f == 1, -2.0, 1.0)).astype(F32)
    heated = jnp.where(f == 3, 1.0, 0.0).astype(F32)
    partner = f + 1 - 2 * (f % 2)
    return nu, couple, heated, partner


def fine_kernel(flags, u, q, k10, k8, k8l, k4, x0, x1, lam,
                first_out, second_out, up_out, down_out, send_out,
                a_s, fe, be, se, cs, w_s, v_s, y_s, g_s):
    mu, keep_low, keep_high = flags[0], flags[1], flags[2]

    def kept(value, p, count):
        if p < 0:
            return value * keep_low
        if p >= count:
            return value * keep_high
        return value

    def combine(f, _):
        for p in range(FINE):
            a_s[f, p] = (5.0 / 24.0) * u[0, f, p] + (1.0 / 3.0) * u[1, f, p] - (1.0 / 24.0) * u[2, f, p]
        return 0

    lax.fori_loop(0, 4, combine, 0)

    def depth_terms(ref, f, p, low, high, base):
        near = [ref[f, p + o + base] for o in (-1, 1) if low <= p + o < high]
        far = [ref[f, p + o + base] for o in (-2, 2) if low <= p + o < high]
        out = None
        if near:
            out = 16.0 * total(near)
        if far:
            out = -total(far) if out is None else out - total(far)
        return out

    def first_stage(f, _):
        nu, couple, heated, partner = field_scalars(f)
        scale = nu * (SLAB_TIME / 12.0)
        for p in range(-2, FINE + 2):
            acc = depth_terms(a_s, f, p, 0, FINE, 0)
            if 0 <= p < FINE:
                centre = a_s[f, p]
                acc = acc + (lateral(centre) - 90.0 * centre)
                value = (scale * acc + (couple * SLAB_TIME) * a_s[partner, p]
                         + (u[0, f, p] + (heated * HALF_TIME) * q[p]))
                rest = (-1.0 / 24.0) * u[0, f, p] - (1.0 / 6.0) * u[1, f, p] + (5.0 / 24.0) * u[2, f, p]
                fe[f, p + 2] = value
                be[f, p + 2] = 0.5 * value + rest
                first_out[f, p] = value
            else:
                value = kept(scale * acc, p, FINE)
                fe[f, p + 2] = value
                be[f, p + 2] = 0.5 * value
                if p < 0:
                    down_out[p + 2, f] = value
                else:
                    up_out[p - FINE, f] = value
        return 0

    lax.fori_loop(0, 4, first_stage, 0)

    def second_stage(f, _):
        nu, couple, heated, partner = field_scalars(f)
        scale = nu * (SLAB_TIME / 12.0)
        for p in range(-4, FINE + 4):
            acc = depth_terms(be, f, p, -2, FINE + 2, 2)
            if -2 <= p < FINE + 2:
                centre = be[f, p + 2]
                acc = acc + (lateral(centre) - 90.0 * centre)
                value = scale * acc + (couple * SLAB_TIME) * be[partner, p + 2] + fe[f, p + 2]
                if 0 <= p < FINE:
                    value = value + (heated * HALF_TIME) * q[p]
            else:
                value = scale * acc
            value = kept(value, p, FINE)
            se[f, p + 4] = value
            c = (1.0 / 6.0) * value
            if -2 <= p < FINE + 2:
                c = c + (2.0 / 3.0) * fe[f, p + 2]
            if 0 <= p < FINE:
                c = c + (1.0 / 6.0) * u[0, f, p]
                second_out[f, p] = value
            elif p < 0:
                down_out[p + 6, f] = value
            else:
                up_out[p - FINE + 2, f] = value
            cs[f, p + 4] = c
        return 0

    lax.fori_loop(0, 4, second_stage, 0)

    def coarse_loop(f, _):
        nu, couple, heated, partner = field_scalars(f)
        scale = nu * (SLAB_TIME / 12.0)
        mean, last, start, defect = [], [], [], []
        for k in range(-2, COARSE + 2):
            mean.append(0.5 * (cs[f, 2 * k + 4] + cs[f, 2 * k + 5]))
            last.append(0.5 * (se[f, 2 * k + 4] + se[f, 2 * k + 5]))
        for k in range(COARSE):
            start.append(0.5 * (u[0, f, 2 * k] + u[0, f, 2 * k + 1]))
        for k in range(-3, COARSE + 3):
            value = None
            for weight, ps in ((-7.0, (2 * k, 2 * k + 1)), (7.5, (2 * k - 1, 2 * k + 2)), (-0.5, (2 * k - 2, 2 * k + 3))):
                part = [cs[f, p + 4] for p in ps if -4 <= p < FINE + 4]
                if part:
                    part = weight * total(part)
                    value = part if value is None else value + part
            value = scale * value
            if -2 <= k < COARSE + 2:
                value = value + (couple * (SLAB_TIME * 0.5)) * (cs[partner, 2 * k + 4] + cs[partner, 2 * k + 5])
            if 0 <= k < COARSE:
                value = value + (heated * (SLAB_TIME * 0.5)) * (q[2 * k] + q[2 * k + 1])
            value = kept(value, k, COARSE)
            if -2 <= k < COARSE + 2:
                value = value - last[k + 2]
            if 0 <= k < COARSE:
                value = value + start[k]
            defect.append(value)
        for k in range(COARSE):
            last[k + 2] = last[k + 2] - mu * start[k]
        c_rows = jnp.concatenate(mean, axis=0)
        c_y = left(k8, c_rows)
        c_yl = left(k8l, c_rows)
        w_y = left(k10, jnp.concatenate(defect, axis=0))
        v_y = left(k8, jnp.concatenate(last, axis=0))
        s_y = left(k4, jnp.concatenate(start, axis=0))
        w_s[f] = right(w_y, x0)
        c_hat = scale * (right(c_y, x1) + right(c_yl, x0))
        w_s[f, pl.ds(CY, 8 * CY)] = w_s[f, pl.ds(CY, 8 * CY)] + c_hat
        v_s[f] = right(v_y, x0)
        y_s[f] = right(s_y, x0)
        return 0

    lax.fori_loop(0, 4, coarse_loop, 0)

    lam_xy = lam[...]

    def plane(ref, f, k, low, high):
        if low <= k < high:
            return ref[f, pl.ds((k - low) * CY, CY)]
        return None

    def coarse_slope(ref, f, k, low, high):
        nu, couple, _, partner = field_scalars(f)
        out = None
        for weight, offsets in ((16.0 / 48.0, (-1, 1)), (-1.0 / 48.0, (-2, 2))):
            part = [plane(ref, f, k + o, low, high) for o in offsets]
            part = [value for value in part if value is not None]
            if part:
                part = weight * total(part)
                out = part if out is None else out + part
        centre = plane(ref, f, k, low, high)
        if centre is None:
            return nu * out
        out = out + (lam_xy - 30.0 / 48.0) * centre
        return nu * out + couple * plane(ref, partner, k, low, high)

    def defect_loop(f, _):
        for k in range(-2, COARSE + 2):
            value = coarse_slope(y_s, f, k, 0, COARSE)
            value = kept((mu * SLAB_TIME) * value, k, COARSE)
            rows = pl.ds((k + 3) * CY, CY)
            w_s[f, rows] = w_s[f, rows] - value
        return 0

    lax.fori_loop(0, 4, defect_loop, 0)

    def packet_loop(f, _):
        for k in range(-SPILL, 16 - SPILL):
            rows = pl.ds((k + SPILL) * CY, CY)
            if k >= COARSE + SPILL:
                g_s[f, rows] = jnp.zeros((CY, CX), F32)
                continue
            value = kept(HALF_TIME * coarse_slope(w_s, f, k, -3, COARSE + 3), k, COARSE)
            for part in (plane(w_s, f, k, -3, COARSE + 3), plane(v_s, f, k, -2, COARSE + 2)):
                if part is not None:
                    value = value + part
            g_s[f, rows] = value
        return 0

    lax.fori_loop(0, 4, packet_loop, 0)

    def pack(p, _):
        values = []
        for half in range(2):
            for f in range(4):
                values.append(g_s[f, pl.ds(half * 8 * CY + p, 8, stride=CY), :])
        for t, value in enumerate(chunk_transpose(values)):
            send_out[t * BLOCKS + p] = value
        return 0

    lax.fori_loop(0, BLOCKS, pack, 0)


def mode_kernel(g, lam_xy, lam_z, lanes, zf, zb, out):
    lam = lam_z[...] + lam_xy[...]
    nu, other, couple, product = (lanes[pl.ds(i, 1)] for i in range(4))
    own = nu * lam
    partner = other * lam
    half_square = 0.5 * SLAB_TIME * SLAB_TIME
    diagonal = 1.0 + SLAB_TIME * own + half_square * (own * own + product)
    mixing = couple * (SLAB_TIME + half_square * (own + partner))
    lane = lax.broadcasted_iota(jnp.int32, (CZ, 128), 1)
    even = (lane & CHUNK) == 0
    left_half = lane < 64

    rows = BLOCKS * 8
    state = None
    states = [jnp.zeros((CZ, 128), F32)]
    for s in range(SLABS):
        both = left(zf, g[pl.ds(s * rows, rows)])
        source = both[:CZ] + rolled(both[CZ:], 64, 1)
        if state is None:
            state = source
        else:
            swapped = jnp.where(even, rolled(state, -CHUNK, 1), rolled(state, CHUNK, 1))
            state = diagonal * state + mixing * swapped + source
        state = jnp.where(left_half, state, 0.0)
        states.append(state)
    for s in range(SLABS):
        packed = states[s] + rolled(states[s + 1], 64, 1)
        out[pl.ds(s * CZ, CZ)] = left(zb, packed)


def paired(x, axis):
    index = lax.broadcasted_iota(jnp.int32, x.shape, axis)
    return x + jnp.where((index & 1) == 0, rolled(x, -1, axis), rolled(x, 1, axis))


def join_kernel(flags, first_c, second_c, low, high, u, first_out, second_out):
    mu = flags[0]

    def body(f, _):
        firsts, seconds = [], []
        for p in range(FINE):
            first = first_c[f, p]
            second = second_c[f, p]
            if p < 2:
                first = first + low[p, f]
            if p >= FINE - 2:
                first = first + high[p - FINE + 2, f]
            if p < 4:
                second = second + low[2 + p, f]
            else:
                second = second + high[2 + p - 4, f]
            firsts.append(first)
            seconds.append(second)
        for k in range(COARSE):
            last = paired(paired(0.125 * (seconds[2 * k] + seconds[2 * k + 1]), 0), 1)
            start = paired(paired((0.125 * mu) * (u[0, f, 2 * k] + u[0, f, 2 * k + 1]), 0), 1)
            middle = 0.5 * (last + start)
            for p in (2 * k, 2 * k + 1):
                first_out[f, p] = firsts[p] - middle
                second_out[f, p] = seconds[p] - last
        return 0

    lax.fori_loop(0, 4, body, 0)


def last_kernel(flags, modes, first, second, before, u, yb, xb, out, h_s):
    leading = 1.0 - flags[0]
    for r in range(8):
        values = [modes[pl.ds(t * 64 + r * 8, 8)] for t in range(SLABS)]
        for g, value in enumerate(chunk_transpose(values)):
            h_s[g, pl.ds(r * 8, 8)] = value

    def body(f, _):
        start = right(left(yb, h_s[f]), xb)
        end = right(left(yb, h_s[4 + f]), xb)
        middle = 0.5 * (start + end)
        for p in range(FINE):
            rows = slice((p // 2) * NY, (p // 2 + 1) * NY)
            out[0, f, p] = before[f, p] + start[rows] + leading * u[0, f, p]
            out[1, f, p] = first[f, p] + middle[rows]
            out[2, f, p] = second[f, p] + end[rows]
        return 0

    lax.fori_loop(0, 4, body, 0)


VM = pl.BlockSpec(memory_space=pltpu.VMEM)
SM = pl.BlockSpec(memory_space=pltpu.SMEM)
NODE0 = pl.BlockSpec((1, 4, FINE, NY, NX), lambda i: (0, 0, 0, 0, 0))


def params(mib):
    return pltpu.CompilerParams(vmem_limit_bytes=mib << 20)


def shape(*sizes):
    return jax.ShapeDtypeStruct(sizes, F32)


def per_device(fine_nodes, heating):
    u = fine_nodes[0]
    tm = lax.axis_index("tm")
    space = lax.axis_index("space")
    flags = jnp.stack([tm > 0, space > 0, space < BLOCKS - 1, space < 0]).astype(F32)
    field = (4, FINE, NY, NX)
    spill = (6, 4, NY, NX)

    with jax.named_scope("fine"):
        first_c, second_c, up, down, packet = pl.pallas_call(
            fine_kernel,
            out_shape=[shape(*field), shape(*field), shape(*spill), shape(*spill), shape(SLABS * BLOCKS, 8, 128)],
            in_specs=[SM] + [VM] * 9,
            out_specs=[VM] * 5,
            scratch_shapes=[
                pltpu.VMEM(field, F32),
                pltpu.VMEM((4, FINE + 4, NY, NX), F32),
                pltpu.VMEM((4, FINE + 4, NY, NX), F32),
                pltpu.VMEM((4, FINE + 8, NY, NX), F32),
                pltpu.VMEM((4, FINE + 8, NY, NX), F32),
                pltpu.VMEM((4, 10 * CY, CX), F32),
                pltpu.VMEM((4, 8 * CY, CX), F32),
                pltpu.VMEM((4, 4 * CY, CX), F32),
                pltpu.VMEM((4, 16 * CY, CX), F32),
            ],
            compiler_params=params(48),
        )(flags, u, heating, K10, K8, K8L, K4, X0, X1, LAM_XY)

    with jax.named_scope("to_modes"):
        modes = lax.all_to_all(packet, AXES, 0, 0, tiled=True)

    with jax.named_scope("spill"):
        low = lax.ppermute(up, "space", [(i, i + 1) for i in range(BLOCKS - 1)])
        high = lax.ppermute(down, "space", [(i + 1, i) for i in range(BLOCKS - 1)])

    with jax.named_scope("join"):
        first, second = pl.pallas_call(
            join_kernel,
            grid=(1,),
            out_shape=[shape(*field), shape(*field)],
            in_specs=[SM] + [VM] * 4 + [NODE0],
            out_specs=[VM] * 2,
            compiler_params=params(32),
        )(flags, first_c, second_c, low, high, u)

    with jax.named_scope("pass"):
        before = lax.ppermute(second, "tm", [(i, i + 1) for i in range(SLABS - 1)])

    with jax.named_scope("modes"):
        lam_xy = lax.dynamic_slice(jnp.asarray(MODE_XY), (tm * BLOCKS + space, 0), (1, 128))
        solved = pl.pallas_call(
            mode_kernel,
            out_shape=shape(SLABS * CZ, 128),
            in_specs=[VM] * 6,
            out_specs=VM,
            compiler_params=params(16),
        )(modes.reshape(SLABS * BLOCKS * 8, 128), lam_xy, LAM_Z_COLUMN, LANES, ZF, ZB)

    with jax.named_scope("from_modes"):
        solved = solved.reshape(SLABS * BLOCKS, COARSE, 128)
        back = lax.all_to_all(solved, AXES, 0, 0, tiled=True).reshape(SLABS * CZ, 128)

    with jax.named_scope("last"):
        out = pl.pallas_call(
            last_kernel,
            grid=(1,),
            out_shape=shape(3, *field),
            in_specs=[SM] + [VM] * 4 + [NODE0] + [VM] * 2,
            out_specs=VM,
            scratch_shapes=[pltpu.VMEM((8, 64, 128), F32)],
            compiler_params=params(32),
        )(flags, back, first, second, before, u, YB, XB)
    return out[None]


def solution(mesh):
    in_specs = (P("tm", None, None, "space", None, None), P("space", None, None))
    out_specs = P("tm", None, None, "space", None, None)
    return jax.shard_map(
        per_device, mesh=mesh, in_specs=in_specs, out_specs=out_specs, check_vma=False
    )
```

time: 405 us -> 110 us (0.27)
  the two profiles are of different devices: /device:TPU:57 before, /device:TPU:1 now
where the time goes in v1:
time: 110 us
  waiting for transfers between devices  37.8 us (34%)
  Pallas kernels  23.9 us (22%)
  starting transfers between devices  21.6 us (20%)
  blocking collectives  16.2 us (15%)
  local copies, waits for them, and re-layouts  10 us (9%)
    all_to_all x1, waiting for transfers between devices, per_device(): modes = lax.all_to_all(packet, AXES, 0, 0, tiled=True)  26.4 us
    all_to_all x1, blocking collectives, per_device(): lax.all_to_all(solved, AXES, 0, 0, tiled=True).reshape(SLABS * CZ, 128)  16.2 us
    pallas_call x1, Pallas kernels, per_device(): pl.pallas_call(fine_kernel, out_shape=[shape(*field), shape(*field), shap...  14.1 us
    all_to_all x1, starting transfers between devices, per_device(): modes = lax.all_to_all(packet, AXES, 0, 0, tiled=True)  9.49 us
    unnamed x36, local copies, waits for them, and re-layouts  9.34 us
    ppermute x1, waiting for transfers between devices, per_device(): low = lax.ppermute(up, 'space', [(i, i + 1) for i in range(BLOCKS - 1)])  6.98 us
    ppermute x1, starting transfers between devices, per_device(): before = lax.ppermute(second, 'tm', [(i, i + 1) for i in range(SLABS - 1)])  5.62 us
    pallas_call x1, Pallas kernels, per_device(): pl.pallas_call(last_kernel, grid=(1,), out_shape=shape(3, *field), in_spe...  5.26 us
  transfers between devices with their start and end apart: 4, of which 3 were waited for; matrix products, arithmetic and copies ran while one was open for 1% of the time, Pallas kernels for 2%

profile of v1, /device:TPU:1, one launch (start us, length us, event | category | flops | bytes accessed | tf_op | source)
XLA Modules:
  0.0 109.8 jit_solution(5292213760901179657)
XLA Ops:
  0.0 0.1 add_convert_fusion.flags
  0.1 1.1 %copy-done.4 = f32[8,32,256]{2,1,0:T(8,128)S(1)} copy-done((f32[8,32,256]{2,1,0:T(8,128)S(1)}, f32[8,32,256]{2,1,0:T(8,128)}, u32[]{:S(2)}) %copy-start.4) | copy-done | bytes 262168
  1.2 0.9 copy-done.5
  2.1 0.9 copy-done.7
  3.0 0.9 copy-done.8
  3.9 0.9 copy-done.9
  4.8 0.9 copy-done.10
  5.7 0.8 copy-done.13
  6.5 0.7 copy-done.16
  7.2 14.1 %fine.1 = (f32[4,8,32,256]{3,2,1,0:T(8,128)S(1)}, f32[4,8,32,256]{3,2,1,0:T(8,128)S(1)}, f32[6,4,32,256]{3,2,1,0:T(8,128)S(1)}, f32[6,4,32,256]{3,2,1,0:T(8,128)S(1)}, f32[128,8,128]{2,1,0:T(8,128)S(1)}) custom-call(f32[4]{0:T(128)S(1)} %add_convert_fusion.flags, f32[3,4,8,32,256]{4,3,2,1,0:T(8,128)} %bitcast.9, f32[8,32,256]{2,1,0:T(8,128)S(1)} %copy-done.4, ...), custom_call_target="tpu_custom_call" | custom-call | tf_op jit(solution)/shard_map/fine/pallas_call | solution.py:502
  21.3 0.0 copy-start.3
  21.3 4.6 %collective-permute-start = (f32[6,4,32,256]{3,2,1,0:T(8,128)S(1)}, f32[6,4,32,256]{3,2,1,0:T(8,128)S(1)}, u32[]{:S(2)}, u32[]{:S(2)}) collective-permute-start(f32[6,4,32,256]{3,2,1,0:T(8,128)S(1)} %get-tuple-element.15), channel_id=1, source_target_pairs={{0,1},{1,2},{2,3},{3,4},{4,5},{5,6},{6,7},{7,8},{8,9},{9,10},{10,1... | collective-permute-start | bytes 2359304 | tf_op jit(solution)/shard_map/spill/ppermute | solution.py:525
  25.9 1.9 %collective-permute-start.1 = (f32[6,4,32,256]{3,2,1,0:T(8,128)S(1)}, f32[6,4,32,256]{3,2,1,0:T(8,128)S(1)}, u32[]{:S(2)}, u32[]{:S(2)}) collective-permute-start(f32[6,4,32,256]{3,2,1,0:T(8,128)S(1)} %get-tuple-element.16), channel_id=1, source_target_pairs={{1,0},{2,1},{3,2},{4,3},{5,4},{6,5},{7,6},{8,7},{9,8},{10,9},{11,1... | collective-permute-start | bytes 2359304 | tf_op jit(solution)/shard_map/spill/ppermute | solution.py:526
  27.8 7.0 %collective-permute-done.low = f32[6,4,32,256]{3,2,1,0:T(8,128)S(1)} collective-permute-done((f32[6,4,32,256]{3,2,1,0:T(8,128)S(1)}, f32[6,4,32,256]{3,2,1,0:T(8,128)S(1)}, u32[]{:S(2)}, u32[]{:S(2)}) %collective-permute-start) | collective-permute-done | bytes 786464 | tf_op jit(solution)/shard_map/spill/ppermute | solution.py:525
  34.8 4.4 %collective-permute-done.1.high = f32[6,4,32,256]{3,2,1,0:T(8,128)S(1)} collective-permute-done((f32[6,4,32,256]{3,2,1,0:T(8,128)S(1)}, f32[6,4,32,256]{3,2,1,0:T(8,128)S(1)}, u32[]{:S(2)}, u32[]{:S(2)}) %collective-permute-start.1) | collective-permute-done | bytes 786464 | tf_op jit(solution)/shard_map/spill/ppermute | solution.py:526
  39.2 0.0 copy-done
  39.2 0.0 copy-start.17
  39.3 0.0 copy-start.6
  39.3 0.0 copy-start.11
  39.3 2.4 %join.1 = (f32[4,8,32,256]{3,2,1,0:T(8,128)S(1)}, f32[4,8,32,256]{3,2,1,0:T(8,128)}) custom-call(f32[4]{0:T(128)S(1)} %add_convert_fusion.flags, f32[4,8,32,256]{3,2,1,0:T(8,128)S(1)} %get-tuple-element.13.first_c, f32[4,8,32,256]{3,2,1,0:T(8,128)S(1)} %get-tuple-element.14.second_c, f32[6,4,32,256]{3,2,1,0:T(8,128)S(1)} %collective-permute-done.low, ...), custom_call_target="tpu_custom_call" | custom-call | tf_op jit(solution)/shard_map/join/pallas_call | solution.py:529
  41.7 1.0 copy-done.1
  42.7 5.6 %collective-permute-start.2 = (f32[4,8,32,256]{3,2,1,0:T(8,128)}, f32[4,8,32,256]{3,2,1,0:T(8,128)}, u32[]{:S(2)}, u32[]{:S(2)}) collective-permute-start(f32[4,8,32,256]{3,2,1,0:T(8,128)} %get-tuple-element.18.second), channel_id=1, source_target_pairs={{0,16},{16,32},{32,48},{48,64},{64,80},{80,96},{96,112},{1,17},{17... | collective-permute-start | bytes 3145736 | tf_op jit(solution)/shard_map/pass/ppermute | solution.py:539
  48.3 9.5 %all-to-all-start = ((f32[128,8,128]{2,1,0:T(8,128)}), f32[128,8,128]{2,1,0:T(8,128)}, u32[]{:S(2)}, u32[]{:S(2)}) async-start(f32[128,8,128]{2,1,0:T(8,128)} %copy-done.3), calls=%async_computation | async-start | bytes 1048576 | tf_op jit(solution)/shard_map/to_modes/all_to_all | solution.py:522
  57.8 0.7 constant_dynamic-slice_fusion.lam_xy
  58.5 26.4 %all-to-all-done = f32[128,8,128]{2,1,0:T(8,128)} async-done(((f32[128,8,128]{2,1,0:T(8,128)}), f32[128,8,128]{2,1,0:T(8,128)}, u32[]{:S(2)}, u32[]{:S(2)}) %all-to-all-start) | async-done | bytes 524320 | tf_op jit(solution)/shard_map/to_modes/all_to_all | solution.py:522
  84.9 0.0 copy-done.17
  84.9 2.1 %modes.1 = f32[512,128]{1,0:T(8,128)S(1)} custom-call(f32[1024,128]{1,0:T(8,128)} %bitcast.5.g, f32[1,128]{1,0:T(1,128)S(1)} %constant_dynamic-slice_fusion.lam_xy, f32[64,128]{1,0:T(8,128)S(1)} %copy-done.15, f32[8,128]{1,0:T(8,128)S(1)} %copy-done.17, bf16[2,128,128]{2,1,0:T(8,128)(2,1)S(1)} %copy-done.12, bf16[2,64,64]{2,1,0:T(8,128)(2,1)S(1)} %copy-done.14), custom_call_target="tpu_custom_call" | custom-call | tf_op jit(solution)/shard_map/modes/pallas_call | solution.py:543
  87.0 16.2 %all_to_all.10 = f32[128,4,128]{2,1,0:T(4,128)S(1)} all-to-all(f32[128,4,128]{2,1,0:T(4,128)S(1)} %bitcast.13), channel_id=1, replica_groups=mesh['tm'=8,'space'=16] {'tm','space'}, dimensions={0} | all-to-all | bytes 524288 | tf_op jit(solution)/shard_map/from_modes/all_to_all | solution.py:553
  103.3 0.0 collective-permute-done.2.before
  103.3 0.0 copy-start.2
  103.3 1.2 %copy-done.2 = f32[4,8,32,256]{3,2,1,0:T(8,128)S(1)} copy-done((f32[4,8,32,256]{3,2,1,0:T(8,128)S(1)}, f32[4,8,32,256]{3,2,1,0:T(8,128)}, u32[]{:S(2)}) %copy-start.2) | copy-done | bytes 1048600
  104.5 5.3 %last.1 = f32[3,4,8,32,256]{4,3,2,1,0:T(8,128)} custom-call(f32[4]{0:T(128)S(1)} %add_convert_fusion.flags, f32[512,128]{1,0:T(8,128)S(1)} %bitcast.12, f32[4,8,32,256]{3,2,1,0:T(8,128)S(1)} %copy-done.2, f32[4,8,32,256]{3,2,1,0:T(8,128)} %get-tuple-element.18.second, f32[4,8,32,256]{3,2,1,0:T(8,128)} %collective-permute-done.2.before, ...), custom_call_target="tpu_custom_call" | custom-call | tf_op jit(solution)/shard_map/last/pallas_call | solution.py:556
  (19 shorter events, 0.0 us)
Async XLA Ops:
  0.0 39.2 %copy-start = (f32[1,3,4,8,32,256]{5,4,3,2,1,0:T(8,128)S(1)}, f32[1,3,4,8,32,256]{5,4,3,2,1,0:T(8,128)}, u32[]{:S(2)}) copy-start(f32[1,3,4,8,32,256]{5,4,3,2,1,0:T(8,128)} %param.16) | copy-start | bytes 9437188
  0.1 1.1 %copy-start.4 = (f32[8,32,256]{2,1,0:T(8,128)S(1)}, f32[8,32,256]{2,1,0:T(8,128)}, u32[]{:S(2)}) copy-start(f32[8,32,256]{2,1,0:T(8,128)} %q.1) | copy-start | bytes 786436
  1.2 0.9 copy-start.5
  2.1 0.9 copy-start.7
  3.0 0.9 copy-start.8
  3.9 0.9 copy-start.9
  4.8 0.9 copy-start.10
  5.7 0.8 copy-start.13
  6.5 0.7 copy-start.16
  21.3 20.4 %copy-start.3 = (f32[128,8,128]{2,1,0:T(8,128)}, f32[128,8,128]{2,1,0:T(8,128)S(1)}, u32[]{:S(2)}) copy-start(f32[128,8,128]{2,1,0:T(8,128)S(1)} %get-tuple-element.12) | copy-start | bytes 1572868
  21.3 13.5 %collective-permute-start = (f32[6,4,32,256]{3,2,1,0:T(8,128)S(1)}, f32[6,4,32,256]{3,2,1,0:T(8,128)S(1)}, u32[]{:S(2)}, u32[]{:S(2)}) collective-permute-start(f32[6,4,32,256]{3,2,1,0:T(8,128)S(1)} %get-tuple-element.15), channel_id=1, source_target_pairs={{0,1},{1,2},{2,3},{3,4},{4,5},{5,6},{6,7},{7,8},{8,9},{9,10},{10,1... | collective-permute-start | bytes 2359304 | tf_op jit(solution)/shard_map/spill/ppermute | solution.py:525
  25.9 13.3 %collective-permute-start.1 = (f32[6,4,32,256]{3,2,1,0:T(8,128)S(1)}, f32[6,4,32,256]{3,2,1,0:T(8,128)S(1)}, u32[]{:S(2)}, u32[]{:S(2)}) collective-permute-start(f32[6,4,32,256]{3,2,1,0:T(8,128)S(1)} %get-tuple-element.16), channel_id=1, source_target_pairs={{1,0},{2,1},{3,2},{4,3},{5,4},{6,5},{7,6},{8,7},{9,8},{10,9},{11,1... | collective-permute-start | bytes 2359304 | tf_op jit(solution)/shard_map/spill/ppermute | solution.py:526
  39.2 45.7 %copy-start.12 = (bf16[2,128,128]{2,1,0:T(8,128)(2,1)S(1)}, bf16[2,128,128]{2,1,0:T(8,128)(2,1)}, u32[]{:S(2)}) copy-start(bf16[2,128,128]{2,1,0:T(8,128)(2,1)} %constant.55.clone.zf) | copy-start | bytes 196612
  39.2 45.7 %copy-start.14 = (bf16[2,64,64]{2,1,0:T(8,128)(2,1)S(1)}, bf16[2,64,64]{2,1,0:T(8,128)(2,1)}, u32[]{:S(2)}) copy-start(bf16[2,64,64]{2,1,0:T(8,128)(2,1)} %constant.56.clone.zb) | copy-start | bytes 49156
  39.2 45.7 %copy-start.15 = (f32[64,128]{1,0:T(8,128)S(1)}, f32[64,128]{1,0:T(8,128)}, u32[]{:S(2)}) copy-start(f32[64,128]{1,0:T(8,128)} %constant.53.clone.lam_z) | copy-start | bytes 98308
  39.2 45.7 %copy-start.17 = (f32[8,128]{1,0:T(8,128)S(1)}, f32[8,128]{1,0:T(8,128)}, u32[]{:S(2)}) copy-start(f32[8,128]{1,0:T(8,128)} %constant.54.clone.lanes) | copy-start | bytes 12292
  39.3 64.0 %copy-start.6 = (bf16[2,128,256]{2,1,0:T(8,128)(2,1)S(1)}, bf16[2,128,256]{2,1,0:T(8,128)(2,1)}, u32[]{:S(2)}) copy-start(bf16[2,128,256]{2,1,0:T(8,128)(2,1)} %constant.58.clone.xb) | copy-start | bytes 393220
  39.3 64.0 %copy-start.11 = (bf16[2,128,64]{2,1,0:T(8,128)(2,1)S(1)}, bf16[2,128,64]{2,1,0:T(8,128)(2,1)}, u32[]{:S(2)}) copy-start(bf16[2,128,64]{2,1,0:T(8,128)(2,1)} %constant.57.clone.yb) | copy-start | bytes 98308
  41.7 1.0 copy-start.1
  42.7 60.6 %collective-permute-start.2 = (f32[4,8,32,256]{3,2,1,0:T(8,128)}, f32[4,8,32,256]{3,2,1,0:T(8,128)}, u32[]{:S(2)}, u32[]{:S(2)}) collective-permute-start(f32[4,8,32,256]{3,2,1,0:T(8,128)} %get-tuple-element.18.second), channel_id=1, source_target_pairs={{0,16},{16,32},{32,48},{48,64},{64,80},{80,96},{96,112},{1,17},{17... | collective-permute-start | bytes 3145736 | tf_op jit(solution)/shard_map/pass/ppermute | solution.py:539
  48.3 36.6 %all-to-all-start = ((f32[128,8,128]{2,1,0:T(8,128)}), f32[128,8,128]{2,1,0:T(8,128)}, u32[]{:S(2)}, u32[]{:S(2)}) async-start(f32[128,8,128]{2,1,0:T(8,128)} %copy-done.3), calls=%async_computation | async-start | bytes 1048576 | tf_op jit(solution)/shard_map/to_modes/all_to_all | solution.py:522
  103.3 1.2 %copy-start.2 = (f32[4,8,32,256]{3,2,1,0:T(8,128)S(1)}, f32[4,8,32,256]{3,2,1,0:T(8,128)}, u32[]{:S(2)}) copy-start(f32[4,8,32,256]{3,2,1,0:T(8,128)} %copy-done.1) | copy-start | bytes 3145732

commit v2 on v1

v2 whole, which is shorter than its diff:
```python
import numpy as np
import jax
import jax.numpy as jnp
from jax import lax
from jax.experimental import pallas as pl
from jax.experimental.pallas import tpu as pltpu
from jax.sharding import PartitionSpec as P

VISCOSITY = 0.4
DIFFUSIVITY = 0.3
SLAB_TIME = 0.25
HALF_TIME = 0.125

SLABS = 8
BLOCKS = 16
NZ, NY, NX = 128, 32, 256
CZ, CY, CX = NZ // 2, NY // 2, NX // 2
FINE = NZ // BLOCKS
COARSE = CZ // BLOCKS
CHUNK = CX // SLABS
SPILL = 5
AXES = ("tm", "space")
F32 = jnp.float32
BF16 = jnp.bfloat16


def real_basis(count):
    j = np.arange(count)
    rows, values = [], []
    for k in range(count):
        theta = 2.0 * np.pi * k / count
        if k == 0:
            row = np.ones(count)
        elif 2 * k == count:
            row = np.cos(np.pi * j)
        elif 2 * k < count:
            row = np.cos(theta * j) * np.sqrt(2.0)
        else:
            row = np.sin(theta * j) * np.sqrt(2.0)
        rows.append(row / np.sqrt(count))
        values.append((32.0 * np.cos(theta) - 2.0 * np.cos(2.0 * theta) - 30.0) / 48.0)
    return np.array(rows), np.array(values)


def pairs(count):
    return np.repeat(np.eye(count), 2, axis=0)


def circulant(count):
    eye = np.eye(count)
    return (
        16.0 * (np.roll(eye, 1, 0) + np.roll(eye, -1, 0))
        - (np.roll(eye, 2, 0) + np.roll(eye, -2, 0))
        - 30.0 * eye
    )


def split(matrix):
    matrix = np.asarray(matrix, np.float32)
    high = matrix.astype(jnp.bfloat16)
    low = (matrix - high.astype(np.float32)).astype(jnp.bfloat16)
    return np.stack([high, low])


FY, LAM_Y = real_basis(CY)
FX, LAM_X = real_basis(CX)


def depth_basis():
    eye = np.eye(CZ)
    band = -30.0 * eye
    for offset, weight in ((1, 16.0), (2, -1.0)):
        band += weight * (np.eye(CZ, k=offset) + np.eye(CZ, k=-offset))
    values, vectors = np.linalg.eigh(band / 48.0)
    return values, vectors


LAM_Z, QZ = depth_basis()

DOWN_Y = FY @ pairs(CY).T * 0.5
DOWN_YL = DOWN_Y @ circulant(NY)
DOWN_X = (FX @ pairs(CX).T * 0.5).T
DOWN_XL = circulant(NX) @ DOWN_X
UP_Y = pairs(CY) @ FY.T
UP_X = FX @ pairs(CX).T


def depth_table(outs, out_low, ins, in_low):
    table = np.zeros((outs, ins))
    for row in range(outs):
        for column in range(ins):
            offset = abs(row + out_low - column - in_low)
            table[row, column] = {0: -30.0, 1: 16.0, 2: -1.0}.get(offset, 0.0)
    return table


def same_plane(outs, out_low, ins, in_low):
    return (np.arange(outs)[:, None] + out_low == np.arange(ins)[None, :] + in_low).astype(np.float64)


def mean_table(outs, out_low, ins, in_low):
    return 0.5 * (np.arange(outs)[:, None] + out_low == (np.arange(ins)[None, :] + in_low) // 2)


def exact(matrix):
    high = np.asarray(matrix, np.float32).astype(jnp.bfloat16)
    assert np.array_equal(high.astype(np.float64), matrix)
    return high


def stacked(matrix):
    return split(matrix).reshape(-1, matrix.shape[1])


EYE_Y = np.eye(NY)
STEP1 = exact(np.kron(depth_table(12, -2, 8, 0), EYE_Y) + np.kron(same_plane(12, -2, 8, 0), circulant(NY)))
STEP2 = exact(np.kron(depth_table(16, -4, 12, -2), EYE_Y) + np.kron(same_plane(16, -4, 12, -2), circulant(NY)))
ALONG = exact(circulant(NX))
MEAN_C = np.kron(mean_table(8, -2, 16, -4), DOWN_Y)
MEAN_L = (
    np.kron(mean_table(10, -3, 20, -6) @ depth_table(20, -6, 16, -4), DOWN_Y)
    + np.kron(mean_table(10, -3, 16, -4), DOWN_YL)
)
DOWN_C = stacked(np.concatenate([MEAN_L, MEAN_C]))
DOWN_S = stacked(MEAN_C)
DOWN_U = stacked(np.kron(mean_table(4, 0, 8, 0), DOWN_Y))
X0 = split(DOWN_X)
X1 = split(DOWN_XL)
LAM_XY = (LAM_Y[:, None] + LAM_X[None, :]).astype(np.float32)


def depth_forward():
    table = np.zeros((2, CZ, BLOCKS, 8))
    for half in range(2):
        for block in range(BLOCKS):
            for slot in range(8):
                z = block * COARSE + half * 8 + slot - SPILL
                if 0 <= z < CZ:
                    table[half, :, block, slot] = QZ[z]
    return table.reshape(2 * CZ, BLOCKS * 8)


ZF = split(depth_forward())
ZB = split(QZ)


def up_y_table():
    table = np.zeros((COARSE, NY, CY, COARSE))
    for z in range(COARSE):
        table[z, :, :, z] = UP_Y
    return table.reshape(COARSE * NY, CY * COARSE)


YB = split(up_y_table())
XB = split(UP_X)


def mode_values():
    table = np.zeros((SLABS, BLOCKS, 2, 4, CHUNK))
    for t in range(SLABS):
        for p in range(BLOCKS):
            table[t, p] = LAM_Y[p] + LAM_X[t * CHUNK:(t + 1) * CHUNK]
    return table.reshape(SLABS * BLOCKS, 128).astype(np.float32)


def lane_constants():
    own = np.array([VISCOSITY, VISCOSITY, VISCOSITY, DIFFUSIVITY])
    partner = np.array([VISCOSITY, VISCOSITY, DIFFUSIVITY, VISCOSITY])
    couple = np.array([2.0, -2.0, 1.0, 1.0])
    product = np.array([-4.0, -4.0, 1.0, 1.0])
    table = np.zeros((8, 2, 4, CHUNK))
    for row, values in enumerate((own, partner, couple, product)):
        table[row] = values[None, :, None]
    return table.reshape(8, 128).astype(np.float32)


MODE_XY = mode_values()
LANES = lane_constants()
LAM_Z_COLUMN = np.repeat(LAM_Z[:, None], 128, axis=1).astype(np.float32)


def halves(x):
    high = x.astype(BF16)
    return high, (x - high.astype(F32)).astype(BF16)


def dot(a, b):
    return jnp.dot(a, b, preferred_element_type=F32)


def left(table, x):
    high, low = halves(x)
    return dot(table[0], high) + (dot(table[0], low) + dot(table[1], high))


def right(x, table):
    high, low = halves(x)
    return dot(high, table[0]) + (dot(low, table[0]) + dot(high, table[1]))


def rolled(x, by, axis):
    return pltpu.roll(x, by % x.shape[axis], axis)


def lateral(x):
    near = rolled(x, 1, 0) + rolled(x, -1, 0) + (rolled(x, 1, 1) + rolled(x, -1, 1))
    far = rolled(x, 2, 0) + rolled(x, -2, 0) + (rolled(x, 2, 1) + rolled(x, -2, 1))
    return 16.0 * near - far


def total(terms):
    out = terms[0]
    for term in terms[1:]:
        out = out + term
    return out


def chunk_transpose(values):
    values = list(values)
    lane = lax.broadcasted_iota(jnp.int32, values[0].shape, 1)
    for bit in (1, 2, 4):
        shift = CHUNK * bit
        low = (lane & shift) == 0
        for i in range(8):
            if i & bit:
                continue
            j = i | bit
            first, second = values[i], values[j]
            values[i] = jnp.where(low, first, rolled(second, shift, 1))
            values[j] = jnp.where(low, rolled(first, -shift, 1), second)
    return values


def left_stacked(table, x):
    high, low = halves(x)
    rows = table.shape[0] // 2
    both = dot(table, high)
    return both[:rows] + (both[rows:] + dot(table[:rows], low))


PLANE = NY
OWN = FINE * PLANE


def fine_kernel(flags, u_hbm, q_hbm, step1_hbm, step2_hbm, along_hbm, down_c_hbm, down_s_hbm, down_u_hbm, x0_hbm, x1_hbm, lam_hbm,
                first_hbm, second_hbm, up_hbm, down_hbm, send_hbm,
                u, q, step1, step2, along, down_c, down_s, down_u, x0, x1, lam,
                a_s, fe, be, se, wy_s, vy_s, cy_s, w_s, v_s, y_s, g_s, send_s, in_sem, u_sem, out_sem, send_sem):
    mu, keep_low, keep_high = flags[0], flags[1], flags[2]
    loads = [
        pltpu.make_async_copy(source, target, in_sem.at[i])
        for i, (source, target) in enumerate((
            (step1_hbm, step1), (along_hbm, along), (q_hbm, q), (step2_hbm, step2), (down_c_hbm, down_c),
            (down_s_hbm, down_s), (down_u_hbm, down_u), (x0_hbm, x0), (x1_hbm, x1), (lam_hbm, lam)))
    ]
    node_loads = [
        [pltpu.make_async_copy(u_hbm.at[n, f], u.at[n, f], u_sem.at[n, f]) for n in range(3)] for f in range(4)
    ]
    for load in node_loads[0] + node_loads[1] + loads + node_loads[2] + node_loads[3]:
        load.start()

    edge = 2 * PLANE
    middle = pl.ds(edge, OWN)
    stores = []

    def store(source, target, sem):
        copy = pltpu.make_async_copy(source, target, sem)
        copy.start()
        stores.append(copy)

    def field(f):
        nu = DIFFUSIVITY if f == 3 else VISCOSITY
        return nu, (2.0, -2.0, 1.0, 1.0)[f], f ^ 1

    def combine(f):
        for load in node_loads[f]:
            load.wait()
        a_s[f] = (5.0 / 24.0) * u[0, f] + (1.0 / 3.0) * u[1, f] - (1.0 / 24.0) * u[2, f]

    def first_stage(f):
        nu, couple, partner = field(f)
        scale = nu * (SLAB_TIME / 12.0)
        high, low = halves(a_s[f])
        column = dot(step1[...], high) + dot(step1[...], low)
        row = dot(high, along[...]) + dot(low, along[...])
        start = u[0, f]
        value = scale * (column[edge:edge + OWN] + row) + (couple * SLAB_TIME) * a_s[partner] + start
        if f == 3:
            value = value + HALF_TIME * q[...]
        fe[f, middle] = value
        be[f, middle] = 0.5 * value + ((-1.0 / 24.0) * start - (1.0 / 6.0) * u[1, f] + (5.0 / 24.0) * u[2, f])
        below = (scale * keep_low) * column[:edge]
        above = (scale * keep_high) * column[edge + OWN:]
        fe[f, pl.ds(0, edge)] = below
        be[f, pl.ds(0, edge)] = 0.5 * below
        fe[f, pl.ds(edge + OWN, edge)] = above
        be[f, pl.ds(edge + OWN, edge)] = 0.5 * above
        store(fe.at[f, middle], first_hbm.at[f], out_sem.at[f, 0])
        store(fe.at[f, pl.ds(0, edge)], down_hbm.at[f, pl.ds(0, edge)], out_sem.at[f, 1])
        store(fe.at[f, pl.ds(edge + OWN, edge)], up_hbm.at[f, pl.ds(0, edge)], out_sem.at[f, 2])

    def second_stage(f, heat_y):
        nu, couple, partner = field(f)
        scale = nu * (SLAB_TIME / 12.0)
        high, low = halves(be[f])
        column = dot(step2[...], high) + dot(step2[...], low)
        row = dot(high, along[...]) + dot(low, along[...])
        first = fe[f]
        value = scale * (column[edge:-edge] + row) + (couple * SLAB_TIME) * be[partner] + first
        centre = value[edge:edge + OWN]
        if f == 3:
            centre = centre + HALF_TIME * q[...]
        below = jnp.concatenate([(scale * keep_low) * column[:edge], keep_low * value[:edge]], axis=0)
        above = jnp.concatenate([keep_high * value[edge + OWN:], (scale * keep_high) * column[-edge:]], axis=0)
        se[f] = jnp.concatenate([below, centre, above], axis=0)
        store(se.at[f, pl.ds(2 * edge, OWN)], second_hbm.at[f], out_sem.at[f, 3])
        store(se.at[f, pl.ds(0, 2 * edge)], down_hbm.at[f, pl.ds(edge, 2 * edge)], out_sem.at[f, 4])
        store(se.at[f, pl.ds(2 * edge + OWN, 2 * edge)], up_hbm.at[f, pl.ds(edge, 2 * edge)], out_sem.at[f, 5])
        c = jnp.concatenate([
            (1.0 / 6.0) * below[:edge],
            (1.0 / 6.0) * below[edge:] + (2.0 / 3.0) * first[:edge],
            (1.0 / 6.0) * (centre + u[0, f]) + (2.0 / 3.0) * first[edge:edge + OWN],
            (1.0 / 6.0) * above[:edge] + (2.0 / 3.0) * first[edge + OWN:],
            (1.0 / 6.0) * above[edge:]], axis=0)
        c_y = left_stacked(down_c[...], c)
        last_y = left_stacked(down_s[...], se[f])
        start_y = left_stacked(down_u[...], u[0, f])
        cy_s[f] = c_y[10 * CY:]
        side = 3 * CY
        own = scale * c_y[side:side + 4 * CY] - last_y[2 * CY:6 * CY] + start_y
        if f == 3:
            own = own + SLAB_TIME * heat_y
        wy_s[f] = jnp.concatenate([
            scale * c_y[:CY],
            scale * c_y[CY:side] - last_y[:2 * CY],
            own,
            scale * c_y[side + 4 * CY:9 * CY] - last_y[6 * CY:],
            scale * c_y[9 * CY:10 * CY]], axis=0)
        vy_s[f, pl.ds(0, 2 * CY)] = last_y[:2 * CY]
        vy_s[f, pl.ds(2 * CY, 4 * CY)] = last_y[2 * CY:6 * CY] - mu * start_y
        vy_s[f, pl.ds(6 * CY, 2 * CY)] = last_y[6 * CY:]
        vy_s[f, pl.ds(8 * CY, 4 * CY)] = start_y

    def across(f):
        nu, couple, partner = field(f)
        scale = nu * (SLAB_TIME / 12.0)
        rows = pl.ds(CY, 8 * CY)
        w_y = wy_s[f]
        mixed = w_y[CY:9 * CY] + (couple * SLAB_TIME) * cy_s[partner]
        w_y = jnp.concatenate([
            keep_low * w_y[:CY], keep_low * mixed[:2 * CY], mixed[2 * CY:6 * CY],
            keep_high * mixed[6 * CY:], keep_high * w_y[9 * CY:]], axis=0)
        w_s[f] = right(w_y, x0)
        w_s[f, rows] = w_s[f, rows] + scale * right(cy_s[f], x1)
        both = right(vy_s[f], x0)
        v_s[f] = both[:8 * CY]
        y_s[f] = both[8 * CY:]

    def kept(value, p, count):
        if p < 0:
            return value * keep_low
        if p >= count:
            return value * keep_high
        return value

    def plane(ref, f, k, low, high):
        if low <= k < high:
            return ref[f, pl.ds((k - low) * CY, CY)]
        return None

    def coarse_slope(ref, f, k, low, high):
        nu, couple, partner = field(f)
        out = None
        for weight, offsets in ((16.0 / 48.0, (-1, 1)), (-1.0 / 48.0, (-2, 2))):
            part = [plane(ref, f, k + o, low, high) for o in offsets]
            part = [value for value in part if value is not None]
            if part:
                part = weight * total(part)
                out = part if out is None else out + part
        centre = plane(ref, f, k, low, high)
        if centre is None:
            return nu * out
        out = out + (lam[...] - 30.0 / 48.0) * centre
        return nu * out + couple * plane(ref, partner, k, low, high)

    def defect(f):
        for k in range(-2, COARSE + 2):
            value = coarse_slope(y_s, f, k, 0, COARSE)
            value = kept((mu * SLAB_TIME) * value, k, COARSE)
            rows = pl.ds((k + 3) * CY, CY)
            w_s[f, rows] = w_s[f, rows] - value

    def packet(f):
        for k in range(-SPILL, 16 - SPILL):
            rows = pl.ds((k + SPILL) * CY, CY)
            if k >= COARSE + SPILL:
                g_s[f, rows] = jnp.zeros((CY, CX), F32)
                continue
            value = kept(HALF_TIME * coarse_slope(w_s, f, k, -3, COARSE + 3), k, COARSE)
            for part in (plane(w_s, f, k, -3, COARSE + 3), plane(v_s, f, k, -2, COARSE + 2)):
                if part is not None:
                    value = value + part
            g_s[f, rows] = value

    for pair in ((0, 1), (2, 3)):
        for f in pair:
            combine(f)
        if pair[0] == 0:
            for load in loads[:3]:
                load.wait()
        for f in pair:
            first_stage(f)
        if pair[0] == 0:
            for load in loads[3:]:
                load.wait()
        heat_y = left_stacked(down_u[...], q[...]) if pair[0] == 2 else None
        for f in pair:
            second_stage(f, heat_y)
        for stage in (across, defect, packet):
            for f in pair:
                stage(f)

    def pack(p, _):
        values = []
        for half in range(2):
            for f in range(4):
                values.append(g_s[f, pl.ds(half * 8 * CY + p, 8, stride=CY), :])
        for t, value in enumerate(chunk_transpose(values)):
            send_s[t * BLOCKS + p] = value
        return 0

    lax.fori_loop(0, BLOCKS, pack, 0, unroll=8)
    store(send_s, send_hbm, send_sem)
    for copy in stores:
        copy.wait()


def mode_kernel(g, lam_xy, lam_z, lanes, zf, zb, out):
    lam = lam_z[...] + lam_xy[...]
    nu, other, couple, product = (lanes[pl.ds(i, 1)] for i in range(4))
    own = nu * lam
    partner = other * lam
    half_square = 0.5 * SLAB_TIME * SLAB_TIME
    diagonal = 1.0 + SLAB_TIME * own + half_square * (own * own + product)
    mixing = couple * (SLAB_TIME + half_square * (own + partner))
    lane = lax.broadcasted_iota(jnp.int32, (CZ, 128), 1)
    even = (lane & CHUNK) == 0
    left_half = lane < 64

    state = None
    states = [jnp.zeros((CZ, 128), F32)]
    for s in range(SLABS):
        both = left(zf, g[pl.ds(s * BLOCKS * 8, BLOCKS * 8)])
        source = both[:CZ] + rolled(both[CZ:], 64, 1)
        if state is None:
            state = source
        else:
            swapped = jnp.where(even, rolled(state, -CHUNK, 1), rolled(state, CHUNK, 1))
            state = diagonal * state + mixing * swapped + source
        state = jnp.where(left_half, state, 0.0)
        states.append(state)
    for s in range(SLABS):
        packed = states[s] + rolled(states[s + 1], 64, 1)
        out[pl.ds(s * CZ, CZ)] = left(zb, packed)


def paired(x, axis):
    index = lax.broadcasted_iota(jnp.int32, x.shape, axis)
    return x + jnp.where((index & 1) == 0, rolled(x, -1, axis), rolled(x, 1, axis))


def end_kernel(second_hbm, low_hbm, high_hbm, second_out, mean_out, second, low, high, end, mean_s, in_sem, out_sem):
    loads = []
    for f in range(4):
        far = pl.ds(2 * PLANE, 4 * PLANE)
        moves = ((second_hbm.at[f], second), (low_hbm.at[f, far], low), (high_hbm.at[f, far], high))
        for i, (source, target) in enumerate(moves):
            load = pltpu.make_async_copy(source, target.at[f], in_sem.at[f, i])
            load.start()
            loads.append(load)
    stores = []
    for f in range(4):
        for load in loads[3 * f:3 * f + 3]:
            load.wait()
        for k in range(COARSE):
            values = []
            for p in (2 * k, 2 * k + 1):
                value = second[f, pl.ds(p * PLANE, PLANE)]
                if p < 4:
                    value = value + low[f, pl.ds(p * PLANE, PLANE)]
                else:
                    value = value + high[f, pl.ds((p - 4) * PLANE, PLANE)]
                values.append(value)
            mean = paired(paired(0.125 * (values[0] + values[1]), 0), 1)
            mean_s[f, pl.ds(k * PLANE, PLANE)] = mean
            for i in range(2):
                end[f, pl.ds((2 * k + i) * PLANE, PLANE)] = values[i] - mean
        for i, (source, target) in enumerate(((end, second_out), (mean_s, mean_out))):
            store = pltpu.make_async_copy(source.at[f], target.at[f], out_sem.at[f, i])
            store.start()
            stores.append(store)
    for store in stores:
        store.wait()


def middle_kernel(flags, first_hbm, low_hbm, high_hbm, mean_hbm, u_hbm, out_hbm, first, low, high, mean, u, out, in_sem, out_sem):
    mu = flags[0]
    loads = []
    for f in range(4):
        near = pl.ds(0, 2 * PLANE)
        moves = ((first_hbm.at[f], first), (low_hbm.at[f, near], low), (high_hbm.at[f, near], high), (mean_hbm.at[f], mean), (u_hbm.at[0, f], u))
        for i, (source, target) in enumerate(moves):
            load = pltpu.make_async_copy(source, target.at[f], in_sem.at[f, i])
            load.start()
            loads.append(load)
    stores = []
    for f in range(4):
        for load in loads[5 * f:5 * f + 5]:
            load.wait()
        for k in range(COARSE):
            pair = [pl.ds((2 * k + i) * PLANE, PLANE) for i in range(2)]
            start = paired(paired((0.125 * mu) * (u[f, pair[0]] + u[f, pair[1]]), 0), 1)
            middle = 0.5 * (mean[f, pl.ds(k * PLANE, PLANE)] + start)
            for i, rows in enumerate(pair):
                p = 2 * k + i
                value = first[f, rows] - middle
                if p < 2:
                    value = value + low[f, pl.ds(p * PLANE, PLANE)]
                if p >= FINE - 2:
                    value = value + high[f, pl.ds((p - FINE + 2) * PLANE, PLANE)]
                out[f, rows] = value
        store = pltpu.make_async_copy(out.at[f], out_hbm.at[f], out_sem.at[f])
        store.start()
        stores.append(store)
    for store in stores:
        store.wait()


def doubled(x):
    return jnp.concatenate([x[(p // 2) * PLANE:(p // 2 + 1) * PLANE] for p in range(FINE)], axis=0)


def nodes_kernel(flags, modes, first_hbm, second_hbm, before_hbm, yb, xb, u_hbm, out, h_s, first, second, before, u, out_s, in_sem, sem):
    leading = 1.0 - flags[0]
    loads = []
    for f in range(4):
        moves = ((first_hbm.at[f], first), (second_hbm.at[f], second), (before_hbm.at[f], before), (u_hbm.at[0, f], u))
        for i, (source, target) in enumerate(moves):
            load = pltpu.make_async_copy(source, target.at[f], in_sem.at[f, i])
            load.start()
            loads.append(load)
    for r in range(8):
        values = [modes[pl.ds(t * 64 + r * 8, 8)] for t in range(SLABS)]
        for g, value in enumerate(chunk_transpose(values)):
            h_s[g, pl.ds(r * 8, 8)] = value
    stores = []
    for f in range(4):
        start = right(left(yb, h_s[f]), xb)
        end = right(left(yb, h_s[4 + f]), xb)
        for load in loads[4 * f:4 * f + 4]:
            load.wait()
        out_s[0, f] = before[f] + leading * u[f] + doubled(start)
        out_s[1, f] = first[f] + doubled(0.5 * (start + end))
        out_s[2, f] = second[f] + doubled(end)
        for n in range(3):
            store = pltpu.make_async_copy(out_s.at[n, f], out.at[n, f], sem.at[n, f])
            store.start()
            stores.append(store)
    for store in stores:
        store.wait()


VM = pl.BlockSpec(memory_space=pltpu.VMEM)
SM = pl.BlockSpec(memory_space=pltpu.SMEM)
ANY = pl.BlockSpec(memory_space=pl.ANY)


GRANT = 60
END_COST = 60
MODE_COST = 20
MIDDLE_COST = 5


def params(mib):
    return pltpu.CompilerParams(vmem_limit_bytes=mib << 20)


def cost(microseconds):
    return pl.CostEstimate(flops=int(microseconds * 1e9), bytes_accessed=0, transcendentals=0)


def shape(*sizes):
    return jax.ShapeDtypeStruct(sizes, F32)


def scratch(*sizes):
    return pltpu.VMEM(sizes, F32)


def like(constant):
    return pltpu.VMEM(constant.shape, constant.dtype)


def per_device(fine_nodes, heating):
    u = fine_nodes.reshape(3, 4, OWN, NX)
    heat = heating.reshape(OWN, NX)
    tm = lax.axis_index("tm")
    space = lax.axis_index("space")
    flags = jnp.stack([tm > 0, space > 0, space < BLOCKS - 1, space < 0]).astype(F32)
    field = (4, OWN, NX)
    spill = (4, 6 * PLANE, NX)
    near = (4, 2 * PLANE, NX)
    far = (4, 4 * PLANE, NX)
    half = (4, OWN // 2, NX)
    tables = (STEP1, STEP2, ALONG, DOWN_C, DOWN_S, DOWN_U, X0, X1, LAM_XY)
    up_pairs = [(i, i + 1) for i in range(BLOCKS - 1)]
    down_pairs = [(i + 1, i) for i in range(BLOCKS - 1)]
    dma = pltpu.SemaphoreType.DMA

    with jax.named_scope("fine"):
        first_c, second_c, up, down, packet = pl.pallas_call(
            fine_kernel,
            out_shape=[shape(*field), shape(*field), shape(*spill), shape(*spill),
                       shape(SLABS * BLOCKS, 8, 128)],
            in_specs=[SM] + [ANY] * (2 + len(tables)),
            out_specs=[ANY] * 5,
            scratch_shapes=[scratch(3, 4, OWN, NX), scratch(OWN, NX)] + [like(table) for table in tables] + [
                scratch(*field),
                scratch(4, 12 * PLANE, NX),
                scratch(4, 12 * PLANE, NX),
                scratch(4, 16 * PLANE, NX),
                scratch(4, 10 * CY, NX),
                scratch(4, 12 * CY, NX),
                scratch(4, 8 * CY, NX),
                scratch(4, 10 * CY, CX),
                scratch(4, 8 * CY, CX),
                scratch(4, 4 * CY, CX),
                scratch(4, 16 * CY, CX),
                scratch(SLABS * BLOCKS, 8, 128),
                dma((10,)), dma((3, 4)), dma((4, 6)), dma,
            ],
            compiler_params=params(GRANT),
        )(flags, u, heat, *tables)

    with jax.named_scope("to_modes"):
        modes = lax.all_to_all(packet, AXES, 0, 0, tiled=True)

    with jax.named_scope("spill"):
        low = lax.ppermute(up, "space", up_pairs)
        high = lax.ppermute(down, "space", down_pairs)

    with jax.named_scope("end"):
        second, mean = pl.pallas_call(
            end_kernel,
            out_shape=[shape(*field), shape(*half)],
            in_specs=[ANY] * 3,
            out_specs=[ANY] * 2,
            scratch_shapes=[scratch(*field), scratch(*far), scratch(*far), scratch(*field), scratch(*half), dma((4, 3)), dma((4, 2))],
            cost_estimate=cost(END_COST),
            compiler_params=params(GRANT),
        )(second_c, low, high)

    with jax.named_scope("pass"):
        before = lax.ppermute(second, "tm", [(i, i + 1) for i in range(SLABS - 1)])

    with jax.named_scope("modes"):
        lam_xy = lax.dynamic_slice(jnp.asarray(MODE_XY), (tm * BLOCKS + space, 0), (1, 128))
        solved = pl.pallas_call(
            mode_kernel,
            out_shape=shape(SLABS * CZ, 128),
            in_specs=[VM] * 6,
            out_specs=VM,
            cost_estimate=cost(MODE_COST),
            compiler_params=params(16),
        )(modes.reshape(SLABS * BLOCKS * 8, 128), lam_xy, LAM_Z_COLUMN, LANES, ZF, ZB)

    with jax.named_scope("middle"):
        first = pl.pallas_call(
            middle_kernel,
            out_shape=shape(*field),
            in_specs=[SM] + [ANY] * 5,
            out_specs=ANY,
            scratch_shapes=[scratch(*field), scratch(*near), scratch(*near), scratch(*half), scratch(*field), scratch(*field),
                            dma((4, 5)), dma((4,))],
            cost_estimate=cost(MIDDLE_COST),
            compiler_params=params(GRANT),
        )(flags, first_c, low, high, mean, u)

    with jax.named_scope("from_modes"):
        solved = solved.reshape(SLABS * BLOCKS, COARSE, 128)
        back = lax.all_to_all(solved, AXES, 0, 0, tiled=True).reshape(SLABS * CZ, 128)

    with jax.named_scope("nodes"):
        out = pl.pallas_call(
            nodes_kernel,
            out_shape=shape(3, *field),
            in_specs=[SM, VM, ANY, ANY, ANY, VM, VM, ANY],
            out_specs=ANY,
            scratch_shapes=[scratch(8, 64, 128)] + [scratch(*field)] * 4 + [scratch(3, *field), dma((4, 4)), dma((3, 4))],
            cost_estimate=cost(5),
            compiler_params=params(GRANT),
        )(flags, back, first, second, before, YB, XB, u)
    return out.reshape(1, 3, 4, FINE, NY, NX)


def solution(mesh):
    in_specs = (P("tm", None, None, "space", None, None), P("space", None, None))
    out_specs = P("tm", None, None, "space", None, None)
    return jax.shard_map(
        per_device, mesh=mesh, in_specs=in_specs, out_specs=out_specs, check_vma=False
    )
```

time: 110 us -> 79.8 us (0.73)
  waiting for transfers between devices: 37.8 us -> 20.7 us
  blocking collectives: 16.2 us -> 0 us
  starting transfers between devices: 21.6 us -> 30.2 us
  local copies, waits for them, and re-layouts: 10 us -> 2.65 us
  Pallas kernels: 23.9 us -> 25.2 us
    all_to_all x1, waiting for transfers between devices: 26.4 us -> 4.09 us  [per_device(): modes = lax.all_to_all(packet, AXES, 0, 0, tiled=True)]
    all_to_all x0 -> x1, waiting for transfers between devices: none -> 16.3 us  [per_device(): lax.all_to_all(solved, AXES, 0, 0, tiled=True).reshape(SLABS * CZ, 128)]
    all_to_all x1 -> x0, blocking collectives: 16.2 us -> none  [per_device(): lax.all_to_all(solved, AXES, 0, 0, tiled=True).reshape(SLABS * CZ, 128)]
    ppermute x2, waiting for transfers between devices: 11.4 us -> 0.33 us  [the longest x1 0.32 us: per_device(): high = lax.ppermute(down, 'space', down_pairs)]
    all_to_all x0 -> x1, starting transfers between devices: none -> 8.29 us  [per_device(): lax.all_to_all(solved, AXES, 0, 0, tiled=True).reshape(SLABS * CZ, 128)]
    unnamed x36 -> x16, local copies, waits for them, and re-layouts: 9.34 us -> 1.95 us
    pallas_call x2 -> x3, Pallas kernels: 7.68 us -> 11.1 us  [the longest x1 4.78 us: per_device(): pl.pallas_call(nodes_kernel, out_shape=shape(3, *field), in_specs=[SM, VM...]
    pallas_call x1, Pallas kernels: 14.1 us -> 12.3 us  [per_device(): pl.pallas_call(fine_kernel, out_shape=[shape(*field), shape(*field), shap...]
  transfers between devices with their start and end apart: 4 -> 5, of which waited for: 3 -> 3; matrix products, arithmetic and copies ran while one was open for 1% -> 1% of each run, Pallas kernels for 2% -> 10%
where the time goes in v2:
time: 79.8 us; the launch traced here: 79.4 us
  starting transfers between devices  30.2 us (38%)
  Pallas kernels  25.2 us (32%)
  waiting for transfers between devices  20.7 us (26%)
  local copies, waits for them, and re-layouts  2.65 us (3%)
    all_to_all x1, waiting for transfers between devices, per_device(): lax.all_to_all(solved, AXES, 0, 0, tiled=True).reshape(SLABS * CZ, 128)  16.3 us
    pallas_call x1, Pallas kernels, per_device(): pl.pallas_call(fine_kernel, out_shape=[shape(*field), shape(*field), shap...  12.3 us
    all_to_all x1, starting transfers between devices, per_device(): modes = lax.all_to_all(packet, AXES, 0, 0, tiled=True)  10.5 us
    all_to_all x1, starting transfers between devices, per_device(): lax.all_to_all(solved, AXES, 0, 0, tiled=True).reshape(SLABS * CZ, 128)  8.29 us
    ppermute x1, starting transfers between devices, per_device(): before = lax.ppermute(second, 'tm', [(i, i + 1) for i in range(SLABS - 1)])  4.81 us
    pallas_call x1, Pallas kernels, per_device(): pl.pallas_call(nodes_kernel, out_shape=shape(3, *field), in_specs=[SM, VM...  4.78 us
    ppermute x1, starting transfers between devices, per_device(): low = lax.ppermute(up, 'space', up_pairs)  4.6 us
    all_to_all x1, waiting for transfers between devices, per_device(): modes = lax.all_to_all(packet, AXES, 0, 0, tiled=True)  4.09 us
  transfers between devices with their start and end apart: 5, of which 3 were waited for; matrix products, arithmetic and copies ran while one was open for 1% of the time, Pallas kernels for 10%

profile of v2, /device:TPU:1, one launch (start us, length us, event | category | flops | bytes accessed | tf_op | source)
XLA Modules:
  0.0 79.4 jit_solution(7598140968686889281)
XLA Ops:
  0.0 0.6 add_convert_fusion.flags
  0.6 12.3 %fine.1 = (f32[4,256,256]{2,1,0:T(8,128)}, f32[4,256,256]{2,1,0:T(8,128)}, f32[4,192,256]{2,1,0:T(8,128)}, f32[4,192,256]{2,1,0:T(8,128)}, f32[128,8,128]{2,1,0:T(8,128)}) custom-call(f32[4]{0:T(128)} %add_convert_fusion.flags, f32[3,4,256,256]{3,2,1,0:T(8,128)} %bitcast.11, f32[256,256]{1,0:T(8,128)} %bitcast.14, ...), custom_call_target="tpu_custom_call" | custom-call | tf_op jit(solution)/shard_map/fine/pallas_call | solution.py:621
  13.0 4.6 %collective-permute-start = (f32[4,192,256]{2,1,0:T(8,128)}, f32[4,192,256]{2,1,0:T(8,128)S(1)}, u32[]{:S(2)}, u32[]{:S(2)}) collective-permute-start(f32[4,192,256]{2,1,0:T(8,128)} %get-tuple-element.14), channel_id=1, source_target_pairs={{0,1},{1,2},{2,3},{3,4},{4,5},{5,6},{6,7},{7,8},{8,9},{9,10},{10,1... | collective-permute-start | bytes 2359304 | tf_op jit(solution)/shard_map/spill/ppermute | solution.py:649
  17.6 1.9 %collective-permute-start.1 = (f32[4,192,256]{2,1,0:T(8,128)}, f32[4,192,256]{2,1,0:T(8,128)S(1)}, u32[]{:S(2)}, u32[]{:S(2)}) collective-permute-start(f32[4,192,256]{2,1,0:T(8,128)} %get-tuple-element.15), channel_id=1, source_target_pairs={{1,0},{2,1},{3,2},{4,3},{5,4},{6,5},{7,6},{8,7},{9,8},{10,9},{11,1... | collective-permute-start | bytes 2359304 | tf_op jit(solution)/shard_map/spill/ppermute | solution.py:650
  19.5 10.5 %all-to-all-start = ((f32[128,8,128]{2,1,0:T(8,128)}), f32[128,8,128]{2,1,0:T(8,128)S(1)}, u32[]{:S(2)}, u32[]{:S(2)}) async-start(f32[128,8,128]{2,1,0:T(8,128)} %get-tuple-element.12), calls=%async_computation | async-start | bytes 1048576 | tf_op jit(solution)/shard_map/to_modes/all_to_all | solution.py:646
  30.1 0.7 constant_dynamic-slice_fusion.lam_xy
  30.8 0.0 collective-permute-done.low_hbm
  30.8 0.0 copy-start.6
  30.8 0.3 collective-permute-done.1.high_hbm
  31.1 0.0 copy-start.7
  31.1 0.6 copy-done.6
  31.7 0.3 copy-done.7
  32.0 0.0 copy-start
  32.0 0.0 copy-start.1
  32.0 0.0 copy-start.2
  32.0 0.0 copy-start.3
  32.0 2.7 %end.1 = (f32[4,256,256]{2,1,0:T(8,128)}, f32[4,128,256]{2,1,0:T(8,128)}) custom-call(f32[4,256,256]{2,1,0:T(8,128)} %get-tuple-element.16.second_hbm, f32[4,192,256]{2,1,0:T(8,128)} %copy-done.6, f32[4,192,256]{2,1,0:T(8,128)} %copy-done.7), custom_call_target="tpu_custom_call" | custom-call | flops 60000002048 | tf_op jit(solution)/shard_map/end/pallas_call | solution.py:653
  34.7 4.8 %collective-permute-start.2 = (f32[4,256,256]{2,1,0:T(8,128)}, f32[4,256,256]{2,1,0:T(8,128)S(1)}, u32[]{:S(2)}, u32[]{:S(2)}) collective-permute-start(f32[4,256,256]{2,1,0:T(8,128)} %get-tuple-element.18.second_hbm), channel_id=1, source_target_pairs={{0,16},{16,32},{32,48},{48,64},{64,80},{80,96},{96,112},{1,17},{17... | collective-permute-start | bytes 3145736 | tf_op jit(solution)/shard_map/pass/ppermute | solution.py:664
  39.5 4.1 %all-to-all-done = f32[128,8,128]{2,1,0:T(8,128)S(1)} async-done(((f32[128,8,128]{2,1,0:T(8,128)}), f32[128,8,128]{2,1,0:T(8,128)S(1)}, u32[]{:S(2)}, u32[]{:S(2)}) %all-to-all-start) | async-done | bytes 524320 | tf_op jit(solution)/shard_map/to_modes/all_to_all | solution.py:646
  43.6 0.0 copy-done
  43.6 0.0 copy-done.1
  43.6 0.0 copy-done.2
  43.6 0.0 copy-done.3
  43.6 1.8 %modes.1 = f32[512,128]{1,0:T(8,128)} custom-call(f32[1024,128]{1,0:T(8,128)S(1)} %bitcast.10, f32[1,128]{1,0:T(1,128)S(1)} %constant_dynamic-slice_fusion.lam_xy, f32[64,128]{1,0:T(8,128)S(1)} %copy-done.2, f32[8,128]{1,0:T(8,128)S(1)} %copy-done.3, bf16[2,128,128]{2,1,0:T(8,128)(2,1)S(1)} %copy-done, bf16[2,64,64]{2,1,0:T(8,128)(2,1)S(1)} %copy-done.1), custom_call_target="tpu_custom_call" | custom-call | flops 20000000000 | tf_op jit(solution)/shard_map/modes/pallas_call | solution.py:668
  45.4 8.3 %all-to-all-start.1 = ((f32[128,4,128]{2,1,0:T(4,128)}), f32[128,4,128]{2,1,0:T(4,128)S(1)}, u32[]{:S(2)}, u32[]{:S(2)}) async-start(f32[128,4,128]{2,1,0:T(4,128)} %bitcast.7), calls=%async_computation.1 | async-start | bytes 524288 | tf_op jit(solution)/shard_map/from_modes/all_to_all | solution.py:691
  53.7 3.6 %middle.1.first_hbm = f32[4,256,256]{2,1,0:T(8,128)} custom-call(f32[4]{0:T(128)} %add_convert_fusion.flags, f32[4,256,256]{2,1,0:T(8,128)} %get-tuple-element.13.first_hbm, f32[4,192,256]{2,1,0:T(8,128)} %copy-done.6, f32[4,192,256]{2,1,0:T(8,128)} %copy-done.7, f32[4,128,256]{2,1,0:T(8,128)} %get-tuple-element.17.mean_hbm, f32[3,4,256,256]{3,2,1,0:T(8,128)} %bitcast.12), custom_call_target="tpu_custom_call" | custom-call | flops 5000000000 | tf_op jit(solution)/shard_map/middle/pallas_call | solution.py:678
  57.3 16.3 %all-to-all-done.1 = f32[128,4,128]{2,1,0:T(4,128)S(1)} async-done(((f32[128,4,128]{2,1,0:T(4,128)}), f32[128,4,128]{2,1,0:T(4,128)S(1)}, u32[]{:S(2)}, u32[]{:S(2)}) %all-to-all-start.1) | async-done | bytes 262176 | tf_op jit(solution)/shard_map/from_modes/all_to_all | solution.py:691
  73.6 0.0 collective-permute-done.2.before_hbm
  73.6 0.0 copy-start.5
  73.6 0.7 copy-done.4
  74.3 0.4 copy-done.5
  74.7 4.8 %nodes.1 = f32[3,4,256,256]{3,2,1,0:T(8,128)} custom-call(f32[4]{0:T(128)} %add_convert_fusion.flags, f32[512,128]{1,0:T(8,128)} %bitcast.15, f32[4,256,256]{2,1,0:T(8,128)} %middle.1.first_hbm, f32[4,256,256]{2,1,0:T(8,128)} %get-tuple-element.18.second_hbm, f32[4,256,256]{2,1,0:T(8,128)} %copy-done.5, bf16[2,128,64]{2,1,0:T(8,128)(2,1)} %constant.63.clone.yb, ...), custom_call_target="tpu_custom_call" | custom-call | flops 5000000000 | tf_op jit(solution)/shard_map/nodes/pallas_call | solution.py:694
  (1 shorter events, 0.0 us)
Async XLA Ops:
  13.0 17.8 %collective-permute-start = (f32[4,192,256]{2,1,0:T(8,128)}, f32[4,192,256]{2,1,0:T(8,128)S(1)}, u32[]{:S(2)}, u32[]{:S(2)}) collective-permute-start(f32[4,192,256]{2,1,0:T(8,128)} %get-tuple-element.14), channel_id=1, source_target_pairs={{0,1},{1,2},{2,3},{3,4},{4,5},{5,6},{6,7},{7,8},{8,9},{9,10},{10,1... | collective-permute-start | bytes 2359304 | tf_op jit(solution)/shard_map/spill/ppermute | solution.py:649
  17.6 13.5 %collective-permute-start.1 = (f32[4,192,256]{2,1,0:T(8,128)}, f32[4,192,256]{2,1,0:T(8,128)S(1)}, u32[]{:S(2)}, u32[]{:S(2)}) collective-permute-start(f32[4,192,256]{2,1,0:T(8,128)} %get-tuple-element.15), channel_id=1, source_target_pairs={{1,0},{2,1},{3,2},{4,3},{5,4},{6,5},{7,6},{8,7},{9,8},{10,9},{11,1... | collective-permute-start | bytes 2359304 | tf_op jit(solution)/shard_map/spill/ppermute | solution.py:650
  19.5 24.1 %all-to-all-start = ((f32[128,8,128]{2,1,0:T(8,128)}), f32[128,8,128]{2,1,0:T(8,128)S(1)}, u32[]{:S(2)}, u32[]{:S(2)}) async-start(f32[128,8,128]{2,1,0:T(8,128)} %get-tuple-element.12), calls=%async_computation | async-start | bytes 1048576 | tf_op jit(solution)/shard_map/to_modes/all_to_all | solution.py:646
  30.8 0.9 %copy-start.6 = (f32[4,192,256]{2,1,0:T(8,128)}, f32[4,192,256]{2,1,0:T(8,128)S(1)}, u32[]{:S(2)}) copy-start(f32[4,192,256]{2,1,0:T(8,128)S(1)} %collective-permute-done.low_hbm) | copy-start | bytes 2359300
  31.1 0.9 %copy-start.7 = (f32[4,192,256]{2,1,0:T(8,128)}, f32[4,192,256]{2,1,0:T(8,128)S(1)}, u32[]{:S(2)}) copy-start(f32[4,192,256]{2,1,0:T(8,128)S(1)} %collective-permute-done.1.high_hbm) | copy-start | bytes 2359300
  32.0 11.6 %copy-start = (bf16[2,128,128]{2,1,0:T(8,128)(2,1)S(1)}, bf16[2,128,128]{2,1,0:T(8,128)(2,1)}, u32[]{:S(2)}) copy-start(bf16[2,128,128]{2,1,0:T(8,128)(2,1)} %constant.61.clone.zf) | copy-start | bytes 196612
  32.0 11.6 %copy-start.1 = (bf16[2,64,64]{2,1,0:T(8,128)(2,1)S(1)}, bf16[2,64,64]{2,1,0:T(8,128)(2,1)}, u32[]{:S(2)}) copy-start(bf16[2,64,64]{2,1,0:T(8,128)(2,1)} %constant.62.clone.zb) | copy-start | bytes 49156
  32.0 11.6 %copy-start.2 = (f32[64,128]{1,0:T(8,128)S(1)}, f32[64,128]{1,0:T(8,128)}, u32[]{:S(2)}) copy-start(f32[64,128]{1,0:T(8,128)} %constant.59.clone.lam_z) | copy-start | bytes 98308
  32.0 11.6 %copy-start.3 = (f32[8,128]{1,0:T(8,128)S(1)}, f32[8,128]{1,0:T(8,128)}, u32[]{:S(2)}) copy-start(f32[8,128]{1,0:T(8,128)} %constant.60.clone.lanes) | copy-start | bytes 12292
  34.7 38.9 %collective-permute-start.2 = (f32[4,256,256]{2,1,0:T(8,128)}, f32[4,256,256]{2,1,0:T(8,128)S(1)}, u32[]{:S(2)}, u32[]{:S(2)}) collective-permute-start(f32[4,256,256]{2,1,0:T(8,128)} %get-tuple-element.18.second_hbm), channel_id=1, source_target_pairs={{0,16},{16,32},{32,48},{48,64},{64,80},{80,96},{96,112},{1,17},{17... | collective-permute-start | bytes 3145736 | tf_op jit(solution)/shard_map/pass/ppermute | solution.py:664
  45.4 28.2 %all-to-all-start.1 = ((f32[128,4,128]{2,1,0:T(4,128)}), f32[128,4,128]{2,1,0:T(4,128)S(1)}, u32[]{:S(2)}, u32[]{:S(2)}) async-start(f32[128,4,128]{2,1,0:T(4,128)} %bitcast.7), calls=%async_computation.1 | async-start | bytes 524288 | tf_op jit(solution)/shard_map/from_modes/all_to_all | solution.py:691
  73.6 0.7 copy-start.4
  73.6 1.1 %copy-start.5 = (f32[4,256,256]{2,1,0:T(8,128)}, f32[4,256,256]{2,1,0:T(8,128)S(1)}, u32[]{:S(2)}) copy-start(f32[4,256,256]{2,1,0:T(8,128)S(1)} %collective-permute-done.2.before_hbm) | copy-start | bytes 3145732

commit v3 on v2

v3 whole, which is shorter than its diff:
```python
import numpy as np
import jax
import jax.numpy as jnp
from jax import lax
from jax.experimental import pallas as pl
from jax.experimental.pallas import tpu as pltpu
from jax.sharding import PartitionSpec as P

VISCOSITY = 0.4
DIFFUSIVITY = 0.3
SLAB_TIME = 0.25
HALF_TIME = 0.125

SLABS = 8
BLOCKS = 16
NZ, NY, NX = 128, 32, 256
CZ, CY, CX = NZ // 2, NY // 2, NX // 2
FINE = NZ // BLOCKS
COARSE = CZ // BLOCKS
CHUNK = CX // SLABS
SPILL = 5
AXES = ("tm", "space")
F32 = jnp.float32
BF16 = jnp.bfloat16


def real_basis(count):
    j = np.arange(count)
    rows, values = [], []
    for k in range(count):
        theta = 2.0 * np.pi * k / count
        if k == 0:
            row = np.ones(count)
        elif 2 * k == count:
            row = np.cos(np.pi * j)
        elif 2 * k < count:
            row = np.cos(theta * j) * np.sqrt(2.0)
        else:
            row = np.sin(theta * j) * np.sqrt(2.0)
        rows.append(row / np.sqrt(count))
        values.append((32.0 * np.cos(theta) - 2.0 * np.cos(2.0 * theta) - 30.0) / 48.0)
    return np.array(rows), np.array(values)


def pairs(count):
    return np.repeat(np.eye(count), 2, axis=0)


def circulant(count):
    eye = np.eye(count)
    return (
        16.0 * (np.roll(eye, 1, 0) + np.roll(eye, -1, 0))
        - (np.roll(eye, 2, 0) + np.roll(eye, -2, 0))
        - 30.0 * eye
    )


def split(matrix):
    matrix = np.asarray(matrix, np.float32)
    high = matrix.astype(jnp.bfloat16)
    low = (matrix - high.astype(np.float32)).astype(jnp.bfloat16)
    return np.stack([high, low])


FY, LAM_Y = real_basis(CY)
FX, LAM_X = real_basis(CX)


def depth_basis():
    eye = np.eye(CZ)
    band = -30.0 * eye
    for offset, weight in ((1, 16.0), (2, -1.0)):
        band += weight * (np.eye(CZ, k=offset) + np.eye(CZ, k=-offset))
    values, vectors = np.linalg.eigh(band / 48.0)
    return values, vectors


LAM_Z, QZ = depth_basis()

DOWN_X = (FX @ pairs(CX).T * 0.5).T
DOWN_XL = circulant(NX) @ DOWN_X
UP_Y = pairs(CY) @ FY.T
UP_X = FX @ pairs(CX).T


def exact(matrix):
    high = np.asarray(matrix, np.float32).astype(jnp.bfloat16)
    assert np.array_equal(high.astype(np.float64), matrix)
    return high


def stacked(matrix):
    return split(matrix).reshape(-1, matrix.shape[1])


ALONG = exact(circulant(NX))
PLANES = 11
F11 = stacked(np.kron(np.eye(PLANES), FY))
X0 = split(DOWN_X)
X1 = split(DOWN_XL)
LAM_XY = (LAM_Y[:, None] + LAM_X[None, :]).astype(np.float32)


def depth_forward():
    table = np.zeros((2, CZ, BLOCKS, 8))
    for half in range(2):
        for block in range(BLOCKS):
            for slot in range(8):
                z = block * COARSE + half * 8 + slot - SPILL
                if 0 <= z < CZ:
                    table[half, :, block, slot] = QZ[z]
    return table.reshape(2 * CZ, BLOCKS * 8)


ZF = split(depth_forward())
ZB = split(QZ)


def up_y_table():
    table = np.zeros((COARSE, NY, CY, COARSE))
    for z in range(COARSE):
        table[z, :, :, z] = UP_Y
    return table.reshape(COARSE * NY, CY * COARSE)


YB = split(up_y_table())
XB = split(UP_X)


def mode_values():
    table = np.zeros((SLABS, BLOCKS, 2, 4, CHUNK))
    for t in range(SLABS):
        for p in range(BLOCKS):
            table[t, p] = LAM_Y[p] + LAM_X[t * CHUNK:(t + 1) * CHUNK]
    return table.reshape(SLABS * BLOCKS, 128).astype(np.float32)


def lane_constants():
    own = np.array([VISCOSITY, VISCOSITY, VISCOSITY, DIFFUSIVITY])
    partner = np.array([VISCOSITY, VISCOSITY, DIFFUSIVITY, VISCOSITY])
    couple = np.array([2.0, -2.0, 1.0, 1.0])
    product = np.array([-4.0, -4.0, 1.0, 1.0])
    table = np.zeros((8, 2, 4, CHUNK))
    for row, values in enumerate((own, partner, couple, product)):
        table[row] = values[None, :, None]
    return table.reshape(8, 128).astype(np.float32)


MODE_XY = mode_values()
LANES = lane_constants()
LAM_Z_COLUMN = np.repeat(LAM_Z[:, None], 128, axis=1).astype(np.float32)


def halves(x):
    high = x.astype(BF16)
    return high, (x - high.astype(F32)).astype(BF16)


def dot(a, b):
    return jnp.dot(a, b, preferred_element_type=F32)


def left(table, x):
    high, low = halves(x)
    return dot(table[0], high) + (dot(table[0], low) + dot(table[1], high))


def right(x, table):
    high, low = halves(x)
    return dot(high, table[0]) + (dot(low, table[0]) + dot(high, table[1]))


def rolled(x, by, axis):
    return pltpu.roll(x, by % x.shape[axis], axis)


def across_y(x):
    near = rolled(x, 1, 0) + rolled(x, -1, 0)
    far = rolled(x, 2, 0) + rolled(x, -2, 0)
    return 16.0 * near - far


def total(terms):
    out = terms[0]
    for term in terms[1:]:
        out = out + term
    return out


def chunk_transpose(values):
    values = list(values)
    lane = lax.broadcasted_iota(jnp.int32, values[0].shape, 1)
    for bit in (1, 2, 4):
        shift = CHUNK * bit
        low = (lane & shift) == 0
        for i in range(8):
            if i & bit:
                continue
            j = i | bit
            first, second = values[i], values[j]
            values[i] = jnp.where(low, first, rolled(second, shift, 1))
            values[j] = jnp.where(low, rolled(first, -shift, 1), second)
    return values


def left_stacked(table, x):
    high, low = halves(x)
    rows = table.shape[0] // 2
    both = dot(table, high)
    return both[:rows] + (both[rows:] + dot(table[:rows], low))


PLANE = NY
OWN = FINE * PLANE


def position():
    tm, space = lax.axis_index("tm"), lax.axis_index("space")
    one = jnp.float32(1.0)
    zero = jnp.float32(0.0)
    return jnp.where(tm > 0, one, zero), jnp.where(space > 0, one, zero), jnp.where(space < BLOCKS - 1, one, zero)


def fine_kernel(u_hbm, q_hbm, along_hbm, f11_hbm, x0_hbm, x1_hbm, lam_hbm,
                first_hbm, second_hbm, up_hbm, down_hbm, send_hbm,
                u, q, along, f11, x0, x1, lam,
                a_s, fe, be, se, cs, rows_s, pair_s, y_s, w_s, g_s, send_s, in_sem, u_sem, out_sem, send_sem):
    mu, keep_low, keep_high = position()
    loads = [
        pltpu.make_async_copy(source, target, in_sem.at[i])
        for i, (source, target) in enumerate((
            (along_hbm, along), (x0_hbm, x0), (x1_hbm, x1), (f11_hbm, f11), (lam_hbm, lam), (q_hbm, q)))
    ]
    node_loads = [
        [pltpu.make_async_copy(u_hbm.at[n, f], u.at[n, f], u_sem.at[n, f]) for n in range(3)] for f in range(4)
    ]
    for load in node_loads[0] + loads[:1] + node_loads[1] + loads[1:5] + node_loads[2] + node_loads[3] + loads[5:]:
        load.start()

    edge = 2 * PLANE
    middle = pl.ds(edge, OWN)
    stores = []

    def store(source, target, sem):
        copy = pltpu.make_async_copy(source, target, sem)
        copy.start()
        stores.append(copy)

    def field(f):
        nu = DIFFUSIVITY if f == 3 else VISCOSITY
        return nu, (2.0, -2.0, 1.0, 1.0)[f], f ^ 1

    def fine_plane(ref, f, p, low):
        return ref[f, pl.ds((p - low) * PLANE, PLANE)]

    def depth(ref, f, p, low, high):
        near = [fine_plane(ref, f, p + o, low) for o in (-1, 1) if low <= p + o < high]
        far = [fine_plane(ref, f, p + o, low) for o in (-2, 2) if low <= p + o < high]
        if not near:
            return -total(far)
        return 16.0 * total(near) - total(far) if far else 16.0 * total(near)

    def along_x(x):
        high, low = halves(x)
        return dot(high, along[...]) + dot(low, along[...])

    def combine(f):
        for load in node_loads[f]:
            load.wait()
        a_s[f] = (5.0 / 24.0) * u[0, f] + (1.0 / 3.0) * u[1, f] - (1.0 / 24.0) * u[2, f]

    def first_stage(f):
        nu, couple, partner = field(f)
        scale = nu * (SLAB_TIME / 12.0)
        row = along_x(a_s[f])
        for p in range(-2, FINE + 2):
            here = pl.ds((p + 2) * PLANE, PLANE)
            acc = depth(a_s, f, p, 0, FINE)
            if 0 <= p < FINE:
                own = pl.ds(p * PLANE, PLANE)
                centre = a_s[f, own]
                start = u[0, f, own]
                acc = acc + (across_y(centre) - 60.0 * centre) + row[p * PLANE:(p + 1) * PLANE]
                value = scale * acc + (couple * SLAB_TIME) * a_s[partner, own] + start
                if f == 3:
                    value = value + HALF_TIME * q[own]
                be[f, here] = 0.5 * value + ((-1.0 / 24.0) * start - (1.0 / 6.0) * u[1, f, own] + (5.0 / 24.0) * u[2, f, own])
            else:
                value = (scale * (keep_low if p < 0 else keep_high)) * acc
                be[f, here] = 0.5 * value
            fe[f, here] = value
        store(fe.at[f, middle], first_hbm.at[f], out_sem.at[f, 0])
        store(fe.at[f, pl.ds(0, edge)], down_hbm.at[f, pl.ds(0, edge)], out_sem.at[f, 1])
        store(fe.at[f, pl.ds(edge + OWN, edge)], up_hbm.at[f, pl.ds(0, edge)], out_sem.at[f, 2])

    def second_stage(f):
        nu, couple, partner = field(f)
        scale = nu * (SLAB_TIME / 12.0)
        row = along_x(be[f])
        for p in range(-4, FINE + 4):
            here = pl.ds((p + 4) * PLANE, PLANE)
            acc = depth(be, f, p, -2, FINE + 2)
            mask = keep_low if p < 0 else keep_high
            if -2 <= p < FINE + 2:
                inner = pl.ds((p + 2) * PLANE, PLANE)
                centre = be[f, inner]
                first = fe[f, inner]
                acc = acc + (across_y(centre) - 60.0 * centre) + row[(p + 2) * PLANE:(p + 3) * PLANE]
                value = scale * acc + (couple * SLAB_TIME) * be[partner, inner] + first
                if 0 <= p < FINE:
                    own = pl.ds(p * PLANE, PLANE)
                    if f == 3:
                        value = value + HALF_TIME * q[own]
                    c = (1.0 / 6.0) * (value + u[0, f, own]) + (2.0 / 3.0) * first
                else:
                    value = mask * value
                    c = (1.0 / 6.0) * value + (2.0 / 3.0) * first
            else:
                value = (scale * mask) * acc
                c = (1.0 / 6.0) * value
            se[f, here] = value
            cs[f, here] = c
        store(se.at[f, pl.ds(2 * edge, OWN)], second_hbm.at[f], out_sem.at[f, 3])
        store(se.at[f, pl.ds(0, 2 * edge)], down_hbm.at[f, pl.ds(edge, 2 * edge)], out_sem.at[f, 4])
        store(se.at[f, pl.ds(2 * edge + OWN, 2 * edge)], up_hbm.at[f, pl.ds(edge, 2 * edge)], out_sem.at[f, 5])

    def put(ref, f, k, value):
        for i in range(2):
            ref[f, i, pl.ds(k * PLANE, PLANE)] = value[:, i * 128:(i + 1) * 128]

    def every_other(ref, f, start, count):
        return jnp.concatenate([ref[f, i, pl.ds(start, count, stride=2), :] for i in range(2)], axis=1)

    def coarse_means(f):
        nu, couple, partner = field(f)
        scale = nu * (SLAB_TIME / 12.0)

        def pair_sum(ref, g, k):
            return fine_plane(ref, g, 2 * k, -4) + fine_plane(ref, g, 2 * k + 1, -4)

        for k in range(-3, COARSE + 3):
            value = None
            inside = -2 <= k < COARSE + 2
            if inside:
                mean = pair_sum(cs, f, k)
                put(pair_s, f, k + 2, mean)
                value = (-7.0 * scale) * mean + (couple * (SLAB_TIME * 0.5)) * pair_sum(cs, partner, k)
            for weight, planes in ((7.5, (2 * k - 1, 2 * k + 2)), (-0.5, (2 * k - 2, 2 * k + 3))):
                part = [fine_plane(cs, f, p, -4) for p in planes if -4 <= p < FINE + 4]
                if part:
                    part = (weight * scale) * total(part)
                    value = part if value is None else value + part
            if f == 3 and 0 <= k < COARSE:
                value = value + (0.5 * SLAB_TIME) * (q[pl.ds(2 * k * PLANE, PLANE)] + q[pl.ds((2 * k + 1) * PLANE, PLANE)])
            if k < 0:
                value = keep_low * value
            if k >= COARSE:
                value = keep_high * value
            if inside:
                last = 0.5 * pair_sum(se, f, k)
                value = value - last
                if 0 <= k < COARSE:
                    start = 0.5 * (u[0, f, pl.ds(2 * k * PLANE, PLANE)] + u[0, f, pl.ds((2 * k + 1) * PLANE, PLANE)])
                    value = value + start
                    last = last - mu * start
                    put(rows_s, f, 18 + k, start)
                put(rows_s, f, 12 + k, last)
            put(rows_s, f, k + 3, value)

    def across(f):
        nu, _, _ = field(f)
        scale = nu * (SLAB_TIME / 12.0)
        count = 22 * CY
        y = 0.5 * (every_other(rows_s, f, 0, count) + every_other(rows_s, f, 1, count))
        even = every_other(pair_s, f, 0, 8 * CY)
        odd = every_other(pair_s, f, 1, 8 * CY)
        mean = even + odd
        curved = []
        for k in range(8):
            rows = slice(k * CY, (k + 1) * CY)
            e, o = even[rows], odd[rows]
            near = rolled(o, 1, 0) + rolled(e, -1, 0)
            far = rolled(e, 1, 0) + rolled(o, -1, 0)
            value = (0.25 * scale) * (15.0 * near - far - 14.0 * mean[rows])
            if k < 2:
                value = keep_low * value
            if k >= 6:
                value = keep_high * value
            curved.append(value)
        y = jnp.concatenate([y[:CY], y[CY:9 * CY] + jnp.concatenate(curved, axis=0), y[9 * CY:]], axis=0)
        both = right(y, x0)
        bent = (0.25 * scale) * right(mean, x1)
        return jnp.concatenate([both[:CY], both[CY:9 * CY] + bent, both[9 * CY:]], axis=0)

    def to_y_modes(pair):
        both = jnp.concatenate([across(f) for f in pair], axis=1)
        half = PLANES * CY
        out = [left_stacked(f11[...], both[i * half:(i + 1) * half]) for i in range(2)]
        out = jnp.concatenate(out, axis=0)
        for i, f in enumerate(pair):
            lanes = slice(i * CX, (i + 1) * CX)
            w_s[f] = out[:18 * CY, lanes]
            y_s[f] = out[18 * CY:, lanes]

    def kept(value, p, count):
        if p < 0:
            return value * keep_low
        if p >= count:
            return value * keep_high
        return value

    def plane(ref, f, k, low, high):
        if low <= k < high:
            return ref[f, pl.ds((k - low) * CY, CY)]
        return None

    def node_plane(f, k):
        if -2 <= k < COARSE + 2:
            return w_s[f, pl.ds((12 + k) * CY, CY)]
        return None

    def coarse_slope(ref, f, k, low, high):
        nu, couple, partner = field(f)
        out = None
        for weight, offsets in ((16.0 / 48.0, (-1, 1)), (-1.0 / 48.0, (-2, 2))):
            part = [plane(ref, f, k + o, low, high) for o in offsets]
            part = [value for value in part if value is not None]
            if part:
                part = weight * total(part)
                out = part if out is None else out + part
        centre = plane(ref, f, k, low, high)
        if centre is None:
            return nu * out
        out = out + (lam[...] - 30.0 / 48.0) * centre
        return nu * out + couple * plane(ref, partner, k, low, high)

    def defect(f):
        for k in range(-2, COARSE + 2):
            value = coarse_slope(y_s, f, k, 0, COARSE)
            value = kept((mu * SLAB_TIME) * value, k, COARSE)
            rows = pl.ds((k + 3) * CY, CY)
            w_s[f, rows] = w_s[f, rows] - value

    def packet(f):
        for k in range(-SPILL, 16 - SPILL):
            rows = pl.ds((k + SPILL) * CY, CY)
            if k >= COARSE + SPILL:
                g_s[f, rows] = jnp.zeros((CY, CX), F32)
                continue
            value = kept(HALF_TIME * coarse_slope(w_s, f, k, -3, COARSE + 3), k, COARSE)
            for part in (plane(w_s, f, k, -3, COARSE + 3), node_plane(f, k)):
                if part is not None:
                    value = value + part
            g_s[f, rows] = value

    for pair in ((0, 1), (2, 3)):
        for f in pair:
            combine(f)
        if pair[0] == 0:
            loads[0].wait()
        else:
            loads[5].wait()
        for f in pair:
            first_stage(f)
        for f in pair:
            second_stage(f)
        for f in pair:
            coarse_means(f)
        if pair[0] == 0:
            for load in loads[1:5]:
                load.wait()
        to_y_modes(pair)
        for stage in (defect, packet):
            for f in pair:
                stage(f)

    def pack(p, _):
        values = []
        for half in range(2):
            for f in range(4):
                values.append(g_s[f, pl.ds(half * 8 * CY + p, 8, stride=CY), :])
        for t, value in enumerate(chunk_transpose(values)):
            send_s[t * BLOCKS + p] = value
        return 0

    lax.fori_loop(0, BLOCKS, pack, 0, unroll=8)
    store(send_s, send_hbm, send_sem)
    for copy in stores:
        copy.wait()


def mode_kernel(g, xy, lam_z, lanes, zf, zb, out):
    index = lax.axis_index("tm") * BLOCKS + lax.axis_index("space")
    lam = lam_z[...] + xy[pl.ds(index, 1)]
    nu, other, couple, product = (lanes[pl.ds(i, 1)] for i in range(4))
    own = nu * lam
    partner = other * lam
    half_square = 0.5 * SLAB_TIME * SLAB_TIME
    diagonal = 1.0 + SLAB_TIME * own + half_square * (own * own + product)
    mixing = couple * (SLAB_TIME + half_square * (own + partner))
    lane = lax.broadcasted_iota(jnp.int32, (CZ, 128), 1)
    even = (lane & CHUNK) == 0
    left_half = lane < 64

    state = None
    states = [jnp.zeros((CZ, 128), F32)]
    for s in range(SLABS):
        both = left(zf, g[pl.ds(s * BLOCKS * 8, BLOCKS * 8)])
        source = both[:CZ] + rolled(both[CZ:], 64, 1)
        if state is None:
            state = source
        else:
            swapped = jnp.where(even, rolled(state, -CHUNK, 1), rolled(state, CHUNK, 1))
            state = diagonal * state + mixing * swapped + source
        state = jnp.where(left_half, state, 0.0)
        states.append(state)
    for s in range(SLABS):
        packed = states[s] + rolled(states[s + 1], 64, 1)
        out[pl.ds(s * CZ, CZ)] = left(zb, packed)


def paired(x, axis):
    index = lax.broadcasted_iota(jnp.int32, x.shape, axis)
    return x + jnp.where((index & 1) == 0, rolled(x, -1, axis), rolled(x, 1, axis))


def block_mean(x, weight):
    return paired(paired(weight * x, 0), 1)


def middle_kernel(first_hbm, low_hbm, high_hbm, most_hbm, rest_hbm, u_hbm, first_out, second_out,
                  first, low, high, second, u, out, in_sem, out_sem):
    mu, _, _ = position()
    near = pl.ds(0, 2 * PLANE)
    loads = []
    for f in range(4):
        source = most_hbm.at[f] if f < SENT_FIRST else rest_hbm.at[f - SENT_FIRST]
        moves = ((first_hbm.at[f], first), (low_hbm.at[f, near], low), (high_hbm.at[f, near], high), (source, second), (u_hbm.at[0, f], u))
        for i, (source, target) in enumerate(moves):
            load = pltpu.make_async_copy(source, target.at[f], in_sem.at[f, i])
            load.start()
            loads.append(load)
    stores = []
    for f in range(4):
        for load in loads[5 * f:5 * f + 5]:
            load.wait()
        for k in range(COARSE):
            pair = [pl.ds((2 * k + i) * PLANE, PLANE) for i in range(2)]
            seconds = [second[f, rows] for rows in pair]
            mean = block_mean(seconds[0] + seconds[1], 0.125)
            start = block_mean(u[f, pair[0]] + u[f, pair[1]], 0.125 * mu)
            middle = 0.5 * (mean + start)
            for i, rows in enumerate(pair):
                p = 2 * k + i
                value = first[f, rows] - middle
                if p < 2:
                    value = value + low[f, pl.ds(p * PLANE, PLANE)]
                if p >= FINE - 2:
                    value = value + high[f, pl.ds((p - FINE + 2) * PLANE, PLANE)]
                out[0, f, rows] = value
                out[1, f, rows] = seconds[i] - mean
        for n, target in enumerate((first_out, second_out)):
            store = pltpu.make_async_copy(out.at[n, f], target.at[f], out_sem.at[n, f])
            store.start()
            stores.append(store)
    for store in stores:
        store.wait()


def doubled(x):
    return jnp.concatenate([x[(p // 2) * PLANE:(p // 2 + 1) * PLANE] for p in range(FINE)], axis=0)


def nodes_kernel(modes, first_hbm, second_hbm, most_hbm, rest_hbm, yb_hbm, xb_hbm, u_hbm, out, h_s, first, second, before, yb, xb, out_s, in_sem, sem):
    mu, _, _ = position()
    leading = lax.axis_index("tm") == 0
    tables = [pltpu.make_async_copy(yb_hbm, yb, in_sem.at[0, 3]), pltpu.make_async_copy(xb_hbm, xb, in_sem.at[1, 3])]
    for load in tables:
        load.start()
    for f in range(4):
        for i, (source, target) in enumerate(((first_hbm, first), (second_hbm, second))):
            pltpu.make_async_copy(source.at[f], target.at[f], in_sem.at[f, i]).start()

        @pl.when(leading)
        def _():
            pltpu.make_async_copy(u_hbm.at[0, f], before.at[f], in_sem.at[f, 2]).start()

        @pl.when(jnp.logical_not(leading))
        def _():
            source = most_hbm.at[f] if f < SENT_FIRST else rest_hbm.at[f - SENT_FIRST]
            pltpu.make_async_copy(source, before.at[f], in_sem.at[f, 2]).start()

    for r in range(8):
        values = [modes[pl.ds(t * 64 + r * 8, 8)] for t in range(SLABS)]
        for g, value in enumerate(chunk_transpose(values)):
            h_s[g, pl.ds(r * 8, 8)] = value
    for load in tables:
        load.wait()
    stores = []
    for f in range(4):
        start = right(left(yb, h_s[f]), xb)
        end = right(left(yb, h_s[4 + f]), xb)
        for i, (source, target) in enumerate(((first_hbm, first), (second_hbm, second), (second_hbm, before))):
            pltpu.make_async_copy(source.at[f], target.at[f], in_sem.at[f, i]).wait()
        for k in range(COARSE):
            pair = [pl.ds((2 * k + i) * PLANE, PLANE) for i in range(2)]
            value = [before[f, rows] for rows in pair]
            shift = start[k * PLANE:(k + 1) * PLANE] - block_mean(value[0] + value[1], 0.125 * mu)
            for i, rows in enumerate(pair):
                out_s[0, f, rows] = value[i] + shift
        out_s[1, f] = first[f] + doubled(0.5 * (start + end))
        out_s[2, f] = second[f] + doubled(end)
        for n in range(3):
            store = pltpu.make_async_copy(out_s.at[n, f], out.at[n, f], sem.at[n, f])
            store.start()
            stores.append(store)
    for store in stores:
        store.wait()


VM = pl.BlockSpec(memory_space=pltpu.VMEM)
ANY = pl.BlockSpec(memory_space=pl.ANY)


GRANT = 60
SENT_FIRST = 3
MODE_COST = 20
MIDDLE_COST = 5


def params(mib):
    return pltpu.CompilerParams(vmem_limit_bytes=mib << 20)


def cost(microseconds):
    return pl.CostEstimate(flops=int(microseconds * 1e9), bytes_accessed=0, transcendentals=0)


def shape(*sizes):
    return jax.ShapeDtypeStruct(sizes, F32)


def scratch(*sizes):
    return pltpu.VMEM(sizes, F32)


def like(constant):
    return pltpu.VMEM(constant.shape, constant.dtype)


def per_device(fine_nodes, heating):
    u = fine_nodes.reshape(3, 4, OWN, NX)
    heat = heating.reshape(OWN, NX)
    field = (4, OWN, NX)
    spill = (4, 6 * PLANE, NX)
    near = (4, 2 * PLANE, NX)
    tables = (ALONG, F11, X0, X1, LAM_XY)
    up_pairs = [(i, i + 1) for i in range(BLOCKS - 1)]
    down_pairs = [(i + 1, i) for i in range(BLOCKS - 1)]
    dma = pltpu.SemaphoreType.DMA

    with jax.named_scope("fine"):
        first_c, second_c, up, down, packet = pl.pallas_call(
            fine_kernel,
            out_shape=[shape(*field), shape(*field), shape(*spill), shape(*spill),
                       shape(SLABS * BLOCKS, 8, 128)],
            in_specs=[ANY] * (2 + len(tables)),
            out_specs=[ANY] * 5,
            scratch_shapes=[scratch(3, 4, OWN, NX), scratch(OWN, NX)] + [like(table) for table in tables] + [
                scratch(*field),
                scratch(4, 12 * PLANE, NX),
                scratch(4, 12 * PLANE, NX),
                scratch(4, 16 * PLANE, NX),
                scratch(4, 16 * PLANE, NX),
                scratch(4, 2, 22 * PLANE, 128),
                scratch(4, 2, 8 * PLANE, 128),
                scratch(4, 4 * CY, CX),
                scratch(4, 18 * CY, CX),
                scratch(4, 16 * CY, CX),
                scratch(SLABS * BLOCKS, 8, 128),
                dma((6,)), dma((3, 4)), dma((4, 6)), dma,
            ],
            compiler_params=params(GRANT),
        )(u, heat, *tables)

    with jax.named_scope("to_modes"):
        modes = lax.all_to_all(packet, AXES, 0, 0, tiled=True)

    with jax.named_scope("spill"):
        low = lax.ppermute(up, "space", up_pairs)
        high = lax.ppermute(down, "space", down_pairs)

    with jax.named_scope("end"):
        far = slice(2 * PLANE, 6 * PLANE)

        def ended(fields):
            return second_c[fields] + jnp.concatenate([low[fields, far], high[fields, far]], axis=1)

        most = ended(slice(0, SENT_FIRST))
        rest = ended(slice(SENT_FIRST, 4))

    with jax.named_scope("pass"):
        later = [(i, i + 1) for i in range(SLABS - 1)]
        most_before = lax.ppermute(most, "tm", later)

    with jax.named_scope("modes"):
        constants = (MODE_XY, LAM_Z_COLUMN, LANES, ZF, ZB)
        solved = pl.pallas_call(
            mode_kernel,
            out_shape=shape(SLABS * CZ, 128),
            in_specs=[VM] * 6,
            out_specs=VM,
            cost_estimate=cost(MODE_COST),
            compiler_params=params(16),
        )(modes.reshape(SLABS * BLOCKS * 8, 128), *constants)

    with jax.named_scope("pass_rest"):
        rest_sent, _ = lax.optimization_barrier((rest, solved))
        rest_before = lax.ppermute(rest_sent, "tm", later)

    with jax.named_scope("middle"):
        first, second = pl.pallas_call(
            middle_kernel,
            out_shape=[shape(*field)] * 2,
            in_specs=[ANY] * 6,
            out_specs=[ANY] * 2,
            scratch_shapes=[scratch(*field), scratch(*near), scratch(*near), scratch(*field), scratch(*field), scratch(2, *field),
                            dma((4, 5)), dma((2, 4))],
            cost_estimate=cost(MIDDLE_COST),
            compiler_params=params(GRANT),
        )(first_c, low, high, most, rest, u)

    with jax.named_scope("from_modes"):
        solved = solved.reshape(SLABS * BLOCKS, COARSE, 128)
        back = lax.all_to_all(solved, AXES, 0, 0, tiled=True).reshape(SLABS * CZ, 128)

    with jax.named_scope("nodes"):
        out = pl.pallas_call(
            nodes_kernel,
            out_shape=shape(3, *field),
            in_specs=[VM] + [ANY] * 7,
            out_specs=ANY,
            scratch_shapes=[scratch(8, 64, 128)] + [scratch(*field)] * 3 + [like(YB), like(XB), scratch(3, *field), dma((4, 4)), dma((3, 4))],
            cost_estimate=cost(5),
            compiler_params=params(GRANT),
        )(back, first, second, most_before, rest_before, YB, XB, u)
    return out.reshape(1, 3, 4, FINE, NY, NX)


def solution(mesh):
    in_specs = (P("tm", None, None, "space", None, None), P("space", None, None))
    out_specs = P("tm", None, None, "space", None, None)
    return jax.shard_map(
        per_device, mesh=mesh, in_specs=in_specs, out_specs=out_specs, check_vma=False
    )
```

time: 79.8 us -> 67.7 us (0.85)
  waiting for transfers between devices: 20.7 us -> 10.8 us
  Pallas kernels: 25.2 us -> 19.9 us
  starting transfers between devices: 30.2 us -> 33.3 us
    all_to_all x1, waiting for transfers between devices: 16.3 us -> 3.31 us  [per_device(): lax.all_to_all(solved, AXES, 0, 0, tiled=True).reshape(SLABS * CZ, 128)]
    ppermute x1 -> x2, starting transfers between devices: 4.81 us -> 10.5 us  [the longest x1 5.55 us: per_device(): most_before = lax.ppermute(most, 'tm', later)]
    pallas_call x3 -> x2, Pallas kernels: 11.1 us -> 8.18 us  [the longest x1 4.9 us: per_device(): pl.pallas_call(nodes_kernel, out_shape=shape(3, *field), in_specs=[VM] +...]
    all_to_all x1, starting transfers between devices: 8.29 us -> 5.57 us  [per_device(): lax.all_to_all(solved, AXES, 0, 0, tiled=True).reshape(SLABS * CZ, 128)]
    pallas_call x1, Pallas kernels: 12.3 us -> 9.9 us  [per_device(): pl.pallas_call(fine_kernel, out_shape=[shape(*field), shape(*field), shap...]
    all_to_all x1, waiting for transfers between devices: 4.09 us -> 6.5 us  [per_device(): modes = lax.all_to_all(packet, AXES, 0, 0, tiled=True)]
    slice x0 -> x4, local copies, waits for them, and re-layouts: none -> 0.98 us  [the longest x2 0.94 us: ended(): high[fields, far]]
    unnamed x16 -> x24, local copies, waits for them, and re-layouts: 1.95 us -> 1.7 us
  transfers between devices with their start and end apart: 5 -> 6, of which waited for: 3 -> 3; matrix products, arithmetic and copies ran while one was open for 1% -> 2% of each run, Pallas kernels for 10% -> 8%
where the time goes in v3:
time: 67.7 us; the launch traced here: 67.1 us
  starting transfers between devices  33.3 us (49%)
  Pallas kernels  19.9 us (29%)
  waiting for transfers between devices  10.8 us (16%)
  local copies, waits for them, and re-layouts  2.68 us (4%)
    all_to_all x1, starting transfers between devices, per_device(): modes = lax.all_to_all(packet, AXES, 0, 0, tiled=True)  10.5 us
    pallas_call x1, Pallas kernels, per_device(): pl.pallas_call(fine_kernel, out_shape=[shape(*field), shape(*field), shap...  9.9 us
    all_to_all x1, waiting for transfers between devices, per_device(): modes = lax.all_to_all(packet, AXES, 0, 0, tiled=True)  6.5 us
    all_to_all x1, starting transfers between devices, per_device(): lax.all_to_all(solved, AXES, 0, 0, tiled=True).reshape(SLABS * CZ, 128)  5.57 us
    ppermute x1, starting transfers between devices, per_device(): most_before = lax.ppermute(most, 'tm', later)  5.55 us
    ppermute x1, starting transfers between devices, per_device(): rest_before = lax.ppermute(rest_sent, 'tm', later)  4.99 us
    pallas_call x1, Pallas kernels, per_device(): pl.pallas_call(nodes_kernel, out_shape=shape(3, *field), in_specs=[VM] +...  4.9 us
    ppermute x1, starting transfers between devices, per_device(): low = lax.ppermute(up, 'space', up_pairs)  4.72 us
  transfers between devices with their start and end apart: 6, of which 3 were waited for; matrix products, arithmetic and copies ran while one was open for 2% of the time, Pallas kernels for 8%

profile of v3, /device:TPU:1, one launch (start us, length us, event | category | flops | bytes accessed | tf_op | source)
XLA Modules:
  0.0 67.1 jit_solution(7347298757193037481)
XLA Ops:
  0.0 9.9 %fine.1 = (f32[4,256,256]{2,1,0:T(8,128)}, f32[4,256,256]{2,1,0:T(8,128)}, f32[4,192,256]{2,1,0:T(8,128)}, f32[4,192,256]{2,1,0:T(8,128)}, f32[128,8,128]{2,1,0:T(8,128)}) custom-call(f32[3,4,256,256]{3,2,1,0:T(8,128)} %bitcast.7, f32[256,256]{1,0:T(8,128)} %bitcast.11, bf16[256,256]{1,0:T(8,128)(2,1)} %constant.24.clone.along_hbm, ...), custom_call_target="tpu_custom_call" | custom-call | tf_op jit(solution)/shard_map/fine/pallas_call | solution.py:663
  9.9 0.0 copy-start.5
  9.9 0.0 copy-start
  9.9 0.0 copy-start.1
  9.9 0.0 copy-start.2
  10.0 0.0 copy-start.3
  10.0 0.0 copy-start.4
  10.0 4.7 %collective-permute-start = (f32[4,192,256]{2,1,0:T(8,128)}, f32[4,192,256]{2,1,0:T(8,128)S(1)}, u32[]{:S(2)}, u32[]{:S(2)}) collective-permute-start(f32[4,192,256]{2,1,0:T(8,128)} %get-tuple-element.15), channel_id=1, source_target_pairs={{0,1},{1,2},{2,3},{3,4},{4,5},{5,6},{6,7},{7,8},{8,9},{9,10},{10,1... | collective-permute-start | bytes 2359304 | tf_op jit(solution)/shard_map/spill/ppermute | solution.py:690
  14.7 1.9 %collective-permute-start.1 = (f32[4,192,256]{2,1,0:T(8,128)}, f32[4,192,256]{2,1,0:T(8,128)S(1)}, u32[]{:S(2)}, u32[]{:S(2)}) collective-permute-start(f32[4,192,256]{2,1,0:T(8,128)} %get-tuple-element.16), channel_id=1, source_target_pairs={{1,0},{2,1},{3,2},{4,3},{5,4},{6,5},{7,6},{8,7},{9,8},{10,9},{11,1... | collective-permute-start | bytes 2359304 | tf_op jit(solution)/shard_map/spill/ppermute | solution.py:691
  16.6 10.5 %all-to-all-start = ((f32[128,8,128]{2,1,0:T(8,128)}), f32[128,8,128]{2,1,0:T(8,128)S(1)}, u32[]{:S(2)}, u32[]{:S(2)}) async-start(f32[128,8,128]{2,1,0:T(8,128)} %get-tuple-element.13), calls=%async_computation | async-start | bytes 1048576 | tf_op jit(solution)/shard_map/to_modes/all_to_all | solution.py:687
  27.2 0.0 collective-permute-done.low_hbm
  27.3 1.0 %collective-permute-done.1.high_hbm = f32[4,192,256]{2,1,0:T(8,128)S(1)} collective-permute-done((f32[4,192,256]{2,1,0:T(8,128)}, f32[4,192,256]{2,1,0:T(8,128)S(1)}, u32[]{:S(2)}, u32[]{:S(2)}) %collective-permute-start.1) | collective-permute-done | bytes 786464 | tf_op jit(solution)/shard_map/spill/ppermute | solution.py:691
  28.3 0.9 %copy-done.8 = f32[4,192,256]{2,1,0:T(8,128)} copy-done((f32[4,192,256]{2,1,0:T(8,128)}, f32[4,192,256]{2,1,0:T(8,128)S(1)}, u32[]{:S(2)}) %copy-start.8) | copy-done | bytes 786456
  29.1 0.1 maximum_add_fusion.most_hbm
  29.2 5.5 %collective-permute-start.2 = (f32[3,256,256]{2,1,0:T(8,128)S(1)}, f32[3,256,256]{2,1,0:T(8,128)}, u32[]{:S(2)}, u32[]{:S(2)}) collective-permute-start(f32[3,256,256]{2,1,0:T(8,128)S(1)} %maximum_add_fusion.most_hbm), channel_id=1, source_target_pairs={{0,16},{16,32},{32,48},{48,64},{64,80},{80,96},{96,112},{1,17},{17... | collective-permute-start | bytes 2359304 | tf_op jit(solution)/shard_map/pass/ppermute | solution.py:704
  34.8 6.5 %all-to-all-done = f32[128,8,128]{2,1,0:T(8,128)S(1)} async-done(((f32[128,8,128]{2,1,0:T(8,128)}), f32[128,8,128]{2,1,0:T(8,128)S(1)}, u32[]{:S(2)}, u32[]{:S(2)}) %all-to-all-start) | async-done | bytes 524320 | tf_op jit(solution)/shard_map/to_modes/all_to_all | solution.py:687
  41.3 0.0 copy-done.2
  41.3 0.0 copy-done.3
  41.3 0.0 copy-done.4
  41.3 1.8 %modes.1 = f32[512,128]{1,0:T(8,128)} custom-call(f32[1024,128]{1,0:T(8,128)S(1)} %bitcast.6, f32[128,128]{1,0:T(8,128)S(1)} %copy-done.1, f32[64,128]{1,0:T(8,128)S(1)} %copy-done.3, f32[8,128]{1,0:T(8,128)S(1)} %copy-done.4, bf16[2,128,128]{2,1,0:T(8,128)(2,1)S(1)} %copy-done, bf16[2,64,64]{2,1,0:T(8,128)(2,1)S(1)} %copy-done.2), custom_call_target="tpu_custom_call" | custom-call | flops 20000000000 | tf_op jit(solution)/shard_map/modes/pallas_call | solution.py:708
  43.1 0.0 copy-done.6
  43.1 5.6 %all-to-all-start.1 = ((f32[128,4,128]{2,1,0:T(4,128)}), f32[128,4,128]{2,1,0:T(4,128)S(1)}, u32[]{:S(2)}, u32[]{:S(2)}) async-start(f32[128,4,128]{2,1,0:T(4,128)} %bitcast.3), calls=%async_computation.1 | async-start | bytes 524288 | tf_op jit(solution)/shard_map/from_modes/all_to_all | solution.py:735
  48.7 0.9 %slice.27 = f32[1,128,256]{2,1,0:T(8,128)S(1)} slice(f32[4,192,256]{2,1,0:T(8,128)} %copy-done.8), slice={[3:4], [64:192], [0:256]} | slice | bytes 262144 | tf_op jit(solution)/shard_map/end/slice | solution.py:697
  49.7 0.0 copy-start.9
  49.7 5.0 %collective-permute-start.3 = (f32[1,256,256]{2,1,0:T(8,128)S(1)}, f32[1,256,256]{2,1,0:T(8,128)S(1)}, u32[]{:S(2)}, u32[]{:S(2)}) collective-permute-start(f32[1,256,256]{2,1,0:T(8,128)S(1)} %maximum_add_fusion.1.rest_hbm), channel_id=1, source_target_pairs={{0,16},{16,32},{32,48},{48,64},{64,80},{80,96},{96,112},{1,17},{17... | collective-permute-start | bytes 786440 | tf_op jit(solution)/shard_map/pass_rest/ppermute | solution.py:719
  54.7 3.3 %middle.1 = (f32[4,256,256]{2,1,0:T(8,128)}, f32[4,256,256]{2,1,0:T(8,128)}) custom-call(f32[4,256,256]{2,1,0:T(8,128)} %get-tuple-element.14.first_hbm, f32[4,192,256]{2,1,0:T(8,128)} %copy-done.7, f32[4,192,256]{2,1,0:T(8,128)} %copy-done.8, f32[3,256,256]{2,1,0:T(8,128)} %copy-done.6, f32[1,256,256]{2,1,0:T(8,128)} %copy-done.9, f32[3,4,256,256]{3,2,1,0:T(8,128)} %bitcast.8), custom_call_target="tpu_custom_call" | custom-call | flops 5000000000 | tf_op jit(solution)/shard_map/middle/pallas_call | solution.py:722
  58.0 3.3 %all-to-all-done.1 = f32[128,4,128]{2,1,0:T(4,128)S(1)} async-done(((f32[128,4,128]{2,1,0:T(4,128)}), f32[128,4,128]{2,1,0:T(4,128)S(1)}, u32[]{:S(2)}, u32[]{:S(2)}) %all-to-all-start.1) | async-done | bytes 262176 | tf_op jit(solution)/shard_map/from_modes/all_to_all | solution.py:735
  61.3 0.0 collective-permute-done.3.rest_hbm
  61.3 0.0 collective-permute-done.2.most_hbm
  61.3 0.7 %copy-done.10 = f32[128,4,128]{2,1,0:T(4,128)} copy-done((f32[128,4,128]{2,1,0:T(4,128)}, f32[128,4,128]{2,1,0:T(4,128)S(1)}, u32[]{:S(2)}) %copy-start.10) | copy-done | bytes 262168
  62.0 0.1 copy-done.11
  62.1 4.9 %nodes.1 = f32[3,4,256,256]{3,2,1,0:T(8,128)} custom-call(f32[512,128]{1,0:T(8,128)} %bitcast.10, f32[4,256,256]{2,1,0:T(8,128)} %get-tuple-element.18.first_hbm, f32[4,256,256]{2,1,0:T(8,128)} %get-tuple-element.19.second_hbm, f32[3,256,256]{2,1,0:T(8,128)} %collective-permute-done.2.most_hbm, f32[1,256,256]{2,1,0:T(8,128)} %copy-done.11, ...), custom_call_target="tpu_custom_call" | custom-call | flops 5000000000 | tf_op jit(solution)/shard_map/nodes/pallas_call | solution.py:738
  (14 shorter events, 0.1 us)
Async XLA Ops:
  9.9 19.2 %copy-start.5 = (f32[4,256,256]{2,1,0:T(8,128)S(1)}, f32[4,256,256]{2,1,0:T(8,128)}, u32[]{:S(2)}) copy-start(f32[4,256,256]{2,1,0:T(8,128)} %get-tuple-element.17) | copy-start | bytes 3145732
  9.9 31.4 %copy-start = (bf16[2,128,128]{2,1,0:T(8,128)(2,1)S(1)}, bf16[2,128,128]{2,1,0:T(8,128)(2,1)}, u32[]{:S(2)}) copy-start(bf16[2,128,128]{2,1,0:T(8,128)(2,1)} %constant.32.clone.zf) | copy-start | bytes 196612
  9.9 31.4 %copy-start.1 = (f32[128,128]{1,0:T(8,128)S(1)}, f32[128,128]{1,0:T(8,128)}, u32[]{:S(2)}) copy-start(f32[128,128]{1,0:T(8,128)} %constant.29.clone.xy) | copy-start | bytes 196612
  9.9 31.4 %copy-start.2 = (bf16[2,64,64]{2,1,0:T(8,128)(2,1)S(1)}, bf16[2,64,64]{2,1,0:T(8,128)(2,1)}, u32[]{:S(2)}) copy-start(bf16[2,64,64]{2,1,0:T(8,128)(2,1)} %constant.33.clone.zb) | copy-start | bytes 49156
  10.0 31.4 %copy-start.3 = (f32[64,128]{1,0:T(8,128)S(1)}, f32[64,128]{1,0:T(8,128)}, u32[]{:S(2)}) copy-start(f32[64,128]{1,0:T(8,128)} %constant.30.clone.lam_z) | copy-start | bytes 98308
  10.0 31.4 %copy-start.4 = (f32[8,128]{1,0:T(8,128)S(1)}, f32[8,128]{1,0:T(8,128)}, u32[]{:S(2)}) copy-start(f32[8,128]{1,0:T(8,128)} %constant.31.clone.lanes) | copy-start | bytes 12292
  10.0 17.2 %collective-permute-start = (f32[4,192,256]{2,1,0:T(8,128)}, f32[4,192,256]{2,1,0:T(8,128)S(1)}, u32[]{:S(2)}, u32[]{:S(2)}) collective-permute-start(f32[4,192,256]{2,1,0:T(8,128)} %get-tuple-element.15), channel_id=1, source_target_pairs={{0,1},{1,2},{2,3},{3,4},{4,5},{5,6},{6,7},{7,8},{8,9},{9,10},{10,1... | collective-permute-start | bytes 2359304 | tf_op jit(solution)/shard_map/spill/ppermute | solution.py:690
  14.7 13.5 %collective-permute-start.1 = (f32[4,192,256]{2,1,0:T(8,128)}, f32[4,192,256]{2,1,0:T(8,128)S(1)}, u32[]{:S(2)}, u32[]{:S(2)}) collective-permute-start(f32[4,192,256]{2,1,0:T(8,128)} %get-tuple-element.16), channel_id=1, source_target_pairs={{1,0},{2,1},{3,2},{4,3},{5,4},{6,5},{7,6},{8,7},{9,8},{10,9},{11,1... | collective-permute-start | bytes 2359304 | tf_op jit(solution)/shard_map/spill/ppermute | solution.py:691
  16.6 24.7 %all-to-all-start = ((f32[128,8,128]{2,1,0:T(8,128)}), f32[128,8,128]{2,1,0:T(8,128)S(1)}, u32[]{:S(2)}, u32[]{:S(2)}) async-start(f32[128,8,128]{2,1,0:T(8,128)} %get-tuple-element.13), calls=%async_computation | async-start | bytes 1048576 | tf_op jit(solution)/shard_map/to_modes/all_to_all | solution.py:687
  27.2 21.5 %copy-start.7 = (f32[4,192,256]{2,1,0:T(8,128)}, f32[4,192,256]{2,1,0:T(8,128)S(1)}, u32[]{:S(2)}) copy-start(f32[4,192,256]{2,1,0:T(8,128)S(1)} %collective-permute-done.low_hbm) | copy-start | bytes 2359300
  28.2 0.9 %copy-start.8 = (f32[4,192,256]{2,1,0:T(8,128)}, f32[4,192,256]{2,1,0:T(8,128)S(1)}, u32[]{:S(2)}) copy-start(f32[4,192,256]{2,1,0:T(8,128)S(1)} %collective-permute-done.1.high_hbm) | copy-start | bytes 2359300
  29.2 13.9 %copy-start.6 = (f32[3,256,256]{2,1,0:T(8,128)}, f32[3,256,256]{2,1,0:T(8,128)S(1)}, u32[]{:S(2)}) copy-start(f32[3,256,256]{2,1,0:T(8,128)S(1)} %maximum_add_fusion.most_hbm) | copy-start | bytes 2359300
  29.2 32.1 %collective-permute-start.2 = (f32[3,256,256]{2,1,0:T(8,128)S(1)}, f32[3,256,256]{2,1,0:T(8,128)}, u32[]{:S(2)}, u32[]{:S(2)}) collective-permute-start(f32[3,256,256]{2,1,0:T(8,128)S(1)} %maximum_add_fusion.most_hbm), channel_id=1, source_target_pairs={{0,16},{16,32},{32,48},{48,64},{64,80},{80,96},{96,112},{1,17},{17... | collective-permute-start | bytes 2359304 | tf_op jit(solution)/shard_map/pass/ppermute | solution.py:704
  43.1 18.2 %all-to-all-start.1 = ((f32[128,4,128]{2,1,0:T(4,128)}), f32[128,4,128]{2,1,0:T(4,128)S(1)}, u32[]{:S(2)}, u32[]{:S(2)}) async-start(f32[128,4,128]{2,1,0:T(4,128)} %bitcast.3), calls=%async_computation.1 | async-start | bytes 524288 | tf_op jit(solution)/shard_map/from_modes/all_to_all | solution.py:735
  49.7 5.0 %copy-start.9 = (f32[1,256,256]{2,1,0:T(8,128)}, f32[1,256,256]{2,1,0:T(8,128)S(1)}, u32[]{:S(2)}) copy-start(f32[1,256,256]{2,1,0:T(8,128)S(1)} %maximum_add_fusion.1.rest_hbm) | copy-start | bytes 786436
  49.7 11.6 %collective-permute-start.3 = (f32[1,256,256]{2,1,0:T(8,128)S(1)}, f32[1,256,256]{2,1,0:T(8,128)S(1)}, u32[]{:S(2)}, u32[]{:S(2)}) collective-permute-start(f32[1,256,256]{2,1,0:T(8,128)S(1)} %maximum_add_fusion.1.rest_hbm), channel_id=1, source_target_pairs={{0,16},{16,32},{32,48},{48,64},{64,80},{80,96},{96,112},{1,17},{17... | collective-permute-start | bytes 786440 | tf_op jit(solution)/shard_map/pass_rest/ppermute | solution.py:719
  61.3 0.7 %copy-start.10 = (f32[128,4,128]{2,1,0:T(4,128)}, f32[128,4,128]{2,1,0:T(4,128)S(1)}, u32[]{:S(2)}) copy-start(f32[128,4,128]{2,1,0:T(4,128)S(1)} %all-to-all-done.1) | copy-start | bytes 786436
  61.3 0.8 %copy-start.11 = (f32[1,256,256]{2,1,0:T(8,128)}, f32[1,256,256]{2,1,0:T(8,128)S(1)}, u32[]{:S(2)}) copy-start(f32[1,256,256]{2,1,0:T(8,128)S(1)} %collective-permute-done.3.rest_hbm) | copy-start | bytes 786436

commit v4 on v3

--- a/solution.py
+++ b/solution.py
@@ -222,7 +222,7 @@
 
 
 def fine_kernel(u_hbm, q_hbm, along_hbm, f11_hbm, x0_hbm, x1_hbm, lam_hbm,
-                first_hbm, second_hbm, up_hbm, down_hbm, send_hbm,
+                first_hbm, second_hbm, near_hbm, across_hbm, send_hbm,
                 u, q, along, f11, x0, x1, lam,
                 a_s, fe, be, se, cs, rows_s, pair_s, y_s, w_s, g_s, send_s, in_sem, u_sem, out_sem, send_sem):
     mu, keep_low, keep_high = position()
@@ -239,6 +239,8 @@
 
     edge = 2 * PLANE
     middle = pl.ds(edge, OWN)
+    odd = lax.axis_index("space") % 2
+    sides = ((near_hbm, 1 - odd), (across_hbm, odd))
     stores = []
 
     def store(source, target, sem):
@@ -290,8 +292,9 @@
                 be[f, here] = 0.5 * value
             fe[f, here] = value
         store(fe.at[f, middle], first_hbm.at[f], out_sem.at[f, 0])
-        store(fe.at[f, pl.ds(0, edge)], down_hbm.at[f, pl.ds(0, edge)], out_sem.at[f, 1])
-        store(fe.at[f, pl.ds(edge + OWN, edge)], up_hbm.at[f, pl.ds(0, edge)], out_sem.at[f, 2])
+        for i, (target, up) in enumerate(sides):
+            rows = pl.ds(pl.multiple_of(up * (edge + OWN), edge), edge)
+            store(fe.at[f, rows], target.at[f, pl.ds(0, edge)], out_sem.at[f, 1 + i])
 
     def second_stage(f):
         nu, couple, partner = field(f)
@@ -321,8 +324,9 @@
             se[f, here] = value
             cs[f, here] = c
         store(se.at[f, pl.ds(2 * edge, OWN)], second_hbm.at[f], out_sem.at[f, 3])
-        store(se.at[f, pl.ds(0, 2 * edge)], down_hbm.at[f, pl.ds(edge, 2 * edge)], out_sem.at[f, 4])
-        store(se.at[f, pl.ds(2 * edge + OWN, 2 * edge)], up_hbm.at[f, pl.ds(edge, 2 * edge)], out_sem.at[f, 5])
+        for i, (target, up) in enumerate(sides):
+            rows = pl.ds(pl.multiple_of(up * (2 * edge + OWN), edge), 2 * edge)
+            store(se.at[f, rows], target.at[f, pl.ds(edge, 2 * edge)], out_sem.at[f, 4 + i])
 
     def put(ref, f, k, value):
         for i in range(2):
@@ -474,17 +478,20 @@
             for f in pair:
                 stage(f)
 
-    def pack(p, _):
+    def pack(p):
         values = []
         for half in range(2):
             for f in range(4):
                 values.append(g_s[f, pl.ds(half * 8 * CY + p, 8, stride=CY), :])
         for t, value in enumerate(chunk_transpose(values)):
-            send_s[t * BLOCKS + p] = value
-        return 0
-
-    lax.fori_loop(0, BLOCKS, pack, 0, unroll=8)
-    store(send_s, send_hbm, send_sem)
+            send_s[t, p] = value
+
+    step = BLOCKS // 4
+    for i in range(4):
+        for p in range(i * step, (i + 1) * step):
+            pack(p)
+        part = pl.ds(i * step, step)
+        store(send_s.at[:, part], send_hbm.at[:, part], send_sem.at[i])
     for copy in stores:
         copy.wait()
 
@@ -528,16 +535,18 @@
     return paired(paired(weight * x, 0), 1)
 
 
-def middle_kernel(first_hbm, low_hbm, high_hbm, most_hbm, rest_hbm, u_hbm, first_out, second_out,
-                  first, low, high, second, u, out, in_sem, out_sem):
+def middle_kernel(first_hbm, near_hbm, across_hbm, most_hbm, rest_hbm, u_hbm, first_out, second_out,
+                  first, spill, second, u, out, in_sem, out_sem):
     mu, _, _ = position()
-    near = pl.ds(0, 2 * PLANE)
+    odd = lax.axis_index("space") % 2
+    part = pl.ds(0, 2 * PLANE)
     loads = []
     for f in range(4):
         source = most_hbm.at[f] if f < SENT_FIRST else rest_hbm.at[f - SENT_FIRST]
-        moves = ((first_hbm.at[f], first), (low_hbm.at[f, near], low), (high_hbm.at[f, near], high), (source, second), (u_hbm.at[0, f], u))
+        moves = ((first_hbm.at[f], first.at[f]), (near_hbm.at[f, part], spill.at[0, f]), (across_hbm.at[f, part], spill.at[1, f]),
+                 (source, second.at[f]), (u_hbm.at[0, f], u.at[f]))
         for i, (source, target) in enumerate(moves):
-            load = pltpu.make_async_copy(source, target.at[f], in_sem.at[f, i])
+            load = pltpu.make_async_copy(source, target, in_sem.at[f, i])
             load.start()
             loads.append(load)
     stores = []
@@ -554,9 +563,9 @@
                 p = 2 * k + i
                 value = first[f, rows] - middle
                 if p < 2:
-                    value = value + low[f, pl.ds(p * PLANE, PLANE)]
+                    value = value + spill[1 - odd, f, pl.ds(p * PLANE, PLANE)]
                 if p >= FINE - 2:
-                    value = value + high[f, pl.ds((p - FINE + 2) * PLANE, PLANE)]
+                    value = value + spill[odd, f, pl.ds((p - FINE + 2) * PLANE, PLANE)]
                 out[0, f, rows] = value
                 out[1, f, rows] = seconds[i] - mean
         for n, target in enumerate((first_out, second_out)):
@@ -571,7 +580,7 @@
     return jnp.concatenate([x[(p // 2) * PLANE:(p // 2 + 1) * PLANE] for p in range(FINE)], axis=0)
 
 
-def nodes_kernel(modes, first_hbm, second_hbm, most_hbm, rest_hbm, yb_hbm, xb_hbm, u_hbm, out, h_s, first, second, before, yb, xb, out_s, in_sem, sem):
+def nodes_kernel(modes, first_hbm, second_hbm, most_hbm, rest_hbm, yb_hbm, xb_hbm, u_hbm, out, h_s, first, second, before, yb, xb, p_s, out_s, in_sem, sem):
     mu, _, _ = position()
     leading = lax.axis_index("tm") == 0
     tables = [pltpu.make_async_copy(yb_hbm, yb, in_sem.at[0, 3]), pltpu.make_async_copy(xb_hbm, xb, in_sem.at[1, 3])]
@@ -596,10 +605,12 @@
             h_s[g, pl.ds(r * 8, 8)] = value
     for load in tables:
         load.wait()
+    for g in range(8):
+        p_s[g] = right(left(yb, h_s[g]), xb)
     stores = []
     for f in range(4):
-        start = right(left(yb, h_s[f]), xb)
-        end = right(left(yb, h_s[4 + f]), xb)
+        start = p_s[f]
+        end = p_s[4 + f]
         for i, (source, target) in enumerate(((first_hbm, first), (second_hbm, second), (second_hbm, before))):
             pltpu.make_async_copy(source.at[f], target.at[f], in_sem.at[f, i]).wait()
         for k in range(COARSE):
@@ -625,7 +636,7 @@
 GRANT = 60
 SENT_FIRST = 3
 MODE_COST = 20
-MIDDLE_COST = 5
+MIDDLE_COST = 3
 
 
 def params(mib):
@@ -655,15 +666,13 @@
     spill = (4, 6 * PLANE, NX)
     near = (4, 2 * PLANE, NX)
     tables = (ALONG, F11, X0, X1, LAM_XY)
-    up_pairs = [(i, i + 1) for i in range(BLOCKS - 1)]
-    down_pairs = [(i + 1, i) for i in range(BLOCKS - 1)]
     dma = pltpu.SemaphoreType.DMA
 
     with jax.named_scope("fine"):
-        first_c, second_c, up, down, packet = pl.pallas_call(
+        first_c, second_c, to_near, to_across, packet = pl.pallas_call(
             fine_kernel,
             out_shape=[shape(*field), shape(*field), shape(*spill), shape(*spill),
-                       shape(SLABS * BLOCKS, 8, 128)],
+                       shape(SLABS, BLOCKS, 8, 128)],
             in_specs=[ANY] * (2 + len(tables)),
             out_specs=[ANY] * 5,
             scratch_shapes=[scratch(3, 4, OWN, NX), scratch(OWN, NX)] + [like(table) for table in tables] + [
@@ -677,24 +686,28 @@
                 scratch(4, 4 * CY, CX),
                 scratch(4, 18 * CY, CX),
                 scratch(4, 16 * CY, CX),
-                scratch(SLABS * BLOCKS, 8, 128),
-                dma((6,)), dma((3, 4)), dma((4, 6)), dma,
+                scratch(SLABS, BLOCKS, 8, 128),
+                dma((6,)), dma((3, 4)), dma((4, 6)), dma((4,)),
             ],
             compiler_params=params(GRANT),
         )(u, heat, *tables)
 
     with jax.named_scope("to_modes"):
-        modes = lax.all_to_all(packet, AXES, 0, 0, tiled=True)
+        modes = lax.all_to_all(packet.reshape(SLABS * BLOCKS, 8, 128), AXES, 0, 0, tiled=True)
 
     with jax.named_scope("spill"):
-        low = lax.ppermute(up, "space", up_pairs)
-        high = lax.ppermute(down, "space", down_pairs)
+        chip = [(i, i ^ 1) for i in range(BLOCKS)]
+        chips = [(i, i + 1) for i in range(1, BLOCKS - 1, 2)]
+        from_near = lax.ppermute(to_near, "space", chip)
+        from_across = lax.ppermute(to_across, "space", chips + [(j, i) for i, j in chips])
 
     with jax.named_scope("end"):
+        odd = lax.axis_index("space") % 2 == 1
         far = slice(2 * PLANE, 6 * PLANE)
 
         def ended(fields):
-            return second_c[fields] + jnp.concatenate([low[fields, far], high[fields, far]], axis=1)
+            near, across = from_near[fields, far], from_across[fields, far]
+            return second_c[fields] + jnp.concatenate([jnp.where(odd, near, across), jnp.where(odd, across, near)], axis=1)
 
         most = ended(slice(0, SENT_FIRST))
         rest = ended(slice(SENT_FIRST, 4))
@@ -724,11 +737,11 @@
             out_shape=[shape(*field)] * 2,
             in_specs=[ANY] * 6,
             out_specs=[ANY] * 2,
-            scratch_shapes=[scratch(*field), scratch(*near), scratch(*near), scratch(*field), scratch(*field), scratch(2, *field),
+            scratch_shapes=[scratch(*field), scratch(2, *near), scratch(*field), scratch(*field), scratch(2, *field),
                             dma((4, 5)), dma((2, 4))],
             cost_estimate=cost(MIDDLE_COST),
             compiler_params=params(GRANT),
-        )(first_c, low, high, most, rest, u)
+        )(first_c, from_near, from_across, most, rest, u)
 
     with jax.named_scope("from_modes"):
         solved = solved.reshape(SLABS * BLOCKS, COARSE, 128)
@@ -740,7 +753,7 @@
             out_shape=shape(3, *field),
             in_specs=[VM] + [ANY] * 7,
             out_specs=ANY,
-            scratch_shapes=[scratch(8, 64, 128)] + [scratch(*field)] * 3 + [like(YB), like(XB), scratch(3, *field), dma((4, 4)), dma((3, 4))],
+            scratch_shapes=[scratch(8, 64, 128)] + [scratch(*field)] * 3 + [like(YB), like(XB), scratch(8, OWN // 2, NX), scratch(3, *field), dma((4, 4)), dma((3, 4))],
             cost_estimate=cost(5),
             compiler_params=params(GRANT),
         )(back, first, second, most_before, rest_before, YB, XB, u)

time: 67.7 us -> 65.6 us (0.969)
  starting transfers between devices: 33.3 us -> 31.1 us
  local copies, waits for them, and re-layouts: 2.68 us -> 1.65 us
  other arithmetic: 0.14 us -> 1.13 us
    ppermute x2, starting transfers between devices: 6.64 us -> 4.81 us  [the longest x1 3.32 us: per_device(): lax.ppermute(to_across, 'space', chips + [(j, i) for i, j in chips])]
    select_n x0 -> x2, other arithmetic: none -> 0.99 us  [ended(): jnp.where(odd, near, across)]
    slice x4 -> x0, local copies, waits for them, and re-layouts: 0.98 us -> none  [the longest x2 0.94 us: ended(): high[fields, far]]
    all_to_all x1, starting transfers between devices: 10.5 us -> 9.82 us  [per_device(): lax.all_to_all(packet.reshape(SLABS * BLOCKS, 8, 128), AXES, 0, 0, tiled=...]
where the time goes in v4:
time: 65.6 us; the launch traced here: 65.3 us
  starting transfers between devices  31.1 us (47%)
  Pallas kernels  19.8 us (30%)
  waiting for transfers between devices  11.3 us (17%)
  local copies, waits for them, and re-layouts  1.65 us (3%)
  other arithmetic  1.13 us (2%)
    all_to_all x1, starting transfers between devices, per_device(): lax.all_to_all(packet.reshape(SLABS * BLOCKS, 8, 128), AXES, 0, 0, tiled=...  9.82 us
    pallas_call x1, Pallas kernels, per_device(): pl.pallas_call(fine_kernel, out_shape=[shape(*field), shape(*field), shap...  9.57 us
    all_to_all x1, waiting for transfers between devices, per_device(): lax.all_to_all(packet.reshape(SLABS * BLOCKS, 8, 128), AXES, 0, 0, tiled=...  7.12 us
    all_to_all x1, starting transfers between devices, per_device(): lax.all_to_all(solved, AXES, 0, 0, tiled=True).reshape(SLABS * CZ, 128)  5.81 us
    ppermute x1, starting transfers between devices, per_device(): most_before = lax.ppermute(most, 'tm', later)  5.63 us
    pallas_call x1, Pallas kernels, per_device(): pl.pallas_call(nodes_kernel, out_shape=shape(3, *field), in_specs=[VM] +...  5.16 us
    ppermute x1, starting transfers between devices, per_device(): rest_before = lax.ppermute(rest_sent, 'tm', later)  4.99 us
    all_to_all x1, waiting for transfers between devices, per_device(): lax.all_to_all(solved, AXES, 0, 0, tiled=True).reshape(SLABS * CZ, 128)  3.89 us
  transfers between devices with their start and end apart: 6, of which 3 were waited for; matrix products, arithmetic and copies ran while one was open for 2% of the time, Pallas kernels for 8%

profile of v4, /device:TPU:1, one launch (start us, length us, event | category | flops | bytes accessed | tf_op | source)
XLA Modules:
  0.0 65.3 jit_solution(8334350049366204141)
XLA Ops:
  0.0 9.6 %fine.1 = (f32[4,256,256]{2,1,0:T(8,128)}, f32[4,256,256]{2,1,0:T(8,128)}, f32[4,192,256]{2,1,0:T(8,128)}, f32[4,192,256]{2,1,0:T(8,128)}, f32[8,16,8,128]{3,2,1,0:T(8,128)}) custom-call(f32[3,4,256,256]{3,2,1,0:T(8,128)} %bitcast.8, f32[256,256]{1,0:T(8,128)} %bitcast.13, bf16[256,256]{1,0:T(8,128)(2,1)} %constant.42.clone.along_hbm, ...), custom_call_target="tpu_custom_call" | custom-call | tf_op jit(solution)/shard_map/fine/pallas_call | solution.py:672
  9.6 0.0 copy-start.5
  9.6 0.0 copy-start
  9.6 0.0 copy-start.1
  9.6 0.0 copy-start.2
  9.6 0.0 copy-start.3
  9.6 0.0 copy-start.4
  9.7 1.5 %collective-permute-start = (f32[4,192,256]{2,1,0:T(8,128)}, f32[4,192,256]{2,1,0:T(8,128)S(1)}, u32[]{:S(2)}, u32[]{:S(2)}) collective-permute-start(f32[4,192,256]{2,1,0:T(8,128)} %get-tuple-element.15), channel_id=1, source_target_pairs={{0,1},{1,0},{2,3},{3,2},{4,5},{5,4},{6,7},{7,6},{8,9},{9,8},{10,11... | collective-permute-start | bytes 2359304 | tf_op jit(solution)/shard_map/spill/ppermute | solution.py:701
  11.1 3.3 %collective-permute-start.1 = (f32[4,192,256]{2,1,0:T(8,128)}, f32[4,192,256]{2,1,0:T(8,128)S(1)}, u32[]{:S(2)}, u32[]{:S(2)}) collective-permute-start(f32[4,192,256]{2,1,0:T(8,128)} %get-tuple-element.16), channel_id=1, source_target_pairs={{1,2},{3,4},{5,6},{7,8},{9,10},{11,12},{13,14},{2,1},{4,3},{6,5},{... | collective-permute-start | bytes 2359304 | tf_op jit(solution)/shard_map/spill/ppermute | solution.py:702
  14.5 9.8 %all-to-all-start = ((f32[128,8,128]{2,1,0:T(8,128)}), f32[128,8,128]{2,1,0:T(8,128)S(1)}, u32[]{:S(2)}, u32[]{:S(2)}) async-start(f32[128,8,128]{2,1,0:T(8,128)} %bitcast.11), calls=%async_computation | async-start | bytes 1048576 | tf_op jit(solution)/shard_map/to_modes/all_to_all | solution.py:696
  24.3 0.0 collective-permute-done.near_hbm
  24.3 0.0 copy-start.7
  24.3 0.3 collective-permute-done.1.across_hbm
  24.7 0.1 slice_select_fusion.1
  24.7 0.8 %copy-done.8 = f32[4,192,256]{2,1,0:T(8,128)} copy-done((f32[4,192,256]{2,1,0:T(8,128)}, f32[4,192,256]{2,1,0:T(8,128)S(1)}, u32[]{:S(2)}) %copy-start.8) | copy-done | bytes 786456
  25.5 0.0 copy-done.5
  25.6 0.1 maximum_add_fusion.most_hbm
  25.7 0.0 copy-start.6
  25.7 5.6 %collective-permute-start.2 = (f32[3,256,256]{2,1,0:T(8,128)S(1)}, f32[3,256,256]{2,1,0:T(8,128)}, u32[]{:S(2)}, u32[]{:S(2)}) collective-permute-start(f32[3,256,256]{2,1,0:T(8,128)S(1)} %maximum_add_fusion.most_hbm), channel_id=1, source_target_pairs={{0,16},{16,32},{32,48},{48,64},{64,80},{80,96},{96,112},{1,17},{17... | collective-permute-start | bytes 2359304 | tf_op jit(solution)/shard_map/pass/ppermute | solution.py:717
  31.3 7.1 %all-to-all-done = f32[128,8,128]{2,1,0:T(8,128)S(1)} async-done(((f32[128,8,128]{2,1,0:T(8,128)}), f32[128,8,128]{2,1,0:T(8,128)S(1)}, u32[]{:S(2)}, u32[]{:S(2)}) %all-to-all-start) | async-done | bytes 524320 | tf_op jit(solution)/shard_map/to_modes/all_to_all | solution.py:696
  38.4 0.0 copy-done.1
  38.4 1.8 %modes.1 = f32[512,128]{1,0:T(8,128)} custom-call(f32[1024,128]{1,0:T(8,128)S(1)} %bitcast.7, f32[128,128]{1,0:T(8,128)S(1)} %copy-done.1, f32[64,128]{1,0:T(8,128)S(1)} %copy-done.3, f32[8,128]{1,0:T(8,128)S(1)} %copy-done.4, bf16[2,128,128]{2,1,0:T(8,128)(2,1)S(1)} %copy-done, bf16[2,64,64]{2,1,0:T(8,128)(2,1)S(1)} %copy-done.2), custom_call_target="tpu_custom_call" | custom-call | flops 20000000000 | tf_op jit(solution)/shard_map/modes/pallas_call | solution.py:721
  40.2 5.8 %all-to-all-start.1 = ((f32[128,4,128]{2,1,0:T(4,128)}), f32[128,4,128]{2,1,0:T(4,128)S(1)}, u32[]{:S(2)}, u32[]{:S(2)}) async-start(f32[128,4,128]{2,1,0:T(4,128)} %bitcast.4), calls=%async_computation.1 | async-start | bytes 524288 | tf_op jit(solution)/shard_map/from_modes/all_to_all | solution.py:748
  46.1 0.9 %slice_select_fusion.3 = (f32[1,128,256]{2,1,0:T(8,128)S(1)}, f32[1,128,256]{2,1,0:T(8,128)S(1)}) fusion(f32[4,192,256]{2,1,0:T(8,128)} %copy-done.8, f32[4,192,256]{2,1,0:T(8,128)S(1)} %collective-permute-done.near_hbm, pred[]{:T(512)S(6)} %eq.5), kind=kLoop, calls=%fused_computation.5 | loop fusion | flops 65536 | bytes 524289 | tf_op jit(solution)/shard_map/end/jit(_where)/select_n | solution.py:710
  47.0 5.0 %collective-permute-start.3 = (f32[1,256,256]{2,1,0:T(8,128)S(1)}, f32[1,256,256]{2,1,0:T(8,128)S(1)}, u32[]{:S(2)}, u32[]{:S(2)}) collective-permute-start(f32[1,256,256]{2,1,0:T(8,128)S(1)} %maximum_add_fusion.1.rest_hbm), channel_id=1, source_target_pairs={{0,16},{16,32},{32,48},{48,64},{64,80},{80,96},{96,112},{1,17},{17... | collective-permute-start | bytes 786440 | tf_op jit(solution)/shard_map/pass_rest/ppermute | solution.py:732
  52.0 3.3 %middle.1 = (f32[4,256,256]{2,1,0:T(8,128)}, f32[4,256,256]{2,1,0:T(8,128)}) custom-call(f32[4,256,256]{2,1,0:T(8,128)} %get-tuple-element.14.first_hbm, f32[4,192,256]{2,1,0:T(8,128)} %copy-done.7, f32[4,192,256]{2,1,0:T(8,128)} %copy-done.8, f32[3,256,256]{2,1,0:T(8,128)} %copy-done.6, f32[1,256,256]{2,1,0:T(8,128)} %copy-done.9, f32[3,4,256,256]{3,2,1,0:T(8,128)} %bitcast.9), custom_call_target="tpu_custom_call" | custom-call | flops 3000000000 | tf_op jit(solution)/shard_map/middle/pallas_call | solution.py:735
  55.3 3.9 %all-to-all-done.1 = f32[128,4,128]{2,1,0:T(4,128)S(1)} async-done(((f32[128,4,128]{2,1,0:T(4,128)}), f32[128,4,128]{2,1,0:T(4,128)S(1)}, u32[]{:S(2)}, u32[]{:S(2)}) %all-to-all-start.1) | async-done | bytes 262176 | tf_op jit(solution)/shard_map/from_modes/all_to_all | solution.py:748
  59.2 0.0 collective-permute-done.3.rest_hbm
  59.2 0.0 collective-permute-done.2.most_hbm
  59.2 0.7 %copy-done.10 = f32[128,4,128]{2,1,0:T(4,128)} copy-done((f32[128,4,128]{2,1,0:T(4,128)}, f32[128,4,128]{2,1,0:T(4,128)S(1)}, u32[]{:S(2)}) %copy-start.10) | copy-done | bytes 262168
  59.9 0.1 copy-done.11
  60.0 5.2 %nodes.1 = f32[3,4,256,256]{3,2,1,0:T(8,128)} custom-call(f32[512,128]{1,0:T(8,128)} %bitcast.12, f32[4,256,256]{2,1,0:T(8,128)} %get-tuple-element.18.first_hbm, f32[4,256,256]{2,1,0:T(8,128)} %get-tuple-element.19.second_hbm, f32[3,256,256]{2,1,0:T(8,128)} %collective-permute-done.2.most_hbm, f32[1,256,256]{2,1,0:T(8,128)} %copy-done.11, ...), custom_call_target="tpu_custom_call" | custom-call | flops 5000000000 | tf_op jit(solution)/shard_map/nodes/pallas_call | solution.py:751
  (12 shorter events, 0.1 us)
Async XLA Ops:
  9.6 16.0 %copy-start.5 = (f32[4,256,256]{2,1,0:T(8,128)S(1)}, f32[4,256,256]{2,1,0:T(8,128)}, u32[]{:S(2)}) copy-start(f32[4,256,256]{2,1,0:T(8,128)} %get-tuple-element.17) | copy-start | bytes 3145732
  9.6 28.8 %copy-start = (bf16[2,128,128]{2,1,0:T(8,128)(2,1)S(1)}, bf16[2,128,128]{2,1,0:T(8,128)(2,1)}, u32[]{:S(2)}) copy-start(bf16[2,128,128]{2,1,0:T(8,128)(2,1)} %constant.50.clone.zf) | copy-start | bytes 196612
  9.6 28.8 %copy-start.1 = (f32[128,128]{1,0:T(8,128)S(1)}, f32[128,128]{1,0:T(8,128)}, u32[]{:S(2)}) copy-start(f32[128,128]{1,0:T(8,128)} %constant.47.clone.xy) | copy-start | bytes 196612
  9.6 28.8 %copy-start.2 = (bf16[2,64,64]{2,1,0:T(8,128)(2,1)S(1)}, bf16[2,64,64]{2,1,0:T(8,128)(2,1)}, u32[]{:S(2)}) copy-start(bf16[2,64,64]{2,1,0:T(8,128)(2,1)} %constant.51.clone.zb) | copy-start | bytes 49156
  9.6 28.8 %copy-start.3 = (f32[64,128]{1,0:T(8,128)S(1)}, f32[64,128]{1,0:T(8,128)}, u32[]{:S(2)}) copy-start(f32[64,128]{1,0:T(8,128)} %constant.48.clone.lam_z) | copy-start | bytes 98308
  9.6 28.8 %copy-start.4 = (f32[8,128]{1,0:T(8,128)S(1)}, f32[8,128]{1,0:T(8,128)}, u32[]{:S(2)}) copy-start(f32[8,128]{1,0:T(8,128)} %constant.49.clone.lanes) | copy-start | bytes 12292
  9.7 14.7 %collective-permute-start = (f32[4,192,256]{2,1,0:T(8,128)}, f32[4,192,256]{2,1,0:T(8,128)S(1)}, u32[]{:S(2)}, u32[]{:S(2)}) collective-permute-start(f32[4,192,256]{2,1,0:T(8,128)} %get-tuple-element.15), channel_id=1, source_target_pairs={{0,1},{1,0},{2,3},{3,2},{4,5},{5,4},{6,7},{7,6},{8,9},{9,8},{10,11... | collective-permute-start | bytes 2359304 | tf_op jit(solution)/shard_map/spill/ppermute | solution.py:701
  11.1 13.5 %collective-permute-start.1 = (f32[4,192,256]{2,1,0:T(8,128)}, f32[4,192,256]{2,1,0:T(8,128)S(1)}, u32[]{:S(2)}, u32[]{:S(2)}) collective-permute-start(f32[4,192,256]{2,1,0:T(8,128)} %get-tuple-element.16), channel_id=1, source_target_pairs={{1,2},{3,4},{5,6},{7,8},{9,10},{11,12},{13,14},{2,1},{4,3},{6,5},{... | collective-permute-start | bytes 2359304 | tf_op jit(solution)/shard_map/spill/ppermute | solution.py:702
  14.5 23.9 %all-to-all-start = ((f32[128,8,128]{2,1,0:T(8,128)}), f32[128,8,128]{2,1,0:T(8,128)S(1)}, u32[]{:S(2)}, u32[]{:S(2)}) async-start(f32[128,8,128]{2,1,0:T(8,128)} %bitcast.11), calls=%async_computation | async-start | bytes 1048576 | tf_op jit(solution)/shard_map/to_modes/all_to_all | solution.py:696
  24.3 21.7 %copy-start.7 = (f32[4,192,256]{2,1,0:T(8,128)}, f32[4,192,256]{2,1,0:T(8,128)S(1)}, u32[]{:S(2)}) copy-start(f32[4,192,256]{2,1,0:T(8,128)S(1)} %collective-permute-done.near_hbm) | copy-start | bytes 2359300
  24.7 0.9 %copy-start.8 = (f32[4,192,256]{2,1,0:T(8,128)}, f32[4,192,256]{2,1,0:T(8,128)S(1)}, u32[]{:S(2)}) copy-start(f32[4,192,256]{2,1,0:T(8,128)S(1)} %collective-permute-done.1.across_hbm) | copy-start | bytes 2359300
  25.7 14.6 %copy-start.6 = (f32[3,256,256]{2,1,0:T(8,128)}, f32[3,256,256]{2,1,0:T(8,128)S(1)}, u32[]{:S(2)}) copy-start(f32[3,256,256]{2,1,0:T(8,128)S(1)} %maximum_add_fusion.most_hbm) | copy-start | bytes 2359300
  25.7 33.6 %collective-permute-start.2 = (f32[3,256,256]{2,1,0:T(8,128)S(1)}, f32[3,256,256]{2,1,0:T(8,128)}, u32[]{:S(2)}, u32[]{:S(2)}) collective-permute-start(f32[3,256,256]{2,1,0:T(8,128)S(1)} %maximum_add_fusion.most_hbm), channel_id=1, source_target_pairs={{0,16},{16,32},{32,48},{48,64},{64,80},{80,96},{96,112},{1,17},{17... | collective-permute-start | bytes 2359304 | tf_op jit(solution)/shard_map/pass/ppermute | solution.py:717
  40.2 19.0 %all-to-all-start.1 = ((f32[128,4,128]{2,1,0:T(4,128)}), f32[128,4,128]{2,1,0:T(4,128)S(1)}, u32[]{:S(2)}, u32[]{:S(2)}) async-start(f32[128,4,128]{2,1,0:T(4,128)} %bitcast.4), calls=%async_computation.1 | async-start | bytes 524288 | tf_op jit(solution)/shard_map/from_modes/all_to_all | solution.py:748
  47.0 5.0 %copy-start.9 = (f32[1,256,256]{2,1,0:T(8,128)}, f32[1,256,256]{2,1,0:T(8,128)S(1)}, u32[]{:S(2)}) copy-start(f32[1,256,256]{2,1,0:T(8,128)S(1)} %maximum_add_fusion.1.rest_hbm) | copy-start | bytes 786436
  47.0 12.2 %collective-permute-start.3 = (f32[1,256,256]{2,1,0:T(8,128)S(1)}, f32[1,256,256]{2,1,0:T(8,128)S(1)}, u32[]{:S(2)}, u32[]{:S(2)}) collective-permute-start(f32[1,256,256]{2,1,0:T(8,128)S(1)} %maximum_add_fusion.1.rest_hbm), channel_id=1, source_target_pairs={{0,16},{16,32},{32,48},{48,64},{64,80},{80,96},{96,112},{1,17},{17... | collective-permute-start | bytes 786440 | tf_op jit(solution)/shard_map/pass_rest/ppermute | solution.py:732
  59.2 0.7 %copy-start.10 = (f32[128,4,128]{2,1,0:T(4,128)}, f32[128,4,128]{2,1,0:T(4,128)S(1)}, u32[]{:S(2)}) copy-start(f32[128,4,128]{2,1,0:T(4,128)S(1)} %all-to-all-done.1) | copy-start | bytes 786436
  59.2 0.8 %copy-start.11 = (f32[1,256,256]{2,1,0:T(8,128)}, f32[1,256,256]{2,1,0:T(8,128)S(1)}, u32[]{:S(2)}) copy-start(f32[1,256,256]{2,1,0:T(8,128)S(1)} %collective-permute-done.3.rest_hbm) | copy-start | bytes 786436

commit v5 on v4

--- a/solution.py
+++ b/solution.py
@@ -580,11 +580,12 @@
     return jnp.concatenate([x[(p // 2) * PLANE:(p // 2 + 1) * PLANE] for p in range(FINE)], axis=0)
 
 
-def nodes_kernel(modes, first_hbm, second_hbm, most_hbm, rest_hbm, yb_hbm, xb_hbm, u_hbm, out, h_s, first, second, before, yb, xb, p_s, out_s, in_sem, sem):
+def nodes_kernel(modes_hbm, first_hbm, second_hbm, most_hbm, rest_hbm, yb_hbm, xb_hbm, u_hbm, out, modes, h_s, first, second, before, yb, xb, p_s, out_s, in_sem, sem):
     mu, _, _ = position()
     leading = lax.axis_index("tm") == 0
+    arrived = pltpu.make_async_copy(modes_hbm, modes, in_sem.at[2, 3])
     tables = [pltpu.make_async_copy(yb_hbm, yb, in_sem.at[0, 3]), pltpu.make_async_copy(xb_hbm, xb, in_sem.at[1, 3])]
-    for load in tables:
+    for load in [arrived] + tables:
         load.start()
     for f in range(4):
         for i, (source, target) in enumerate(((first_hbm, first), (second_hbm, second))):
@@ -599,6 +600,7 @@
             source = most_hbm.at[f] if f < SENT_FIRST else rest_hbm.at[f - SENT_FIRST]
             pltpu.make_async_copy(source, before.at[f], in_sem.at[f, 2]).start()
 
+    arrived.wait()
     for r in range(8):
         values = [modes[pl.ds(t * 64 + r * 8, 8)] for t in range(SLABS)]
         for g, value in enumerate(chunk_transpose(values)):
@@ -751,9 +753,9 @@
         out = pl.pallas_call(
             nodes_kernel,
             out_shape=shape(3, *field),
-            in_specs=[VM] + [ANY] * 7,
+            in_specs=[ANY] * 8,
             out_specs=ANY,
-            scratch_shapes=[scratch(8, 64, 128)] + [scratch(*field)] * 3 + [like(YB), like(XB), scratch(8, OWN // 2, NX), scratch(3, *field), dma((4, 4)), dma((3, 4))],
+            scratch_shapes=[scratch(SLABS * CZ, 128), scratch(8, 64, 128)] + [scratch(*field)] * 3 + [like(YB), like(XB), scratch(8, OWN // 2, NX), scratch(3, *field), dma((4, 4)), dma((3, 4))],
             cost_estimate=cost(5),
             compiler_params=params(GRANT),
         )(back, first, second, most_before, rest_before, YB, XB, u)

time: 65.6 us -> 65 us (level)
  no operation moved by 1% of the time
where the time goes in v5:
time: 65 us; the launch traced here: 64.7 us
  starting transfers between devices  31.1 us (48%)
  Pallas kernels  19.2 us (30%)
  waiting for transfers between devices  11.3 us (17%)
  local copies, waits for them, and re-layouts  1.65 us (3%)
  other arithmetic  1.13 us (2%)
    all_to_all x1, starting transfers between devices, per_device(): lax.all_to_all(packet.reshape(SLABS * BLOCKS, 8, 128), AXES, 0, 0, tiled=...  9.82 us
    pallas_call x1, Pallas kernels, per_device(): pl.pallas_call(fine_kernel, out_shape=[shape(*field), shape(*field), shap...  9.57 us
    all_to_all x1, waiting for transfers between devices, per_device(): lax.all_to_all(packet.reshape(SLABS * BLOCKS, 8, 128), AXES, 0, 0, tiled=...  7.12 us
    all_to_all x1, starting transfers between devices, per_device(): lax.all_to_all(solved, AXES, 0, 0, tiled=True).reshape(SLABS * CZ, 128)  5.81 us
    ppermute x1, starting transfers between devices, per_device(): most_before = lax.ppermute(most, 'tm', later)  5.63 us
    ppermute x1, starting transfers between devices, per_device(): rest_before = lax.ppermute(rest_sent, 'tm', later)  4.99 us
    pallas_call x1, Pallas kernels, per_device(): pl.pallas_call(nodes_kernel, out_shape=shape(3, *field), in_specs=[ANY] *...  4.59 us
    all_to_all x1, waiting for transfers between devices, per_device(): lax.all_to_all(solved, AXES, 0, 0, tiled=True).reshape(SLABS * CZ, 128)  3.89 us
  transfers between devices with their start and end apart: 6, of which 3 were waited for; matrix products, arithmetic and copies ran while one was open for 2% of the time, Pallas kernels for 8%

profile of v5, /device:TPU:1, one launch (start us, length us, event | category | flops | bytes accessed | tf_op | source)
XLA Modules:
  0.0 64.7 jit_solution(14945435203844296367)
XLA Ops:
  0.0 9.6 %fine.1 = (f32[4,256,256]{2,1,0:T(8,128)}, f32[4,256,256]{2,1,0:T(8,128)}, f32[4,192,256]{2,1,0:T(8,128)}, f32[4,192,256]{2,1,0:T(8,128)}, f32[8,16,8,128]{3,2,1,0:T(8,128)}) custom-call(f32[3,4,256,256]{3,2,1,0:T(8,128)} %bitcast.8, f32[256,256]{1,0:T(8,128)} %bitcast.13, bf16[256,256]{1,0:T(8,128)(2,1)} %constant.42.clone.along_hbm, ...), custom_call_target="tpu_custom_call" | custom-call | tf_op jit(solution)/shard_map/fine/pallas_call | solution.py:674
  9.6 0.0 copy-start.5
  9.6 0.0 copy-start
  9.6 0.0 copy-start.1
  9.6 0.0 copy-start.2
  9.6 0.0 copy-start.3
  9.6 0.0 copy-start.4
  9.7 1.5 %collective-permute-start = (f32[4,192,256]{2,1,0:T(8,128)}, f32[4,192,256]{2,1,0:T(8,128)S(1)}, u32[]{:S(2)}, u32[]{:S(2)}) collective-permute-start(f32[4,192,256]{2,1,0:T(8,128)} %get-tuple-element.15), channel_id=1, source_target_pairs={{0,1},{1,0},{2,3},{3,2},{4,5},{5,4},{6,7},{7,6},{8,9},{9,8},{10,11... | collective-permute-start | bytes 2359304 | tf_op jit(solution)/shard_map/spill/ppermute | solution.py:703
  11.1 3.3 %collective-permute-start.1 = (f32[4,192,256]{2,1,0:T(8,128)}, f32[4,192,256]{2,1,0:T(8,128)S(1)}, u32[]{:S(2)}, u32[]{:S(2)}) collective-permute-start(f32[4,192,256]{2,1,0:T(8,128)} %get-tuple-element.16), channel_id=1, source_target_pairs={{1,2},{3,4},{5,6},{7,8},{9,10},{11,12},{13,14},{2,1},{4,3},{6,5},{... | collective-permute-start | bytes 2359304 | tf_op jit(solution)/shard_map/spill/ppermute | solution.py:704
  14.5 9.8 %all-to-all-start = ((f32[128,8,128]{2,1,0:T(8,128)}), f32[128,8,128]{2,1,0:T(8,128)S(1)}, u32[]{:S(2)}, u32[]{:S(2)}) async-start(f32[128,8,128]{2,1,0:T(8,128)} %bitcast.11), calls=%async_computation | async-start | bytes 1048576 | tf_op jit(solution)/shard_map/to_modes/all_to_all | solution.py:698
  24.3 0.0 collective-permute-done.near_hbm
  24.3 0.0 copy-start.7
  24.3 0.3 collective-permute-done.1.across_hbm
  24.7 0.1 slice_select_fusion.1
  24.7 0.8 %copy-done.8 = f32[4,192,256]{2,1,0:T(8,128)} copy-done((f32[4,192,256]{2,1,0:T(8,128)}, f32[4,192,256]{2,1,0:T(8,128)S(1)}, u32[]{:S(2)}) %copy-start.8) | copy-done | bytes 786456
  25.5 0.0 copy-done.5
  25.6 0.1 maximum_add_fusion.most_hbm
  25.7 0.0 copy-start.6
  25.7 5.6 %collective-permute-start.2 = (f32[3,256,256]{2,1,0:T(8,128)S(1)}, f32[3,256,256]{2,1,0:T(8,128)}, u32[]{:S(2)}, u32[]{:S(2)}) collective-permute-start(f32[3,256,256]{2,1,0:T(8,128)S(1)} %maximum_add_fusion.most_hbm), channel_id=1, source_target_pairs={{0,16},{16,32},{32,48},{48,64},{64,80},{80,96},{96,112},{1,17},{17... | collective-permute-start | bytes 2359304 | tf_op jit(solution)/shard_map/pass/ppermute | solution.py:719
  31.3 7.1 %all-to-all-done = f32[128,8,128]{2,1,0:T(8,128)S(1)} async-done(((f32[128,8,128]{2,1,0:T(8,128)}), f32[128,8,128]{2,1,0:T(8,128)S(1)}, u32[]{:S(2)}, u32[]{:S(2)}) %all-to-all-start) | async-done | bytes 524320 | tf_op jit(solution)/shard_map/to_modes/all_to_all | solution.py:698
  38.4 0.0 copy-done.1
  38.4 1.8 %modes.1 = f32[512,128]{1,0:T(8,128)} custom-call(f32[1024,128]{1,0:T(8,128)S(1)} %bitcast.7, f32[128,128]{1,0:T(8,128)S(1)} %copy-done.1, f32[64,128]{1,0:T(8,128)S(1)} %copy-done.3, f32[8,128]{1,0:T(8,128)S(1)} %copy-done.4, bf16[2,128,128]{2,1,0:T(8,128)(2,1)S(1)} %copy-done, bf16[2,64,64]{2,1,0:T(8,128)(2,1)S(1)} %copy-done.2), custom_call_target="tpu_custom_call" | custom-call | flops 20000000000 | tf_op jit(solution)/shard_map/modes/pallas_call | solution.py:723
  40.2 5.8 %all-to-all-start.1 = ((f32[128,4,128]{2,1,0:T(4,128)}), f32[128,4,128]{2,1,0:T(4,128)S(1)}, u32[]{:S(2)}, u32[]{:S(2)}) async-start(f32[128,4,128]{2,1,0:T(4,128)} %bitcast.4), calls=%async_computation.1 | async-start | bytes 524288 | tf_op jit(solution)/shard_map/from_modes/all_to_all | solution.py:750
  46.1 0.9 %slice_select_fusion.3 = (f32[1,128,256]{2,1,0:T(8,128)S(1)}, f32[1,128,256]{2,1,0:T(8,128)S(1)}) fusion(f32[4,192,256]{2,1,0:T(8,128)} %copy-done.8, f32[4,192,256]{2,1,0:T(8,128)S(1)} %collective-permute-done.near_hbm, pred[]{:T(512)S(6)} %eq.5), kind=kLoop, calls=%fused_computation.5 | loop fusion | flops 65536 | bytes 524289 | tf_op jit(solution)/shard_map/end/jit(_where)/select_n | solution.py:712
  47.0 5.0 %collective-permute-start.3 = (f32[1,256,256]{2,1,0:T(8,128)S(1)}, f32[1,256,256]{2,1,0:T(8,128)S(1)}, u32[]{:S(2)}, u32[]{:S(2)}) collective-permute-start(f32[1,256,256]{2,1,0:T(8,128)S(1)} %maximum_add_fusion.1.rest_hbm), channel_id=1, source_target_pairs={{0,16},{16,32},{32,48},{48,64},{64,80},{80,96},{96,112},{1,17},{17... | collective-permute-start | bytes 786440 | tf_op jit(solution)/shard_map/pass_rest/ppermute | solution.py:734
  52.0 3.3 %middle.1 = (f32[4,256,256]{2,1,0:T(8,128)}, f32[4,256,256]{2,1,0:T(8,128)}) custom-call(f32[4,256,256]{2,1,0:T(8,128)} %get-tuple-element.14.first_hbm, f32[4,192,256]{2,1,0:T(8,128)} %copy-done.7, f32[4,192,256]{2,1,0:T(8,128)} %copy-done.8, f32[3,256,256]{2,1,0:T(8,128)} %copy-done.6, f32[1,256,256]{2,1,0:T(8,128)} %copy-done.9, f32[3,4,256,256]{3,2,1,0:T(8,128)} %bitcast.9), custom_call_target="tpu_custom_call" | custom-call | flops 3000000000 | tf_op jit(solution)/shard_map/middle/pallas_call | solution.py:737
  55.3 3.9 %all-to-all-done.1 = f32[128,4,128]{2,1,0:T(4,128)S(1)} async-done(((f32[128,4,128]{2,1,0:T(4,128)}), f32[128,4,128]{2,1,0:T(4,128)S(1)}, u32[]{:S(2)}, u32[]{:S(2)}) %all-to-all-start.1) | async-done | bytes 262176 | tf_op jit(solution)/shard_map/from_modes/all_to_all | solution.py:750
  59.2 0.0 collective-permute-done.3.rest_hbm
  59.2 0.0 collective-permute-done.2.most_hbm
  59.2 0.7 %copy-done.10 = f32[128,4,128]{2,1,0:T(4,128)} copy-done((f32[128,4,128]{2,1,0:T(4,128)}, f32[128,4,128]{2,1,0:T(4,128)S(1)}, u32[]{:S(2)}) %copy-start.10) | copy-done | bytes 262168
  59.9 0.1 copy-done.11
  60.0 4.6 %nodes.1 = f32[3,4,256,256]{3,2,1,0:T(8,128)} custom-call(f32[512,128]{1,0:T(8,128)} %bitcast.12, f32[4,256,256]{2,1,0:T(8,128)} %get-tuple-element.18.first_hbm, f32[4,256,256]{2,1,0:T(8,128)} %get-tuple-element.19.second_hbm, f32[3,256,256]{2,1,0:T(8,128)} %collective-permute-done.2.most_hbm, f32[1,256,256]{2,1,0:T(8,128)} %copy-done.11, ...), custom_call_target="tpu_custom_call" | custom-call | flops 5000000000 | tf_op jit(solution)/shard_map/nodes/pallas_call | solution.py:753
  (12 shorter events, 0.1 us)
Async XLA Ops:
  9.6 16.0 %copy-start.5 = (f32[4,256,256]{2,1,0:T(8,128)S(1)}, f32[4,256,256]{2,1,0:T(8,128)}, u32[]{:S(2)}) copy-start(f32[4,256,256]{2,1,0:T(8,128)} %get-tuple-element.17) | copy-start | bytes 3145732
  9.6 28.8 %copy-start = (bf16[2,128,128]{2,1,0:T(8,128)(2,1)S(1)}, bf16[2,128,128]{2,1,0:T(8,128)(2,1)}, u32[]{:S(2)}) copy-start(bf16[2,128,128]{2,1,0:T(8,128)(2,1)} %constant.50.clone.zf) | copy-start | bytes 196612
  9.6 28.8 %copy-start.1 = (f32[128,128]{1,0:T(8,128)S(1)}, f32[128,128]{1,0:T(8,128)}, u32[]{:S(2)}) copy-start(f32[128,128]{1,0:T(8,128)} %constant.47.clone.xy) | copy-start | bytes 196612
  9.6 28.8 %copy-start.2 = (bf16[2,64,64]{2,1,0:T(8,128)(2,1)S(1)}, bf16[2,64,64]{2,1,0:T(8,128)(2,1)}, u32[]{:S(2)}) copy-start(bf16[2,64,64]{2,1,0:T(8,128)(2,1)} %constant.51.clone.zb) | copy-start | bytes 49156
  9.6 28.8 %copy-start.3 = (f32[64,128]{1,0:T(8,128)S(1)}, f32[64,128]{1,0:T(8,128)}, u32[]{:S(2)}) copy-start(f32[64,128]{1,0:T(8,128)} %constant.48.clone.lam_z) | copy-start | bytes 98308
  9.6 28.8 %copy-start.4 = (f32[8,128]{1,0:T(8,128)S(1)}, f32[8,128]{1,0:T(8,128)}, u32[]{:S(2)}) copy-start(f32[8,128]{1,0:T(8,128)} %constant.49.clone.lanes) | copy-start | bytes 12292
  9.7 14.7 %collective-permute-start = (f32[4,192,256]{2,1,0:T(8,128)}, f32[4,192,256]{2,1,0:T(8,128)S(1)}, u32[]{:S(2)}, u32[]{:S(2)}) collective-permute-start(f32[4,192,256]{2,1,0:T(8,128)} %get-tuple-element.15), channel_id=1, source_target_pairs={{0,1},{1,0},{2,3},{3,2},{4,5},{5,4},{6,7},{7,6},{8,9},{9,8},{10,11... | collective-permute-start | bytes 2359304 | tf_op jit(solution)/shard_map/spill/ppermute | solution.py:703
  11.1 13.5 %collective-permute-start.1 = (f32[4,192,256]{2,1,0:T(8,128)}, f32[4,192,256]{2,1,0:T(8,128)S(1)}, u32[]{:S(2)}, u32[]{:S(2)}) collective-permute-start(f32[4,192,256]{2,1,0:T(8,128)} %get-tuple-element.16), channel_id=1, source_target_pairs={{1,2},{3,4},{5,6},{7,8},{9,10},{11,12},{13,14},{2,1},{4,3},{6,5},{... | collective-permute-start | bytes 2359304 | tf_op jit(solution)/shard_map/spill/ppermute | solution.py:704
  14.5 23.9 %all-to-all-start = ((f32[128,8,128]{2,1,0:T(8,128)}), f32[128,8,128]{2,1,0:T(8,128)S(1)}, u32[]{:S(2)}, u32[]{:S(2)}) async-start(f32[128,8,128]{2,1,0:T(8,128)} %bitcast.11), calls=%async_computation | async-start | bytes 1048576 | tf_op jit(solution)/shard_map/to_modes/all_to_all | solution.py:698
  24.3 21.7 %copy-start.7 = (f32[4,192,256]{2,1,0:T(8,128)}, f32[4,192,256]{2,1,0:T(8,128)S(1)}, u32[]{:S(2)}) copy-start(f32[4,192,256]{2,1,0:T(8,128)S(1)} %collective-permute-done.near_hbm) | copy-start | bytes 2359300
  24.7 0.9 %copy-start.8 = (f32[4,192,256]{2,1,0:T(8,128)}, f32[4,192,256]{2,1,0:T(8,128)S(1)}, u32[]{:S(2)}) copy-start(f32[4,192,256]{2,1,0:T(8,128)S(1)} %collective-permute-done.1.across_hbm) | copy-start | bytes 2359300
  25.7 14.6 %copy-start.6 = (f32[3,256,256]{2,1,0:T(8,128)}, f32[3,256,256]{2,1,0:T(8,128)S(1)}, u32[]{:S(2)}) copy-start(f32[3,256,256]{2,1,0:T(8,128)S(1)} %maximum_add_fusion.most_hbm) | copy-start | bytes 2359300
  25.7 33.6 %collective-permute-start.2 = (f32[3,256,256]{2,1,0:T(8,128)S(1)}, f32[3,256,256]{2,1,0:T(8,128)}, u32[]{:S(2)}, u32[]{:S(2)}) collective-permute-start(f32[3,256,256]{2,1,0:T(8,128)S(1)} %maximum_add_fusion.most_hbm), channel_id=1, source_target_pairs={{0,16},{16,32},{32,48},{48,64},{64,80},{80,96},{96,112},{1,17},{17... | collective-permute-start | bytes 2359304 | tf_op jit(solution)/shard_map/pass/ppermute | solution.py:719
  40.2 19.0 %all-to-all-start.1 = ((f32[128,4,128]{2,1,0:T(4,128)}), f32[128,4,128]{2,1,0:T(4,128)S(1)}, u32[]{:S(2)}, u32[]{:S(2)}) async-start(f32[128,4,128]{2,1,0:T(4,128)} %bitcast.4), calls=%async_computation.1 | async-start | bytes 524288 | tf_op jit(solution)/shard_map/from_modes/all_to_all | solution.py:750
  47.0 5.0 %copy-start.9 = (f32[1,256,256]{2,1,0:T(8,128)}, f32[1,256,256]{2,1,0:T(8,128)S(1)}, u32[]{:S(2)}) copy-start(f32[1,256,256]{2,1,0:T(8,128)S(1)} %maximum_add_fusion.1.rest_hbm) | copy-start | bytes 786436
  47.0 12.2 %collective-permute-start.3 = (f32[1,256,256]{2,1,0:T(8,128)S(1)}, f32[1,256,256]{2,1,0:T(8,128)S(1)}, u32[]{:S(2)}, u32[]{:S(2)}) collective-permute-start(f32[1,256,256]{2,1,0:T(8,128)S(1)} %maximum_add_fusion.1.rest_hbm), channel_id=1, source_target_pairs={{0,16},{16,32},{32,48},{48,64},{64,80},{80,96},{96,112},{1,17},{17... | collective-permute-start | bytes 786440 | tf_op jit(solution)/shard_map/pass_rest/ppermute | solution.py:734
  59.2 0.7 %copy-start.10 = (f32[128,4,128]{2,1,0:T(4,128)}, f32[128,4,128]{2,1,0:T(4,128)S(1)}, u32[]{:S(2)}) copy-start(f32[128,4,128]{2,1,0:T(4,128)S(1)} %all-to-all-done.1) | copy-start | bytes 786436
  59.2 0.8 %copy-start.11 = (f32[1,256,256]{2,1,0:T(8,128)}, f32[1,256,256]{2,1,0:T(8,128)S(1)}, u32[]{:S(2)}) copy-start(f32[1,256,256]{2,1,0:T(8,128)S(1)} %collective-permute-done.3.rest_hbm) | copy-start | bytes 786436

commit v6 on v5

--- a/solution.py
+++ b/solution.py
@@ -610,23 +610,29 @@
     for g in range(8):
         p_s[g] = right(left(yb, h_s[g]), xb)
     stores = []
+
+    def send(n, f):
+        store = pltpu.make_async_copy(out_s.at[n, f], out.at[n, f], sem.at[n, f])
+        store.start()
+        stores.append(store)
+
     for f in range(4):
         start = p_s[f]
         end = p_s[4 + f]
-        for i, (source, target) in enumerate(((first_hbm, first), (second_hbm, second), (second_hbm, before))):
-            pltpu.make_async_copy(source.at[f], target.at[f], in_sem.at[f, i]).wait()
+        pltpu.make_async_copy(first_hbm.at[f], first.at[f], in_sem.at[f, 0]).wait()
+        out_s[1, f] = first[f] + doubled(0.5 * (start + end))
+        send(1, f)
+        pltpu.make_async_copy(second_hbm.at[f], second.at[f], in_sem.at[f, 1]).wait()
+        out_s[2, f] = second[f] + doubled(end)
+        send(2, f)
+        pltpu.make_async_copy(second_hbm.at[f], before.at[f], in_sem.at[f, 2]).wait()
         for k in range(COARSE):
             pair = [pl.ds((2 * k + i) * PLANE, PLANE) for i in range(2)]
             value = [before[f, rows] for rows in pair]
             shift = start[k * PLANE:(k + 1) * PLANE] - block_mean(value[0] + value[1], 0.125 * mu)
             for i, rows in enumerate(pair):
                 out_s[0, f, rows] = value[i] + shift
-        out_s[1, f] = first[f] + doubled(0.5 * (start + end))
-        out_s[2, f] = second[f] + doubled(end)
-        for n in range(3):
-            store = pltpu.make_async_copy(out_s.at[n, f], out.at[n, f], sem.at[n, f])
-            store.start()
-            stores.append(store)
+        send(0, f)
     for store in stores:
         store.wait()
 

time: 65 us -> 64.9 us (level)
  no operation moved by 1% of the time
where the time goes in v6:
time: 64.9 us; the launch traced here: 64.6 us
  starting transfers between devices  31.1 us (48%)
  Pallas kernels  19.1 us (29%)
  waiting for transfers between devices  11.3 us (17%)
  local copies, waits for them, and re-layouts  1.65 us (3%)
  other arithmetic  1.13 us (2%)
    all_to_all x1, starting transfers between devices, per_device(): lax.all_to_all(packet.reshape(SLABS * BLOCKS, 8, 128), AXES, 0, 0, tiled=...  9.82 us
    pallas_call x1, Pallas kernels, per_device(): pl.pallas_call(fine_kernel, out_shape=[shape(*field), shape(*field), shap...  9.57 us
    all_to_all x1, waiting for transfers between devices, per_device(): lax.all_to_all(packet.reshape(SLABS * BLOCKS, 8, 128), AXES, 0, 0, tiled=...  7.12 us
    all_to_all x1, starting transfers between devices, per_device(): lax.all_to_all(solved, AXES, 0, 0, tiled=True).reshape(SLABS * CZ, 128)  5.81 us
    ppermute x1, starting transfers between devices, per_device(): most_before = lax.ppermute(most, 'tm', later)  5.63 us
    ppermute x1, starting transfers between devices, per_device(): rest_before = lax.ppermute(rest_sent, 'tm', later)  4.99 us
    pallas_call x1, Pallas kernels, per_device(): pl.pallas_call(nodes_kernel, out_shape=shape(3, *field), in_specs=[ANY] *...  4.45 us
    all_to_all x1, waiting for transfers between devices, per_device(): lax.all_to_all(solved, AXES, 0, 0, tiled=True).reshape(SLABS * CZ, 128)  3.89 us
  transfers between devices with their start and end apart: 6, of which 3 were waited for; matrix products, arithmetic and copies ran while one was open for 2% of the time, Pallas kernels for 8%

profile of v6, /device:TPU:1, one launch (start us, length us, event | category | flops | bytes accessed | tf_op | source)
XLA Modules:
  0.0 64.6 jit_solution(14256336069474553135)
XLA Ops:
  0.0 9.6 %fine.1 = (f32[4,256,256]{2,1,0:T(8,128)}, f32[4,256,256]{2,1,0:T(8,128)}, f32[4,192,256]{2,1,0:T(8,128)}, f32[4,192,256]{2,1,0:T(8,128)}, f32[8,16,8,128]{3,2,1,0:T(8,128)}) custom-call(f32[3,4,256,256]{3,2,1,0:T(8,128)} %bitcast.8, f32[256,256]{1,0:T(8,128)} %bitcast.13, bf16[256,256]{1,0:T(8,128)(2,1)} %constant.42.clone.along_hbm, ...), custom_call_target="tpu_custom_call" | custom-call | tf_op jit(solution)/shard_map/fine/pallas_call | solution.py:680
  9.6 0.0 copy-start.5
  9.6 0.0 copy-start
  9.6 0.0 copy-start.1
  9.6 0.0 copy-start.2
  9.6 0.0 copy-start.3
  9.6 0.0 copy-start.4
  9.7 1.5 %collective-permute-start = (f32[4,192,256]{2,1,0:T(8,128)}, f32[4,192,256]{2,1,0:T(8,128)S(1)}, u32[]{:S(2)}, u32[]{:S(2)}) collective-permute-start(f32[4,192,256]{2,1,0:T(8,128)} %get-tuple-element.15), channel_id=1, source_target_pairs={{0,1},{1,0},{2,3},{3,2},{4,5},{5,4},{6,7},{7,6},{8,9},{9,8},{10,11... | collective-permute-start | bytes 2359304 | tf_op jit(solution)/shard_map/spill/ppermute | solution.py:709
  11.1 3.3 %collective-permute-start.1 = (f32[4,192,256]{2,1,0:T(8,128)}, f32[4,192,256]{2,1,0:T(8,128)S(1)}, u32[]{:S(2)}, u32[]{:S(2)}) collective-permute-start(f32[4,192,256]{2,1,0:T(8,128)} %get-tuple-element.16), channel_id=1, source_target_pairs={{1,2},{3,4},{5,6},{7,8},{9,10},{11,12},{13,14},{2,1},{4,3},{6,5},{... | collective-permute-start | bytes 2359304 | tf_op jit(solution)/shard_map/spill/ppermute | solution.py:710
  14.5 9.8 %all-to-all-start = ((f32[128,8,128]{2,1,0:T(8,128)}), f32[128,8,128]{2,1,0:T(8,128)S(1)}, u32[]{:S(2)}, u32[]{:S(2)}) async-start(f32[128,8,128]{2,1,0:T(8,128)} %bitcast.11), calls=%async_computation | async-start | bytes 1048576 | tf_op jit(solution)/shard_map/to_modes/all_to_all | solution.py:704
  24.3 0.0 collective-permute-done.near_hbm
  24.3 0.0 copy-start.7
  24.3 0.3 collective-permute-done.1.across_hbm
  24.7 0.1 slice_select_fusion.1
  24.7 0.8 %copy-done.8 = f32[4,192,256]{2,1,0:T(8,128)} copy-done((f32[4,192,256]{2,1,0:T(8,128)}, f32[4,192,256]{2,1,0:T(8,128)S(1)}, u32[]{:S(2)}) %copy-start.8) | copy-done | bytes 786456
  25.5 0.0 copy-done.5
  25.6 0.1 maximum_add_fusion.most_hbm
  25.7 0.0 copy-start.6
  25.7 5.6 %collective-permute-start.2 = (f32[3,256,256]{2,1,0:T(8,128)S(1)}, f32[3,256,256]{2,1,0:T(8,128)}, u32[]{:S(2)}, u32[]{:S(2)}) collective-permute-start(f32[3,256,256]{2,1,0:T(8,128)S(1)} %maximum_add_fusion.most_hbm), channel_id=1, source_target_pairs={{0,16},{16,32},{32,48},{48,64},{64,80},{80,96},{96,112},{1,17},{17... | collective-permute-start | bytes 2359304 | tf_op jit(solution)/shard_map/pass/ppermute | solution.py:725
  31.3 7.1 %all-to-all-done = f32[128,8,128]{2,1,0:T(8,128)S(1)} async-done(((f32[128,8,128]{2,1,0:T(8,128)}), f32[128,8,128]{2,1,0:T(8,128)S(1)}, u32[]{:S(2)}, u32[]{:S(2)}) %all-to-all-start) | async-done | bytes 524320 | tf_op jit(solution)/shard_map/to_modes/all_to_all | solution.py:704
  38.4 0.0 copy-done.1
  38.4 1.8 %modes.1 = f32[512,128]{1,0:T(8,128)} custom-call(f32[1024,128]{1,0:T(8,128)S(1)} %bitcast.7, f32[128,128]{1,0:T(8,128)S(1)} %copy-done.1, f32[64,128]{1,0:T(8,128)S(1)} %copy-done.3, f32[8,128]{1,0:T(8,128)S(1)} %copy-done.4, bf16[2,128,128]{2,1,0:T(8,128)(2,1)S(1)} %copy-done, bf16[2,64,64]{2,1,0:T(8,128)(2,1)S(1)} %copy-done.2), custom_call_target="tpu_custom_call" | custom-call | flops 20000000000 | tf_op jit(solution)/shard_map/modes/pallas_call | solution.py:729
  40.2 5.8 %all-to-all-start.1 = ((f32[128,4,128]{2,1,0:T(4,128)}), f32[128,4,128]{2,1,0:T(4,128)S(1)}, u32[]{:S(2)}, u32[]{:S(2)}) async-start(f32[128,4,128]{2,1,0:T(4,128)} %bitcast.4), calls=%async_computation.1 | async-start | bytes 524288 | tf_op jit(solution)/shard_map/from_modes/all_to_all | solution.py:756
  46.1 0.9 %slice_select_fusion.3 = (f32[1,128,256]{2,1,0:T(8,128)S(1)}, f32[1,128,256]{2,1,0:T(8,128)S(1)}) fusion(f32[4,192,256]{2,1,0:T(8,128)} %copy-done.8, f32[4,192,256]{2,1,0:T(8,128)S(1)} %collective-permute-done.near_hbm, pred[]{:T(512)S(6)} %eq.5), kind=kLoop, calls=%fused_computation.5 | loop fusion | flops 65536 | bytes 524289 | tf_op jit(solution)/shard_map/end/jit(_where)/select_n | solution.py:718
  47.0 5.0 %collective-permute-start.3 = (f32[1,256,256]{2,1,0:T(8,128)S(1)}, f32[1,256,256]{2,1,0:T(8,128)S(1)}, u32[]{:S(2)}, u32[]{:S(2)}) collective-permute-start(f32[1,256,256]{2,1,0:T(8,128)S(1)} %maximum_add_fusion.1.rest_hbm), channel_id=1, source_target_pairs={{0,16},{16,32},{32,48},{48,64},{64,80},{80,96},{96,112},{1,17},{17... | collective-permute-start | bytes 786440 | tf_op jit(solution)/shard_map/pass_rest/ppermute | solution.py:740
  52.0 3.3 %middle.1 = (f32[4,256,256]{2,1,0:T(8,128)}, f32[4,256,256]{2,1,0:T(8,128)}) custom-call(f32[4,256,256]{2,1,0:T(8,128)} %get-tuple-element.14.first_hbm, f32[4,192,256]{2,1,0:T(8,128)} %copy-done.7, f32[4,192,256]{2,1,0:T(8,128)} %copy-done.8, f32[3,256,256]{2,1,0:T(8,128)} %copy-done.6, f32[1,256,256]{2,1,0:T(8,128)} %copy-done.9, f32[3,4,256,256]{3,2,1,0:T(8,128)} %bitcast.9), custom_call_target="tpu_custom_call" | custom-call | flops 3000000000 | tf_op jit(solution)/shard_map/middle/pallas_call | solution.py:743
  55.3 3.9 %all-to-all-done.1 = f32[128,4,128]{2,1,0:T(4,128)S(1)} async-done(((f32[128,4,128]{2,1,0:T(4,128)}), f32[128,4,128]{2,1,0:T(4,128)S(1)}, u32[]{:S(2)}, u32[]{:S(2)}) %all-to-all-start.1) | async-done | bytes 262176 | tf_op jit(solution)/shard_map/from_modes/all_to_all | solution.py:756
  59.2 0.0 collective-permute-done.3.rest_hbm
  59.2 0.0 collective-permute-done.2.most_hbm
  59.2 0.7 %copy-done.10 = f32[128,4,128]{2,1,0:T(4,128)} copy-done((f32[128,4,128]{2,1,0:T(4,128)}, f32[128,4,128]{2,1,0:T(4,128)S(1)}, u32[]{:S(2)}) %copy-start.10) | copy-done | bytes 262168
  59.9 0.1 copy-done.11
  60.0 4.4 %nodes.1 = f32[3,4,256,256]{3,2,1,0:T(8,128)} custom-call(f32[512,128]{1,0:T(8,128)} %bitcast.12, f32[4,256,256]{2,1,0:T(8,128)} %get-tuple-element.18.first_hbm, f32[4,256,256]{2,1,0:T(8,128)} %get-tuple-element.19.second_hbm, f32[3,256,256]{2,1,0:T(8,128)} %collective-permute-done.2.most_hbm, f32[1,256,256]{2,1,0:T(8,128)} %copy-done.11, ...), custom_call_target="tpu_custom_call" | custom-call | flops 5000000000 | tf_op jit(solution)/shard_map/nodes/pallas_call | solution.py:759
  (12 shorter events, 0.1 us)
Async XLA Ops:
  9.6 16.0 %copy-start.5 = (f32[4,256,256]{2,1,0:T(8,128)S(1)}, f32[4,256,256]{2,1,0:T(8,128)}, u32[]{:S(2)}) copy-start(f32[4,256,256]{2,1,0:T(8,128)} %get-tuple-element.17) | copy-start | bytes 3145732
  9.6 28.8 %copy-start = (bf16[2,128,128]{2,1,0:T(8,128)(2,1)S(1)}, bf16[2,128,128]{2,1,0:T(8,128)(2,1)}, u32[]{:S(2)}) copy-start(bf16[2,128,128]{2,1,0:T(8,128)(2,1)} %constant.50.clone.zf) | copy-start | bytes 196612
  9.6 28.8 %copy-start.1 = (f32[128,128]{1,0:T(8,128)S(1)}, f32[128,128]{1,0:T(8,128)}, u32[]{:S(2)}) copy-start(f32[128,128]{1,0:T(8,128)} %constant.47.clone.xy) | copy-start | bytes 196612
  9.6 28.8 %copy-start.2 = (bf16[2,64,64]{2,1,0:T(8,128)(2,1)S(1)}, bf16[2,64,64]{2,1,0:T(8,128)(2,1)}, u32[]{:S(2)}) copy-start(bf16[2,64,64]{2,1,0:T(8,128)(2,1)} %constant.51.clone.zb) | copy-start | bytes 49156
  9.6 28.8 %copy-start.3 = (f32[64,128]{1,0:T(8,128)S(1)}, f32[64,128]{1,0:T(8,128)}, u32[]{:S(2)}) copy-start(f32[64,128]{1,0:T(8,128)} %constant.48.clone.lam_z) | copy-start | bytes 98308
  9.6 28.8 %copy-start.4 = (f32[8,128]{1,0:T(8,128)S(1)}, f32[8,128]{1,0:T(8,128)}, u32[]{:S(2)}) copy-start(f32[8,128]{1,0:T(8,128)} %constant.49.clone.lanes) | copy-start | bytes 12292
  9.7 14.7 %collective-permute-start = (f32[4,192,256]{2,1,0:T(8,128)}, f32[4,192,256]{2,1,0:T(8,128)S(1)}, u32[]{:S(2)}, u32[]{:S(2)}) collective-permute-start(f32[4,192,256]{2,1,0:T(8,128)} %get-tuple-element.15), channel_id=1, source_target_pairs={{0,1},{1,0},{2,3},{3,2},{4,5},{5,4},{6,7},{7,6},{8,9},{9,8},{10,11... | collective-permute-start | bytes 2359304 | tf_op jit(solution)/shard_map/spill/ppermute | solution.py:709
  11.1 13.5 %collective-permute-start.1 = (f32[4,192,256]{2,1,0:T(8,128)}, f32[4,192,256]{2,1,0:T(8,128)S(1)}, u32[]{:S(2)}, u32[]{:S(2)}) collective-permute-start(f32[4,192,256]{2,1,0:T(8,128)} %get-tuple-element.16), channel_id=1, source_target_pairs={{1,2},{3,4},{5,6},{7,8},{9,10},{11,12},{13,14},{2,1},{4,3},{6,5},{... | collective-permute-start | bytes 2359304 | tf_op jit(solution)/shard_map/spill/ppermute | solution.py:710
  14.5 23.9 %all-to-all-start = ((f32[128,8,128]{2,1,0:T(8,128)}), f32[128,8,128]{2,1,0:T(8,128)S(1)}, u32[]{:S(2)}, u32[]{:S(2)}) async-start(f32[128,8,128]{2,1,0:T(8,128)} %bitcast.11), calls=%async_computation | async-start | bytes 1048576 | tf_op jit(solution)/shard_map/to_modes/all_to_all | solution.py:704
  24.3 21.7 %copy-start.7 = (f32[4,192,256]{2,1,0:T(8,128)}, f32[4,192,256]{2,1,0:T(8,128)S(1)}, u32[]{:S(2)}) copy-start(f32[4,192,256]{2,1,0:T(8,128)S(1)} %collective-permute-done.near_hbm) | copy-start | bytes 2359300
  24.7 0.9 %copy-start.8 = (f32[4,192,256]{2,1,0:T(8,128)}, f32[4,192,256]{2,1,0:T(8,128)S(1)}, u32[]{:S(2)}) copy-start(f32[4,192,256]{2,1,0:T(8,128)S(1)} %collective-permute-done.1.across_hbm) | copy-start | bytes 2359300
  25.7 14.6 %copy-start.6 = (f32[3,256,256]{2,1,0:T(8,128)}, f32[3,256,256]{2,1,0:T(8,128)S(1)}, u32[]{:S(2)}) copy-start(f32[3,256,256]{2,1,0:T(8,128)S(1)} %maximum_add_fusion.most_hbm) | copy-start | bytes 2359300
  25.7 33.6 %collective-permute-start.2 = (f32[3,256,256]{2,1,0:T(8,128)S(1)}, f32[3,256,256]{2,1,0:T(8,128)}, u32[]{:S(2)}, u32[]{:S(2)}) collective-permute-start(f32[3,256,256]{2,1,0:T(8,128)S(1)} %maximum_add_fusion.most_hbm), channel_id=1, source_target_pairs={{0,16},{16,32},{32,48},{48,64},{64,80},{80,96},{96,112},{1,17},{17... | collective-permute-start | bytes 2359304 | tf_op jit(solution)/shard_map/pass/ppermute | solution.py:725
  40.2 19.0 %all-to-all-start.1 = ((f32[128,4,128]{2,1,0:T(4,128)}), f32[128,4,128]{2,1,0:T(4,128)S(1)}, u32[]{:S(2)}, u32[]{:S(2)}) async-start(f32[128,4,128]{2,1,0:T(4,128)} %bitcast.4), calls=%async_computation.1 | async-start | bytes 524288 | tf_op jit(solution)/shard_map/from_modes/all_to_all | solution.py:756
  47.0 5.0 %copy-start.9 = (f32[1,256,256]{2,1,0:T(8,128)}, f32[1,256,256]{2,1,0:T(8,128)S(1)}, u32[]{:S(2)}) copy-start(f32[1,256,256]{2,1,0:T(8,128)S(1)} %maximum_add_fusion.1.rest_hbm) | copy-start | bytes 786436
  47.0 12.2 %collective-permute-start.3 = (f32[1,256,256]{2,1,0:T(8,128)S(1)}, f32[1,256,256]{2,1,0:T(8,128)S(1)}, u32[]{:S(2)}, u32[]{:S(2)}) collective-permute-start(f32[1,256,256]{2,1,0:T(8,128)S(1)} %maximum_add_fusion.1.rest_hbm), channel_id=1, source_target_pairs={{0,16},{16,32},{32,48},{48,64},{64,80},{80,96},{96,112},{1,17},{17... | collective-permute-start | bytes 786440 | tf_op jit(solution)/shard_map/pass_rest/ppermute | solution.py:740
  59.2 0.7 %copy-start.10 = (f32[128,4,128]{2,1,0:T(4,128)}, f32[128,4,128]{2,1,0:T(4,128)S(1)}, u32[]{:S(2)}) copy-start(f32[128,4,128]{2,1,0:T(4,128)S(1)} %all-to-all-done.1) | copy-start | bytes 786436
  59.2 0.8 %copy-start.11 = (f32[1,256,256]{2,1,0:T(8,128)}, f32[1,256,256]{2,1,0:T(8,128)S(1)}, u32[]{:S(2)}) copy-start(f32[1,256,256]{2,1,0:T(8,128)S(1)} %collective-permute-done.3.rest_hbm) | copy-start | bytes 786436
